TPU v7x, 32 devices: a whole 2x2x4 slice. The times are simulated.
32 devices in a mesh: ctx: 8 (over z, y), head: 4 (over x, core).
Axes of the slice: x: 2, y: 2, z: 4, core: 2. Of those that a mesh axis runs over, the one named last changes fastest.
Arguments:
- queries: bfloat16 [2048, 32, 128], P('ctx', 'head'), may hold values from -6 to 6
- key_states: bfloat16 [2048, 4, 128], P('ctx', 'head'), may hold values from -6 to 6
- value_states: bfloat16 [2048, 4, 128], P('ctx', 'head'), may hold values from -6 to 6
- doc_lengths: int32 [8], replicated, may hold values from 1 to 1792, 2048 in all
- grad_attended: bfloat16 [2048, 4096], P(('ctx', 'head')), may hold values from -6 to 6
Outputs:
- attended: bfloat16 [2048, 4096], P(('ctx', 'head'))
- grad_queries: bfloat16 [2048, 32, 128], P('ctx', 'head')
- grad_keys: bfloat16 [2048, 4, 128], P('ctx', 'head')
- grad_values: bfloat16 [2048, 4, 128], P('ctx', 'head')
All inputs are finite; a program needn't handle non-finite values.
Results may differ from a plain program's by a relative error of at most 0.022.
Values may be sent and summed in bfloat16 or wider, within the bound.
No kernel may reach another device: no remote copies, remote signals or barrier semaphores. Data moves between devices by JAX's collectives and lax.ppermute only.
A program may use at most 64 MiB of HBM per device.

v0:
```python
import functools
import math

import jax
import jax.numpy as jnp
from jax import lax
from jax.experimental import pallas as pl
from jax.experimental.pallas import tpu as pltpu
from jax.sharding import PartitionSpec as P

DOC_MOST = 1792
NEG_FILL = -1e30
TILE = 256
CHUNK = 128
LOG2_E = 1.4426950408889634
SMALL_VMEM = 8 * 1024 * 1024


def dot(a, b):
    return jnp.dot(a, b, preferred_element_type=jnp.float32)


def dot_nt(a, b):
    return lax.dot_general(a, b, (((1,), (1,)), ((), ())), preferred_element_type=jnp.float32)


def unit(size):
    rows = lax.broadcasted_iota(jnp.int32, (size, size), 0)
    return (rows == lax.broadcasted_iota(jnp.int32, (size, size), 1)).astype(jnp.bfloat16)


def twice(column):
    return jnp.concatenate([column, column], axis=1)


def attention_kernel(
    doc_ref,
    q_rows,
    q_cols,
    do_rows,
    do_cols,
    own_ref,
    near_ref,
    *refs,
    back,
    whole,
    ranks,
    heads,
    width,
    scale,
):
    arrived, far, refs = refs[:back], refs[back : 2 * back], refs[2 * back :]
    out_parts, dq_acc, refs = refs[:ranks], refs[ranks], refs[ranks + 1 :]
    d_refs, refs = refs[: 2 * back + 2], refs[2 * back + 2 :]
    (o_ref, keys, values, scores, accum, top, delta, d_blocks) = refs
    tok = own_ref.shape[0] // 2
    part_rows = tok // ranks
    docs = doc_ref.shape[0]
    ctx = lax.axis_index("ctx")
    rank = lax.axis_index("head")
    parity = lax.rem(ctx, 2)
    base = 0 if whole else (ctx - parity - 2 * back) * tok
    own = ctx if whole else 2 * back + parity
    ones = jnp.ones((width, width), jnp.bfloat16)

    def pair_of(k):
        return (ctx // 2) ^ k if whole else back - k

    values[:, width:] = jnp.ones_like(values[:, width:])
    for k in range(back + 1):
        pair = pair_of(k)
        mine, other = (own_ref, near_ref) if k == 0 else (arrived[k - 1], far[k - 1])
        for ref, place in ((mine, 2 * pair + parity), (other, 2 * pair + 1 - parity)):
            at = pl.ds(pl.multiple_of(place * tok, tok), tok)
            keys[at, :] = ref[0:tok, :]
            values[at, 0:width] = ref[tok:, :]
    d_blocks[...] = jnp.zeros_like(d_blocks)

    def chunk_step(chunk, carry):
        here = pl.ds(pl.multiple_of(chunk * CHUNK, CHUNK), CHUNK)
        top[...] = jnp.full_like(top, NEG_FILL)

        t_first = base + own * TILE + chunk * CHUNK
        t_last = t_first + CHUNK - 1
        t_col = t_first + lax.broadcasted_iota(jnp.int32, (CHUNK, width), 0)
        end = jnp.int32(0)
        start_first, start_last = jnp.int32(0), jnp.int32(0)
        start_col = jnp.zeros((CHUNK, width), jnp.int32)
        for i in range(docs):
            end = end + doc_ref[i]
            start_first = jnp.where(end <= t_first, end, start_first)
            start_last = jnp.where(end <= t_last, end, start_last)
            start_col = jnp.where(t_col >= end, end, start_col)
        low = jnp.maximum(start_first - base, 0) // TILE
        clear = jnp.clip((start_last - base + TILE - 1) // TILE, low, own)

        def score_tile(i, masked):
            at = pl.ds(pl.multiple_of(i * TILE, TILE), TILE)
            tile = dot_nt(q_rows[chunk], keys[at, :]) * (scale * LOG2_E)
            if masked:
                s_row = base + i * TILE + lax.broadcasted_iota(jnp.int32, (CHUNK, TILE), 1)
                live = (s_row >= twice(start_col)) & (s_row <= twice(t_col))
                tile = jnp.concatenate(
                    [
                        jnp.where(live, tile[j * CHUNK : (j + 1) * CHUNK], NEG_FILL)
                        for j in range(heads)
                    ],
                    axis=0,
                )
            scores[i] = tile
            top[...] = jnp.maximum(top[...], jnp.maximum(tile[:, :width], tile[:, width:]))

        def edge_step(n, carry):
            score_tile(jnp.where(n < clear - low, low + n, own), True)
            return carry

        def inner_step(i, carry):
            score_tile(i, False)
            return carry

        lax.fori_loop(0, clear - low + 1, edge_step, 0)
        lax.fori_loop(clear, own, inner_step, 0)
        top[...] = jnp.broadcast_to(jnp.max(top[...], axis=1, keepdims=True), top.shape)
        accum[...] = jnp.zeros_like(accum)

        def weigh_step(i, carry):
            at = pl.ds(pl.multiple_of(i * TILE, TILE), TILE)
            weights = jnp.exp2(scores[i] - twice(top[...])).astype(jnp.bfloat16)
            accum[...] += dot(weights, values[at, :])
            return carry

        lax.fori_loop(low, own + 1, weigh_step, 0)
        total = accum[:, width:]
        out = (accum[:, 0:width] / total).astype(jnp.bfloat16)
        for j in range(heads):
            o_ref[here, j * width : (j + 1) * width] = out[j * CHUNK : (j + 1) * CHUNK]
        top[...] = top[...] + jnp.log2(total)
        product = do_rows[chunk].astype(jnp.float32) * out.astype(jnp.float32)
        coarse = product.astype(jnp.bfloat16)
        fine = (product - coarse.astype(jnp.float32)).astype(jnp.bfloat16)
        delta[...] = dot(coarse, ones) + dot(fine, ones)
        dq_acc[chunk] = jnp.zeros(dq_acc.shape[1:], jnp.float32)

        def back_step(i, carry):
            at = pl.ds(pl.multiple_of(i * TILE, TILE), TILE)
            probs = jnp.exp2(scores[i] - twice(top[...]))
            d_probs = dot_nt(do_rows[chunk], values[at, 0:width])
            d_scores = (probs * (d_probs - twice(delta[...]))).astype(jnp.bfloat16)
            dq_acc[chunk] += dot(d_scores, keys[at, :])
            d_blocks[i, 0:width, :] += dot(q_cols[chunk], d_scores)
            d_blocks[i, width:, :] += dot(do_cols[chunk], probs.astype(jnp.bfloat16))
            return carry

        lax.fori_loop(low, own + 1, back_step, 0)
        return carry

    lax.fori_loop(0, tok // CHUNK, chunk_step, 0)
    for k in range(ranks):
        at = pl.ds(pl.multiple_of((rank ^ k) * part_rows, part_rows), part_rows)
        out_parts[k][...] = o_ref[at, :]
    for k in range(back + 1):
        pair = jnp.maximum(ctx // 2 - k, 0) if whole else back - k
        mine, other = 2 * pair + parity, 2 * pair + 1 - parity
        mine_ref, other_ref = d_refs[2 * k], d_refs[2 * k + 1]
        mine_ref[0:width, :] = d_blocks[mine, 0:width, :] * scale
        mine_ref[width:, :] = d_blocks[mine, width:, :]
        other_ref[0:width, :] = (d_blocks[other, 0:width, :] * scale).astype(jnp.bfloat16)
        other_ref[width:, :] = d_blocks[other, width:, :].astype(jnp.bfloat16)


def attend(doc_lengths, prepared, own, near, arrived, far, ranks, whole):
    chunks, rows, width = prepared[0].shape
    tok = chunks * CHUNK
    heads = rows // CHUNK
    back = len(arrived)
    tiles = 2 * (back + 1)
    span = tiles * tok
    vmem = pl.BlockSpec(memory_space=pltpu.VMEM)
    smem = pl.BlockSpec(memory_space=pltpu.SMEM)
    out_part = jax.ShapeDtypeStruct((tok // ranks, heads * width), jnp.bfloat16)
    return pl.pallas_call(
        functools.partial(
            attention_kernel,
            back=back,
            whole=whole,
            ranks=ranks,
            heads=heads,
            width=width,
            scale=1.0 / math.sqrt(width),
        ),
        out_shape=[out_part] * ranks
        + [
            jax.ShapeDtypeStruct((chunks, rows, width), jnp.float32),
        ]
        + [
            jax.ShapeDtypeStruct((2 * width, tok), dtype)
            for _ in range(back + 1)
            for dtype in (jnp.float32, jnp.bfloat16)
        ],
        in_specs=[smem] + [vmem] * (6 + 2 * back),
        out_specs=[vmem] * (ranks + 2 * back + 3),
        scratch_shapes=[
            pltpu.VMEM((tok, heads * width), jnp.bfloat16),
            pltpu.VMEM((span, width), jnp.bfloat16),
            pltpu.VMEM((span, 2 * width), jnp.bfloat16),
            pltpu.VMEM((tiles, rows, TILE), jnp.float32),
            pltpu.VMEM((rows, 2 * width), jnp.float32),
            pltpu.VMEM((rows, width), jnp.float32),
            pltpu.VMEM((rows, width), jnp.float32),
            pltpu.VMEM((tiles, 2 * width, tok), jnp.float32),
        ],
        compiler_params=pltpu.CompilerParams(vmem_limit_bytes=32 * 1024 * 1024),
        cost_estimate=pl.CostEstimate(
            flops=14 * tok * heads * width * span,
            bytes_accessed=4 * tok * heads * width * 2 + 4 * span * width * 2,
            transcendentals=tok * heads * span,
        ),
        name="attention",
    )(doc_lengths, *prepared, own, near, *arrived, *far)


def split_kernel(grad_ref, *part_refs):
    size = part_refs[0].shape[1]
    for k, ref in enumerate(part_refs):
        at = pl.multiple_of((lax.axis_index("head") ^ k) * size, size)
        ref[...] = grad_ref[:, pl.ds(at, size)]


def split(grad_attended, ranks):
    rows, columns = grad_attended.shape
    vmem = pl.BlockSpec(memory_space=pltpu.VMEM)
    part = jax.ShapeDtypeStruct((rows, columns // ranks), grad_attended.dtype)
    return pl.pallas_call(
        split_kernel,
        out_shape=[part] * ranks,
        in_specs=[vmem],
        out_specs=[vmem] * ranks,
        compiler_params=pltpu.CompilerParams(vmem_limit_bytes=SMALL_VMEM),
        name="split",
    )(grad_attended)


def arrange_kernel(q_ref, rows_ref, cols_ref, wide):
    small = unit(q_ref.shape[2])
    wide[...] = q_ref[...].astype(jnp.float32)
    for chunk in range(rows_ref.shape[0]):
        for j in range(q_ref.shape[1]):
            rows_ref[chunk, j * CHUNK : (j + 1) * CHUNK, :] = wide[
                chunk * CHUNK : (chunk + 1) * CHUNK, j, :
            ].astype(jnp.bfloat16)
        cols_ref[chunk] = dot_nt(small, rows_ref[chunk]).astype(jnp.bfloat16)


def arrange_grads_kernel(*refs):
    parts, (rows_ref, cols_ref, grads) = refs[:-3], refs[-3:]
    width = rows_ref.shape[2]
    small = unit(width)
    size = parts[0].shape[0]
    for k, ref in enumerate(parts):
        at = pl.multiple_of((lax.axis_index("head") ^ k) * size, size)
        grads[pl.ds(at, size), :] = ref[...]
    for chunk in range(rows_ref.shape[0]):
        for j in range(rows_ref.shape[1] // CHUNK):
            rows_ref[chunk, j * CHUNK : (j + 1) * CHUNK, :] = grads[
                chunk * CHUNK : (chunk + 1) * CHUNK, j * width : (j + 1) * width
            ]
        cols_ref[chunk] = dot_nt(small, rows_ref[chunk]).astype(jnp.bfloat16)


def arrange(kernel, arrays, shape, scratch):
    tok, heads, width = shape
    vmem = pl.BlockSpec(memory_space=pltpu.VMEM)
    chunks, rows = tok // CHUNK, heads * CHUNK
    return pl.pallas_call(
        kernel,
        out_shape=[
            jax.ShapeDtypeStruct((chunks, rows, width), jnp.bfloat16),
            jax.ShapeDtypeStruct((chunks, width, rows), jnp.bfloat16),
        ],
        in_specs=[vmem] * len(arrays),
        out_specs=[vmem, vmem],
        scratch_shapes=[scratch],
        compiler_params=pltpu.CompilerParams(vmem_limit_bytes=SMALL_VMEM),
        name="arrange",
    )(*arrays)


def join_kernel(*refs):
    parts, (rows_ref, out_ref, dq_ref, wide) = refs[:-4], refs[-4:]
    size = parts[0].shape[1]
    for k, ref in enumerate(parts):
        at = pl.multiple_of((lax.axis_index("head") ^ k) * size, size)
        out_ref[:, pl.ds(at, size)] = ref[...]
    scale = 1.0 / math.sqrt(rows_ref.shape[2])
    for chunk in range(rows_ref.shape[0]):
        for j in range(dq_ref.shape[1]):
            wide[chunk * CHUNK : (chunk + 1) * CHUNK, j, :] = (
                rows_ref[chunk, j * CHUNK : (j + 1) * CHUNK, :] * scale
            )
    dq_ref[...] = wide[...].astype(jnp.bfloat16)


def join(parts, dq_rows, shape):
    rows, size = parts[0].shape
    vmem = pl.BlockSpec(memory_space=pltpu.VMEM)
    return pl.pallas_call(
        join_kernel,
        out_shape=(
            jax.ShapeDtypeStruct((rows, size * len(parts)), parts[0].dtype),
            jax.ShapeDtypeStruct(shape, jnp.bfloat16),
        ),
        in_specs=[vmem] * (len(parts) + 1),
        out_specs=(vmem, vmem),
        scratch_shapes=[pltpu.VMEM(shape, jnp.float32)],
        compiler_params=pltpu.CompilerParams(vmem_limit_bytes=SMALL_VMEM),
        name="join",
    )(*parts, dq_rows)


def merge_kernel(*refs):
    total = refs[0][...]
    for ref in refs[1:-1]:
        total = total + ref[...].astype(jnp.float32)
    refs[-1][...] = total.astype(jnp.bfloat16)


def merge(*blocks):
    vmem = pl.BlockSpec(memory_space=pltpu.VMEM)
    return pl.pallas_call(
        merge_kernel,
        out_shape=jax.ShapeDtypeStruct(blocks[0].shape, jnp.bfloat16),
        in_specs=[vmem] * len(blocks),
        out_specs=vmem,
        compiler_params=pltpu.CompilerParams(vmem_limit_bytes=SMALL_VMEM),
        name="merge",
    )(*blocks)


def finish_kernel(own_ref, *refs):
    arrived = refs[:-2]
    dk_ref, dv_ref = refs[-2:]
    total = own_ref[...]
    for ref in arrived:
        total = total + ref[...].astype(jnp.float32)
    total = total.astype(jnp.bfloat16)
    width = dk_ref.shape[1]
    large = unit(dk_ref.shape[0])
    dk_ref[...] = dot_nt(large, total[:width]).astype(jnp.bfloat16)
    dv_ref[...] = dot_nt(large, total[width:]).astype(jnp.bfloat16)


def finish(own_part, arrived):
    both, tok = own_part.shape
    vmem = pl.BlockSpec(memory_space=pltpu.VMEM)
    shape = jax.ShapeDtypeStruct((tok, both // 2), jnp.bfloat16)
    return pl.pallas_call(
        finish_kernel,
        out_shape=(shape, shape),
        in_specs=[vmem] * (1 + len(arrived)),
        out_specs=(vmem, vmem),
        compiler_params=pltpu.CompilerParams(vmem_limit_bytes=SMALL_VMEM),
        name="finish",
    )(own_part, *arrived)


def shifted(block, by, count):
    pairs = [(i, i + by) for i in range(count) if 0 <= i + by < count]
    return lax.ppermute(block, "ctx", pairs)


def exchanged(block, axis, by):
    return lax.ppermute(block, axis, [(i, i ^ by) for i in range(lax.axis_size(axis))])


def after(value, *others):
    return lax.optimization_barrier((value, *others))


def body(queries, key_states, value_states, doc_lengths, grad_attended):
    tok, heads, width = queries.shape
    count = lax.axis_size("ctx")
    ranks = lax.axis_size("head")
    reach = min((DOC_MOST + tok - 2) // tok, count - 1)
    back = min((reach + 1) // 2, count // 2 - 1)
    whole = count == 8 and back == 3 and ranks == 4
    own = jnp.concatenate(
        [key_states.reshape(tok, width), value_states.reshape(tok, width)], axis=0
    )
    near = exchanged(own, "ctx", 1)
    if whole:
        beside = exchanged(own, "ctx", 2)
        across = exchanged(own, "ctx", 4)
    else:
        arrived = [shifted(own, 2 * k, count) for k in range(1, back + 1)]
    grads = split(grad_attended, ranks)
    grads = [part if k == 0 else exchanged(part, "head", k) for k, part in enumerate(grads)]
    prepared = arrange(
        arrange_kernel, [queries], queries.shape, pltpu.VMEM(queries.shape, jnp.float32)
    )
    if whole:
        beside, near = after(beside, near)
        far_beside = exchanged(beside, "ctx", 1)
        across, grads[1], *prepared = after(across, grads[1], *prepared)
        passed = exchanged(across, "ctx", 2)
        far_across = exchanged(across, "ctx", 1)
    prepared = [*prepared, *arrange(
        arrange_grads_kernel,
        grads,
        queries.shape,
        pltpu.VMEM((tok, heads * width), jnp.bfloat16),
    )]
    if whole:
        passed, far_beside, *prepared = after(passed, far_beside, *prepared)
        far_passed = exchanged(passed, "ctx", 1)
        arrived = [beside, across, passed]
        far = [far_beside, far_across, far_passed]
    else:
        far = [exchanged(block, "ctx", 1) for block in arrived]
    outputs = attend(doc_lengths, prepared, own, near, arrived, far, ranks, whole)
    outs, dq_rows, parts = list(outputs[:ranks]), outputs[ranks], outputs[ranks + 1 :]
    mine, other = list(parts[0::2]), list(parts[1::2])
    outs = [part if k == 0 else exchanged(part, "head", k) for k, part in enumerate(outs)]
    for k in range(back, 1, -1):
        other[k] = exchanged(other[k], "ctx", 1)
    other[back], *outs[1:2] = after(other[back], *outs[1:2])
    returned = []
    for k in range(back, 0, -1):
        if k == back - 1:
            other[k], *outs[2:3] = after(other[k], *outs[2:3])
        block = merge(mine[k], other[k])
        if k == back:
            block, other[1] = after(block, other[1])
            other[1] = exchanged(other[1], "ctx", 1)
            other[0], other[1] = after(other[0], other[1])
            other[0] = exchanged(other[0], "ctx", 1)
        returned.append(shifted(block, -2 * k, count))
    grad_keys, grad_values = finish(mine[0], [other[0]] + returned)
    attended, grad_queries = join(outs, dq_rows, queries.shape)
    grad_keys = grad_keys.reshape(tok, 1, width)
    grad_values = grad_values.reshape(tok, 1, width)
    return attended, grad_queries, grad_keys, grad_values


def solution(mesh):
    in_specs = (
        P("ctx", "head", None),
        P("ctx", "head", None),
        P("ctx", "head", None),
        P(),
        P(("ctx", "head"), None),
    )
    out_specs = (
        P(("ctx", "head"), None),
        P("ctx", "head", None),
        P("ctx", "head", None),
        P("ctx", "head", None),
    )
    return jax.shard_map(body, mesh=mesh, in_specs=in_specs, out_specs=out_specs, check_vma=False)
```

profile of v0, /device:TPU:9, one launch (start us, length us, event | category | flops | bytes accessed | tf_op | source)
XLA Modules:
  0.0 64.9 jit_solution(4098419024975018344)
XLA Ops:
  0.6 0.9 %pad_maximum_fusion.own_ref = bf16[512,128]{1,0:T(8,128)(2,1)S(1)} fusion(bf16[256,128]{1,0:T(8,128)(2,1)} %bitcast.4, bf16[256,128]{1,0:T(8,128)(2,1)} %bitcast.5), kind=kLoop, calls=%fused_computation | loop fusion | flops 262144 | bytes 262144 | tf_op jit(solution)/shard_map/concatenate | solution.py:386
  1.5 1.3 %collective-permute-start.4 = (bf16[512,128]{1,0:T(8,128)(2,1)S(1)}, bf16[512,128]{1,0:T(8,128)(2,1)S(1)}, u32[]{:S(2)}, u32[]{:S(2)}) collective-permute-start(bf16[512,128]{1,0:T(8,128)(2,1)S(1)} %pad_maximum_fusion.own_ref), channel_id=1, source_target_pairs={{0,4},{4,0},{8,12},{12,8},{16,20},{20,16},{24,28},{28,24},{1,5},{5... | collective-permute-start | bytes 393224 | tf_op jit(solution)/shard_map/ppermute | solution.py:372
  2.8 0.2 collective-permute-start.3
  3.0 2.3 %collective-permute-start = (bf16[512,128]{1,0:T(8,128)(2,1)S(1)}, bf16[512,128]{1,0:T(8,128)(2,1)S(1)}, u32[]{:S(2)}, u32[]{:S(2)}) collective-permute-start(bf16[512,128]{1,0:T(8,128)(2,1)S(1)} %pad_maximum_fusion.own_ref), channel_id=1, source_target_pairs={{0,16},{4,20},{8,24},{12,28},{16,0},{20,4},{24,8},{28,12},{1,17},{... | collective-permute-start | bytes 393224 | tf_op jit(solution)/shard_map/ppermute | solution.py:372
  5.3 0.0 copy-start
  5.3 1.0 %copy-done = bf16[64,4096]{1,0:T(8,128)(2,1)S(1)} copy-done((bf16[64,4096]{1,0:T(8,128)(2,1)S(1)}, bf16[64,4096]{1,0:T(8,128)(2,1)}, u32[]{:S(2)}) %copy-start) | copy-done | bytes 524312
  6.3 0.0 copy-start.1
  6.4 1.6 %collective-permute-start.1 = (bf16[64,1024]{1,0:T(8,128)(2,1)S(1)}, bf16[64,1024]{1,0:T(8,128)(2,1)S(1)}, u32[]{:S(2)}, u32[]{:S(2)}) collective-permute-start(bf16[64,1024]{1,0:T(8,128)(2,1)S(1)} %get-tuple-element.49), channel_id=1, source_target_pairs={{0,1},{1,0},{2,3},{3,2},{4,5},{5,4},{6,7},{7,6},{8,9},{9,8},{10,11... | collective-permute-start | bytes 393224 | tf_op jit(solution)/shard_map/ppermute | solution.py:372
  8.0 1.2 %collective-permute-start.6 = (bf16[64,1024]{1,0:T(8,128)(2,1)S(1)}, bf16[64,1024]{1,0:T(8,128)(2,1)S(1)}, u32[]{:S(2)}, u32[]{:S(2)}) collective-permute-start(bf16[64,1024]{1,0:T(8,128)(2,1)S(1)} %get-tuple-element.58), channel_id=1, source_target_pairs={{0,2},{1,3},{2,0},{3,1},{4,6},{5,7},{6,4},{7,5},{8,10},{9,11},{10,... | collective-permute-start | bytes 393224 | tf_op jit(solution)/shard_map/ppermute | solution.py:372
  9.2 0.0 copy-done.1
  9.2 1.5 %arrange.2 = (bf16[2,1024,128]{2,1,0:T(8,128)(2,1)S(1)}, bf16[2,128,1024]{2,1,0:T(8,128)(2,1)S(1)}) custom-call(bf16[256,8,128]{2,1,0:T(8,128)(2,1)S(1)} %copy-done.1), custom_call_target="tpu_custom_call" | custom-call | tf_op jit(solution)/shard_map/arrange/pallas_call | solution.py:274
  10.7 0.0 collective-permute-done.4.near_ref
  10.7 0.9 %collective-permute-start.7 = (bf16[64,1024]{1,0:T(8,128)(2,1)S(1)}, bf16[64,1024]{1,0:T(8,128)(2,1)S(1)}, u32[]{:S(2)}, u32[]{:S(2)}) collective-permute-start(bf16[64,1024]{1,0:T(8,128)(2,1)S(1)} %get-tuple-element.59), channel_id=1, source_target_pairs={{0,3},{1,2},{2,1},{3,0},{4,7},{5,6},{6,5},{7,4},{8,11},{9,10},{10,... | collective-permute-start | bytes 393224 | tf_op jit(solution)/shard_map/ppermute | solution.py:372
  11.6 0.0 collective-permute-done.3.refs_0_
  11.6 0.2 collective-permute-start.5
  11.8 0.0 collective-permute-done.refs_1_
  11.8 0.0 collective-permute-done.1.refs_1_
  11.8 1.3 %collective-permute-start.2 = (bf16[512,128]{1,0:T(8,128)(2,1)S(1)}, bf16[512,128]{1,0:T(8,128)(2,1)S(1)}, u32[]{:S(2)}, u32[]{:S(2)}) collective-permute-start(bf16[512,128]{1,0:T(8,128)(2,1)S(1)} %collective-permute-done.refs_1_), channel_id=1, source_target_pairs={{0,8},{4,12},{8,0},{12,4},{16,24},{20,28},{24,16},{28,20},{1,9},{5... | collective-permute-start | bytes 393224 | tf_op jit(solution)/shard_map/ppermute | solution.py:372
  13.1 1.2 %collective-permute-start.8 = (bf16[512,128]{1,0:T(8,128)(2,1)S(1)}, bf16[512,128]{1,0:T(8,128)(2,1)S(1)}, u32[]{:S(2)}, u32[]{:S(2)}) collective-permute-start(bf16[512,128]{1,0:T(8,128)(2,1)S(1)} %collective-permute-done.refs_1_), channel_id=1, source_target_pairs={{0,4},{4,0},{8,12},{12,8},{16,20},{20,16},{24,28},{28,24},{1,5},{5... | collective-permute-start | bytes 393224 | tf_op jit(solution)/shard_map/ppermute | solution.py:372
  14.3 0.0 collective-permute-done.6.refs_2_
  14.4 2.2 %collective-permute-done.7.refs_3_ = bf16[64,1024]{1,0:T(8,128)(2,1)S(1)} collective-permute-done((bf16[64,1024]{1,0:T(8,128)(2,1)S(1)}, bf16[64,1024]{1,0:T(8,128)(2,1)S(1)}, u32[]{:S(2)}, u32[]{:S(2)}) %collective-permute-start.7) | collective-permute-done | bytes 131104 | tf_op jit(solution)/shard_map/ppermute | solution.py:372
  16.5 0.4 arrange.3
  16.9 0.0 collective-permute-done.5.refs_3_
  16.9 0.0 collective-permute-done.2.refs_2_
  16.9 0.0 copy-start.2
  16.9 1.1 %collective-permute-start.9 = (bf16[512,128]{1,0:T(8,128)(2,1)S(1)}, bf16[512,128]{1,0:T(8,128)(2,1)S(1)}, u32[]{:S(2)}, u32[]{:S(2)}) collective-permute-start(bf16[512,128]{1,0:T(8,128)(2,1)S(1)} %collective-permute-done.2.refs_2_), channel_id=1, source_target_pairs={{0,4},{4,0},{8,12},{12,8},{16,20},{20,16},{24,28},{28,24},{1,5},{5... | collective-permute-start | bytes 393224 | tf_op jit(solution)/shard_map/ppermute | solution.py:372
  18.0 1.5 %collective-permute-done.8.refs_4_ = bf16[512,128]{1,0:T(8,128)(2,1)S(1)} collective-permute-done((bf16[512,128]{1,0:T(8,128)(2,1)S(1)}, bf16[512,128]{1,0:T(8,128)(2,1)S(1)}, u32[]{:S(2)}, u32[]{:S(2)}) %collective-permute-start.8) | collective-permute-done | bytes 131104 | tf_op jit(solution)/shard_map/ppermute | solution.py:372
  19.5 2.1 %collective-permute-done.9.refs_5_ = bf16[512,128]{1,0:T(8,128)(2,1)S(1)} collective-permute-done((bf16[512,128]{1,0:T(8,128)(2,1)S(1)}, bf16[512,128]{1,0:T(8,128)(2,1)S(1)}, u32[]{:S(2)}, u32[]{:S(2)}) %collective-permute-start.9) | collective-permute-done | bytes 131104 | tf_op jit(solution)/shard_map/ppermute | solution.py:372
  21.6 0.0 copy-done.2
  21.6 10.2 %attention.1 = (bf16[64,1024]{1,0:T(8,128)(2,1)S(1)}, bf16[64,1024]{1,0:T(8,128)(2,1)S(1)}, bf16[64,1024]{1,0:T(8,128)(2,1)S(1)}, bf16[64,1024]{1,0:T(8,128)(2,1...) custom-call(s32[8]{0:T(128)S(1)} %copy-done.2, ...), custom_call_target="tpu_custom_call" | custom-call | flops 7516192768 | bytes 4194304 | tf_op jit(solution)/shard_map/attention/pallas_call | solution.py:181
  31.9 2.9 %collective-permute-start.10 = (bf16[256,256]{1,0:T(8,128)(2,1)S(1)}, bf16[256,256]{1,0:T(8,128)(2,1)S(1)}, u32[]{:S(2)}, u32[]{:S(2)}) collective-permute-start(bf16[256,256]{1,0:T(8,128)(2,1)S(1)} %get-tuple-element.70), channel_id=1, source_target_pairs={{0,4},{4,0},{8,12},{12,8},{16,20},{20,16},{24,28},{28,24},{1,5},{5... | collective-permute-start | bytes 393224 | tf_op jit(solution)/shard_map/ppermute | solution.py:372
  34.8 2.4 %collective-permute-start.11 = (bf16[64,1024]{1,0:T(8,128)(2,1)S(1)}, bf16[64,1024]{1,0:T(8,128)(2,1)S(1)}, u32[]{:S(2)}, u32[]{:S(2)}) collective-permute-start(bf16[64,1024]{1,0:T(8,128)(2,1)S(1)} %get-tuple-element.71), channel_id=1, source_target_pairs={{0,1},{1,0},{2,3},{3,2},{4,5},{5,4},{6,7},{7,6},{8,9},{9,8},{10,11... | collective-permute-start | bytes 393224 | tf_op jit(solution)/shard_map/ppermute | solution.py:372
  37.2 0.0 collective-permute-start.12
  37.2 0.9 %collective-permute-start.13 = (bf16[64,1024]{1,0:T(8,128)(2,1)S(1)}, bf16[64,1024]{1,0:T(8,128)(2,1)S(1)}, u32[]{:S(2)}, u32[]{:S(2)}) collective-permute-start(bf16[64,1024]{1,0:T(8,128)(2,1)S(1)} %get-tuple-element.74), channel_id=1, source_target_pairs={{0,2},{1,3},{2,0},{3,1},{4,6},{5,7},{6,4},{7,5},{8,10},{9,11},{10,... | collective-permute-start | bytes 393224 | tf_op jit(solution)/shard_map/ppermute | solution.py:372
  38.0 0.0 collective-permute-done.10.refs_1_
  38.0 0.1 collective-permute-done.11.refs_1_
  38.2 1.4 %collective-permute-start.15 = (bf16[256,256]{1,0:T(8,128)(2,1)S(1)}, bf16[256,256]{1,0:T(8,128)(2,1)S(1)}, u32[]{:S(2)}, u32[]{:S(2)}) collective-permute-start(bf16[256,256]{1,0:T(8,128)(2,1)S(1)} %get-tuple-element.85), channel_id=1, source_target_pairs={{0,4},{4,0},{8,12},{12,8},{16,20},{20,16},{24,28},{28,24},{1,5},{5... | collective-permute-start | bytes 393224 | tf_op jit(solution)/shard_map/ppermute | solution.py:372
  39.6 4.8 %collective-permute-start.14 = (bf16[64,1024]{1,0:T(8,128)(2,1)S(1)}, bf16[64,1024]{1,0:T(8,128)(2,1)S(1)}, u32[]{:S(2)}, u32[]{:S(2)}) collective-permute-start(bf16[64,1024]{1,0:T(8,128)(2,1)S(1)} %get-tuple-element.76), channel_id=1, source_target_pairs={{0,3},{1,2},{2,1},{3,0},{4,7},{5,6},{6,5},{7,4},{8,11},{9,10},{10,... | collective-permute-start | bytes 393224 | tf_op jit(solution)/shard_map/ppermute | solution.py:372
  44.4 0.7 %collective-permute-start.17 = (bf16[256,256]{1,0:T(8,128)(2,1)S(1)}, bf16[256,256]{1,0:T(8,128)(2,1)S(1)}, u32[]{:S(2)}, u32[]{:S(2)}) collective-permute-start(bf16[256,256]{1,0:T(8,128)(2,1)S(1)} %merge.3), channel_id=1, source_target_pairs={{24,0},{28,4},{25,1},{29,5},{26,2},{30,6},{27,3},{31,7}} | collective-permute-start | bytes 393224 | tf_op jit(solution)/shard_map/ppermute | solution.py:368
  45.1 0.0 collective-permute-done.12.refs_1_
  45.1 0.0 collective-permute-done.13.refs_2_
  45.1 1.3 %collective-permute-start.18 = (bf16[256,256]{1,0:T(8,128)(2,1)S(1)}, bf16[256,256]{1,0:T(8,128)(2,1)S(1)}, u32[]{:S(2)}, u32[]{:S(2)}) collective-permute-start(bf16[256,256]{1,0:T(8,128)(2,1)S(1)} %merge.4), channel_id=1, source_target_pairs={{16,0},{20,4},{24,8},{28,12},{17,1},{21,5},{25,9},{29,13},{18,2},{... | collective-permute-start | bytes 393224 | tf_op jit(solution)/shard_map/ppermute | solution.py:368
  46.4 0.0 collective-permute-done.15.refs_1_
  46.4 0.1 collective-permute-start.16
  46.5 1.9 %collective-permute-start.19 = (bf16[256,256]{1,0:T(8,128)(2,1)S(1)}, bf16[256,256]{1,0:T(8,128)(2,1)S(1)}, u32[]{:S(2)}, u32[]{:S(2)}) collective-permute-start(bf16[256,256]{1,0:T(8,128)(2,1)S(1)} %merge.5), channel_id=1, source_target_pairs={{8,0},{12,4},{16,8},{20,12},{24,16},{28,20},{9,1},{13,5},{17,9},{2... | collective-permute-start | bytes 393224 | tf_op jit(solution)/shard_map/ppermute | solution.py:368
  48.5 0.0 collective-permute-done.14.refs_3_
  48.5 1.5 %join.1 = (bf16[64,4096]{1,0:T(8,128)(2,1)}, bf16[256,8,128]{2,1,0:T(8,128)(2,1)}) custom-call(bf16[64,1024]{1,0:T(8,128)(2,1)S(1)} %get-tuple-element.69.refs_0_, bf16[64,1024]{1,0:T(8,128)(2,1)S(1)} %collective-permute-done.11.refs_1_, bf16[64,1024]{1,0:T(8,128)(2,1)S(1)} %collective-permute-done.13.refs_2_, ...), custom_call_target="tpu_custom_call" | custom-call | tf_op jit(solution)/shard_map/join/pallas_call | solution.py:306
  50.0 0.0 collective-permute-done.17.refs_1_
  50.0 14.0 %collective-permute-done.18.refs_2_ = bf16[256,256]{1,0:T(8,128)(2,1)S(1)} collective-permute-done((bf16[256,256]{1,0:T(8,128)(2,1)S(1)}, bf16[256,256]{1,0:T(8,128)(2,1)S(1)}, u32[]{:S(2)}, u32[]{:S(2)}) %collective-permute-start.18) | collective-permute-done | bytes 131104 | tf_op jit(solution)/shard_map/ppermute | solution.py:368
  64.0 0.0 collective-permute-done.16.refs_0_
  64.0 0.0 collective-permute-done.19.refs_3_
  64.0 0.9 %finish.1 = (bf16[256,128]{1,0:T(8,128)(2,1)}, bf16[256,128]{1,0:T(8,128)(2,1)}) custom-call(f32[256,256]{1,0:T(8,128)S(1)} %get-tuple-element.80.own_ref, bf16[256,256]{1,0:T(8,128)(2,1)S(1)} %collective-permute-done.16.refs_0_, bf16[256,256]{1,0:T(8,128)(2,1)S(1)} %collective-permute-done.17.refs_1_, bf16[256,256]{1,0:T(8,128)(2,1)S(1)} %collective-permute-done.18.refs_2_, ...), custom_call_target="tpu_custom_call" | custom-call | tf_op jit(solution)/shard_map/finish/pallas_call | solution.py:356
  (4 shorter events, 0.1 us)
Async XLA Ops:
  1.5 9.2 %collective-permute-start.4 = (bf16[512,128]{1,0:T(8,128)(2,1)S(1)}, bf16[512,128]{1,0:T(8,128)(2,1)S(1)}, u32[]{:S(2)}, u32[]{:S(2)}) collective-permute-start(bf16[512,128]{1,0:T(8,128)(2,1)S(1)} %pad_maximum_fusion.own_ref), channel_id=1, source_target_pairs={{0,4},{4,0},{8,12},{12,8},{16,20},{20,16},{24,28},{28,24},{1,5},{5... | collective-permute-start | bytes 393224 | tf_op jit(solution)/shard_map/ppermute | solution.py:372
  2.8 8.8 %collective-permute-start.3 = (bf16[512,128]{1,0:T(8,128)(2,1)S(1)}, bf16[512,128]{1,0:T(8,128)(2,1)S(1)}, u32[]{:S(2)}, u32[]{:S(2)}) collective-permute-start(bf16[512,128]{1,0:T(8,128)(2,1)S(1)} %pad_maximum_fusion.own_ref), channel_id=1, source_target_pairs={{0,8},{4,12},{8,0},{12,4},{16,24},{20,28},{24,16},{28,20},{1,9},{5... | collective-permute-start | bytes 393224 | tf_op jit(solution)/shard_map/ppermute | solution.py:372
  3.0 8.8 %collective-permute-start = (bf16[512,128]{1,0:T(8,128)(2,1)S(1)}, bf16[512,128]{1,0:T(8,128)(2,1)S(1)}, u32[]{:S(2)}, u32[]{:S(2)}) collective-permute-start(bf16[512,128]{1,0:T(8,128)(2,1)S(1)} %pad_maximum_fusion.own_ref), channel_id=1, source_target_pairs={{0,16},{4,20},{8,24},{12,28},{16,0},{20,4},{24,8},{28,12},{1,17},{... | collective-permute-start | bytes 393224 | tf_op jit(solution)/shard_map/ppermute | solution.py:372
  5.3 1.0 %copy-start = (bf16[64,4096]{1,0:T(8,128)(2,1)S(1)}, bf16[64,4096]{1,0:T(8,128)(2,1)}, u32[]{:S(2)}) copy-start(bf16[64,4096]{1,0:T(8,128)(2,1)} %grad_ref.1) | copy-start | bytes 1572868
  6.3 2.8 %copy-start.1 = (bf16[256,8,128]{2,1,0:T(8,128)(2,1)S(1)}, bf16[256,8,128]{2,1,0:T(8,128)(2,1)}, u32[]{:S(2)}) copy-start(bf16[256,8,128]{2,1,0:T(8,128)(2,1)} %q_ref.1) | copy-start | bytes 1572868
  6.4 5.4 %collective-permute-start.1 = (bf16[64,1024]{1,0:T(8,128)(2,1)S(1)}, bf16[64,1024]{1,0:T(8,128)(2,1)S(1)}, u32[]{:S(2)}, u32[]{:S(2)}) collective-permute-start(bf16[64,1024]{1,0:T(8,128)(2,1)S(1)} %get-tuple-element.49), channel_id=1, source_target_pairs={{0,1},{1,0},{2,3},{3,2},{4,5},{5,4},{6,7},{7,6},{8,9},{9,8},{10,11... | collective-permute-start | bytes 393224 | tf_op jit(solution)/shard_map/ppermute | solution.py:372
  8.0 6.4 %collective-permute-start.6 = (bf16[64,1024]{1,0:T(8,128)(2,1)S(1)}, bf16[64,1024]{1,0:T(8,128)(2,1)S(1)}, u32[]{:S(2)}, u32[]{:S(2)}) collective-permute-start(bf16[64,1024]{1,0:T(8,128)(2,1)S(1)} %get-tuple-element.58), channel_id=1, source_target_pairs={{0,2},{1,3},{2,0},{3,1},{4,6},{5,7},{6,4},{7,5},{8,10},{9,11},{10,... | collective-permute-start | bytes 393224 | tf_op jit(solution)/shard_map/ppermute | solution.py:372
  10.7 5.8 %collective-permute-start.7 = (bf16[64,1024]{1,0:T(8,128)(2,1)S(1)}, bf16[64,1024]{1,0:T(8,128)(2,1)S(1)}, u32[]{:S(2)}, u32[]{:S(2)}) collective-permute-start(bf16[64,1024]{1,0:T(8,128)(2,1)S(1)} %get-tuple-element.59), channel_id=1, source_target_pairs={{0,3},{1,2},{2,1},{3,0},{4,7},{5,6},{6,5},{7,4},{8,11},{9,10},{10,... | collective-permute-start | bytes 393224 | tf_op jit(solution)/shard_map/ppermute | solution.py:372
  11.6 5.3 %collective-permute-start.5 = (bf16[512,128]{1,0:T(8,128)(2,1)S(1)}, bf16[512,128]{1,0:T(8,128)(2,1)S(1)}, u32[]{:S(2)}, u32[]{:S(2)}) collective-permute-start(bf16[512,128]{1,0:T(8,128)(2,1)S(1)} %collective-permute-done.3.refs_0_), channel_id=1, source_target_pairs={{0,4},{4,0},{8,12},{12,8},{16,20},{20,16},{24,28},{28,24},{1,5},{5... | collective-permute-start | bytes 393224 | tf_op jit(solution)/shard_map/ppermute | solution.py:372
  11.8 5.1 %collective-permute-start.2 = (bf16[512,128]{1,0:T(8,128)(2,1)S(1)}, bf16[512,128]{1,0:T(8,128)(2,1)S(1)}, u32[]{:S(2)}, u32[]{:S(2)}) collective-permute-start(bf16[512,128]{1,0:T(8,128)(2,1)S(1)} %collective-permute-done.refs_1_), channel_id=1, source_target_pairs={{0,8},{4,12},{8,0},{12,4},{16,24},{20,28},{24,16},{28,20},{1,9},{5... | collective-permute-start | bytes 393224 | tf_op jit(solution)/shard_map/ppermute | solution.py:372
  13.1 6.4 %collective-permute-start.8 = (bf16[512,128]{1,0:T(8,128)(2,1)S(1)}, bf16[512,128]{1,0:T(8,128)(2,1)S(1)}, u32[]{:S(2)}, u32[]{:S(2)}) collective-permute-start(bf16[512,128]{1,0:T(8,128)(2,1)S(1)} %collective-permute-done.refs_1_), channel_id=1, source_target_pairs={{0,4},{4,0},{8,12},{12,8},{16,20},{20,16},{24,28},{28,24},{1,5},{5... | collective-permute-start | bytes 393224 | tf_op jit(solution)/shard_map/ppermute | solution.py:372
  16.9 4.7 %copy-start.2 = (s32[8]{0:T(128)S(1)}, s32[8]{0:T(128)}, u32[]{:S(2)}) copy-start(s32[8]{0:T(128)} %doc_ref.1) | copy-start | bytes 100
  16.9 4.7 %collective-permute-start.9 = (bf16[512,128]{1,0:T(8,128)(2,1)S(1)}, bf16[512,128]{1,0:T(8,128)(2,1)S(1)}, u32[]{:S(2)}, u32[]{:S(2)}) collective-permute-start(bf16[512,128]{1,0:T(8,128)(2,1)S(1)} %collective-permute-done.2.refs_2_), channel_id=1, source_target_pairs={{0,4},{4,0},{8,12},{12,8},{16,20},{20,16},{24,28},{28,24},{1,5},{5... | collective-permute-start | bytes 393224 | tf_op jit(solution)/shard_map/ppermute | solution.py:372
  31.9 6.2 %collective-permute-start.10 = (bf16[256,256]{1,0:T(8,128)(2,1)S(1)}, bf16[256,256]{1,0:T(8,128)(2,1)S(1)}, u32[]{:S(2)}, u32[]{:S(2)}) collective-permute-start(bf16[256,256]{1,0:T(8,128)(2,1)S(1)} %get-tuple-element.70), channel_id=1, source_target_pairs={{0,4},{4,0},{8,12},{12,8},{16,20},{20,16},{24,28},{28,24},{1,5},{5... | collective-permute-start | bytes 393224 | tf_op jit(solution)/shard_map/ppermute | solution.py:372
  34.8 3.4 %collective-permute-start.11 = (bf16[64,1024]{1,0:T(8,128)(2,1)S(1)}, bf16[64,1024]{1,0:T(8,128)(2,1)S(1)}, u32[]{:S(2)}, u32[]{:S(2)}) collective-permute-start(bf16[64,1024]{1,0:T(8,128)(2,1)S(1)} %get-tuple-element.71), channel_id=1, source_target_pairs={{0,1},{1,0},{2,3},{3,2},{4,5},{5,4},{6,7},{7,6},{8,9},{9,8},{10,11... | collective-permute-start | bytes 393224 | tf_op jit(solution)/shard_map/ppermute | solution.py:372
  37.2 7.9 %collective-permute-start.12 = (bf16[256,256]{1,0:T(8,128)(2,1)S(1)}, bf16[256,256]{1,0:T(8,128)(2,1)S(1)}, u32[]{:S(2)}, u32[]{:S(2)}) collective-permute-start(bf16[256,256]{1,0:T(8,128)(2,1)S(1)} %get-tuple-element.73), channel_id=1, source_target_pairs={{0,4},{4,0},{8,12},{12,8},{16,20},{20,16},{24,28},{28,24},{1,5},{5... | collective-permute-start | bytes 393224 | tf_op jit(solution)/shard_map/ppermute | solution.py:372
  37.2 7.9 %collective-permute-start.13 = (bf16[64,1024]{1,0:T(8,128)(2,1)S(1)}, bf16[64,1024]{1,0:T(8,128)(2,1)S(1)}, u32[]{:S(2)}, u32[]{:S(2)}) collective-permute-start(bf16[64,1024]{1,0:T(8,128)(2,1)S(1)} %get-tuple-element.74), channel_id=1, source_target_pairs={{0,2},{1,3},{2,0},{3,1},{4,6},{5,7},{6,4},{7,5},{8,10},{9,11},{10,... | collective-permute-start | bytes 393224 | tf_op jit(solution)/shard_map/ppermute | solution.py:372
  38.2 8.2 %collective-permute-start.15 = (bf16[256,256]{1,0:T(8,128)(2,1)S(1)}, bf16[256,256]{1,0:T(8,128)(2,1)S(1)}, u32[]{:S(2)}, u32[]{:S(2)}) collective-permute-start(bf16[256,256]{1,0:T(8,128)(2,1)S(1)} %get-tuple-element.85), channel_id=1, source_target_pairs={{0,4},{4,0},{8,12},{12,8},{16,20},{20,16},{24,28},{28,24},{1,5},{5... | collective-permute-start | bytes 393224 | tf_op jit(solution)/shard_map/ppermute | solution.py:372
  39.6 8.9 %collective-permute-start.14 = (bf16[64,1024]{1,0:T(8,128)(2,1)S(1)}, bf16[64,1024]{1,0:T(8,128)(2,1)S(1)}, u32[]{:S(2)}, u32[]{:S(2)}) collective-permute-start(bf16[64,1024]{1,0:T(8,128)(2,1)S(1)} %get-tuple-element.76), channel_id=1, source_target_pairs={{0,3},{1,2},{2,1},{3,0},{4,7},{5,6},{6,5},{7,4},{8,11},{9,10},{10,... | collective-permute-start | bytes 393224 | tf_op jit(solution)/shard_map/ppermute | solution.py:372
  44.4 5.6 %collective-permute-start.17 = (bf16[256,256]{1,0:T(8,128)(2,1)S(1)}, bf16[256,256]{1,0:T(8,128)(2,1)S(1)}, u32[]{:S(2)}, u32[]{:S(2)}) collective-permute-start(bf16[256,256]{1,0:T(8,128)(2,1)S(1)} %merge.3), channel_id=1, source_target_pairs={{24,0},{28,4},{25,1},{29,5},{26,2},{30,6},{27,3},{31,7}} | collective-permute-start | bytes 393224 | tf_op jit(solution)/shard_map/ppermute | solution.py:368
  45.1 18.9 %collective-permute-start.18 = (bf16[256,256]{1,0:T(8,128)(2,1)S(1)}, bf16[256,256]{1,0:T(8,128)(2,1)S(1)}, u32[]{:S(2)}, u32[]{:S(2)}) collective-permute-start(bf16[256,256]{1,0:T(8,128)(2,1)S(1)} %merge.4), channel_id=1, source_target_pairs={{16,0},{20,4},{24,8},{28,12},{17,1},{21,5},{25,9},{29,13},{18,2},{... | collective-permute-start | bytes 393224 | tf_op jit(solution)/shard_map/ppermute | solution.py:368
  46.4 17.6 %collective-permute-start.16 = (bf16[256,256]{1,0:T(8,128)(2,1)S(1)}, bf16[256,256]{1,0:T(8,128)(2,1)S(1)}, u32[]{:S(2)}, u32[]{:S(2)}) collective-permute-start(bf16[256,256]{1,0:T(8,128)(2,1)S(1)} %get-tuple-element.86), channel_id=1, source_target_pairs={{0,4},{4,0},{8,12},{12,8},{16,20},{20,16},{24,28},{28,24},{1,5},{5... | collective-permute-start | bytes 393224 | tf_op jit(solution)/shard_map/ppermute | solution.py:372
  46.5 17.4 %collective-permute-start.19 = (bf16[256,256]{1,0:T(8,128)(2,1)S(1)}, bf16[256,256]{1,0:T(8,128)(2,1)S(1)}, u32[]{:S(2)}, u32[]{:S(2)}) collective-permute-start(bf16[256,256]{1,0:T(8,128)(2,1)S(1)} %merge.5), channel_id=1, source_target_pairs={{8,0},{12,4},{16,8},{20,12},{24,16},{28,20},{9,1},{13,5},{17,9},{2... | collective-permute-start | bytes 393224 | tf_op jit(solution)/shard_map/ppermute | solution.py:368
where the time goes:
time: 65.6 us; the launch traced here: 64.9 us
  starting transfers between devices  27.7 us (42%)
  waiting for transfers between devices  19.9 us (30%)
  Pallas kernels  14.7 us (22%)
  local copies, waits for them, and re-layouts  1.05 us (2%)
  other arithmetic  0.88 us (1%)
  between operations  0.79 us (1%)
    ppermute x17, starting transfers between devices, exchanged(): lax.ppermute(block, axis, [(i, i ^ by) for i in range(lax.axis_size(axis))])  23.8 us
    ppermute x3, waiting for transfers between devices, shifted(): return lax.ppermute(block, 'ctx', pairs)  14 us
    pallas_call x1, Pallas kernels, attend(): pl.pallas_call(functools.partial(attention_kernel, back=back, whole=whole...  10.2 us
    ppermute x17, waiting for transfers between devices, exchanged(): lax.ppermute(block, axis, [(i, i ^ by) for i in range(lax.axis_size(axis))])  5.89 us
    ppermute x3, starting transfers between devices, shifted(): return lax.ppermute(block, 'ctx', pairs)  3.87 us
    pallas_call x2, Pallas kernels, arrange(): pl.pallas_call(kernel, out_shape=[jax.ShapeDtypeStruct((chunks, rows, wid...  1.86 us
    pallas_call x1, Pallas kernels, join(): pl.pallas_call(join_kernel, out_shape=(jax.ShapeDtypeStruct((rows, size *...  1.5 us
  transfers between devices with their start and end apart: 20, of which 5 were waited for; matrix products, arithmetic and copies ran while one was open for 0% of the time, Pallas kernels for 5%

commit v1 on v0

--- a/solution.py
+++ b/solution.py
@@ -14,6 +14,7 @@
 CHUNK = 128
 LOG2_E = 1.4426950408889634
 SMALL_VMEM = 8 * 1024 * 1024
+KERNEL_VMEM = 16 * 1024 * 1024
 
 
 def dot(a, b):
@@ -31,6 +32,40 @@
 
 def twice(column):
     return jnp.concatenate([column, column], axis=1)
+
+
+def starts_in(doc_ref, positions):
+    end, found = jnp.int32(0), jnp.zeros_like(positions)
+    for i in range(doc_ref.shape[0]):
+        end = end + doc_ref[i]
+        found = jnp.where(positions >= end, end, found)
+    return found
+
+
+def here(tok, back, whole):
+    ctx = lax.axis_index("ctx")
+    parity = lax.rem(ctx, 2)
+    last = ctx // 2 if whole else back
+    base = 0 if whole else (ctx - parity - 2 * back) * tok
+    return parity, last, base, 2 * last + parity
+
+
+def back_tile(i, slot, chunk, width, refs):
+    q_cols, do_rows, do_cols, keys, values, scores, top, delta, dq_acc, d_blocks = refs
+    at = pl.ds(pl.multiple_of(i * TILE, TILE), TILE)
+    probs = jnp.exp2(scores[chunk, i] - twice(top[chunk]))
+    d_probs = dot_nt(do_rows[chunk], values[at, 0:width])
+    d_scores = (probs * (d_probs - twice(delta[chunk]))).astype(jnp.bfloat16)
+    dq_acc[chunk] += dot(d_scores, keys[at, :])
+    d_blocks[slot, 0:width, :] += dot(q_cols[chunk], d_scores)
+    d_blocks[slot, width:, :] += dot(do_cols[chunk], probs.astype(jnp.bfloat16))
+
+
+def put(d_blocks, mine, other, mine_ref, other_ref, width, scale):
+    mine_ref[0:width, :] = d_blocks[mine, 0:width, :] * scale
+    mine_ref[width:, :] = d_blocks[mine, width:, :]
+    other_ref[0:width, :] = (d_blocks[other, 0:width, :] * scale).astype(jnp.bfloat16)
+    other_ref[width:, :] = d_blocks[other, width:, :].astype(jnp.bfloat16)
 
 
 def attention_kernel(
@@ -50,49 +85,36 @@
     scale,
 ):
     arrived, far, refs = refs[:back], refs[back : 2 * back], refs[2 * back :]
-    out_parts, dq_acc, refs = refs[:ranks], refs[ranks], refs[ranks + 1 :]
-    d_refs, refs = refs[: 2 * back + 2], refs[2 * back + 2 :]
-    (o_ref, keys, values, scores, accum, top, delta, d_blocks) = refs
+    out_parts, refs = refs[:ranks], refs[ranks:]
+    (scores, top, delta, keys, values, dq_acc), refs = refs[:6], refs[6:]
+    d_refs, (o_ref, accum, d_blocks) = refs[:-3], refs[-3:]
     tok = own_ref.shape[0] // 2
     part_rows = tok // ranks
-    docs = doc_ref.shape[0]
-    ctx = lax.axis_index("ctx")
     rank = lax.axis_index("head")
-    parity = lax.rem(ctx, 2)
-    base = 0 if whole else (ctx - parity - 2 * back) * tok
-    own = ctx if whole else 2 * back + parity
+    parity, last, base, own = here(tok, back, whole)
+    cut = 2 * (last - 1)
     ones = jnp.ones((width, width), jnp.bfloat16)
-
-    def pair_of(k):
-        return (ctx // 2) ^ k if whole else back - k
 
     values[:, width:] = jnp.ones_like(values[:, width:])
     for k in range(back + 1):
-        pair = pair_of(k)
+        pair = last ^ k if whole else last - k
         mine, other = (own_ref, near_ref) if k == 0 else (arrived[k - 1], far[k - 1])
         for ref, place in ((mine, 2 * pair + parity), (other, 2 * pair + 1 - parity)):
             at = pl.ds(pl.multiple_of(place * tok, tok), tok)
             keys[at, :] = ref[0:tok, :]
             values[at, 0:width] = ref[tok:, :]
     d_blocks[...] = jnp.zeros_like(d_blocks)
+    top[...] = jnp.full_like(top, NEG_FILL)
+    dq_acc[...] = jnp.zeros_like(dq_acc)
 
     def chunk_step(chunk, carry):
-        here = pl.ds(pl.multiple_of(chunk * CHUNK, CHUNK), CHUNK)
-        top[...] = jnp.full_like(top, NEG_FILL)
-
+        rows_at = pl.ds(pl.multiple_of(chunk * CHUNK, CHUNK), CHUNK)
         t_first = base + own * TILE + chunk * CHUNK
         t_last = t_first + CHUNK - 1
         t_col = t_first + lax.broadcasted_iota(jnp.int32, (CHUNK, width), 0)
-        end = jnp.int32(0)
-        start_first, start_last = jnp.int32(0), jnp.int32(0)
-        start_col = jnp.zeros((CHUNK, width), jnp.int32)
-        for i in range(docs):
-            end = end + doc_ref[i]
-            start_first = jnp.where(end <= t_first, end, start_first)
-            start_last = jnp.where(end <= t_last, end, start_last)
-            start_col = jnp.where(t_col >= end, end, start_col)
-        low = jnp.maximum(start_first - base, 0) // TILE
-        clear = jnp.clip((start_last - base + TILE - 1) // TILE, low, own)
+        start_col = starts_in(doc_ref, t_col)
+        low = jnp.maximum(starts_in(doc_ref, t_first) - base, 0) // TILE
+        clear = jnp.clip((starts_in(doc_ref, t_last) - base + TILE - 1) // TILE, low, own)
 
         def score_tile(i, masked):
             at = pl.ds(pl.multiple_of(i * TILE, TILE), TILE)
@@ -107,8 +129,8 @@
                     ],
                     axis=0,
                 )
-            scores[i] = tile
-            top[...] = jnp.maximum(top[...], jnp.maximum(tile[:, :width], tile[:, width:]))
+            scores[chunk, i] = tile
+            top[chunk] = jnp.maximum(top[chunk], jnp.maximum(tile[:, :width], tile[:, width:]))
 
         def edge_step(n, carry):
             score_tile(jnp.where(n < clear - low, low + n, own), True)
@@ -120,12 +142,12 @@
 
         lax.fori_loop(0, clear - low + 1, edge_step, 0)
         lax.fori_loop(clear, own, inner_step, 0)
-        top[...] = jnp.broadcast_to(jnp.max(top[...], axis=1, keepdims=True), top.shape)
+        top[chunk] = jnp.broadcast_to(jnp.max(top[chunk], axis=1, keepdims=True), top.shape[1:])
         accum[...] = jnp.zeros_like(accum)
 
         def weigh_step(i, carry):
             at = pl.ds(pl.multiple_of(i * TILE, TILE), TILE)
-            weights = jnp.exp2(scores[i] - twice(top[...])).astype(jnp.bfloat16)
+            weights = jnp.exp2(scores[chunk, i] - twice(top[chunk])).astype(jnp.bfloat16)
             accum[...] += dot(weights, values[at, :])
             return carry
 
@@ -133,39 +155,31 @@
         total = accum[:, width:]
         out = (accum[:, 0:width] / total).astype(jnp.bfloat16)
         for j in range(heads):
-            o_ref[here, j * width : (j + 1) * width] = out[j * CHUNK : (j + 1) * CHUNK]
-        top[...] = top[...] + jnp.log2(total)
+            o_ref[rows_at, j * width : (j + 1) * width] = out[j * CHUNK : (j + 1) * CHUNK]
+        top[chunk] = top[chunk] + jnp.log2(total)
         product = do_rows[chunk].astype(jnp.float32) * out.astype(jnp.float32)
         coarse = product.astype(jnp.bfloat16)
         fine = (product - coarse.astype(jnp.float32)).astype(jnp.bfloat16)
-        delta[...] = dot(coarse, ones) + dot(fine, ones)
-        dq_acc[chunk] = jnp.zeros(dq_acc.shape[1:], jnp.float32)
+        delta[chunk] = dot(coarse, ones) + dot(fine, ones)
 
         def back_step(i, carry):
-            at = pl.ds(pl.multiple_of(i * TILE, TILE), TILE)
-            probs = jnp.exp2(scores[i] - twice(top[...]))
-            d_probs = dot_nt(do_rows[chunk], values[at, 0:width])
-            d_scores = (probs * (d_probs - twice(delta[...]))).astype(jnp.bfloat16)
-            dq_acc[chunk] += dot(d_scores, keys[at, :])
-            d_blocks[i, 0:width, :] += dot(q_cols[chunk], d_scores)
-            d_blocks[i, width:, :] += dot(do_cols[chunk], probs.astype(jnp.bfloat16))
+            refs = (
+                q_cols, do_rows, do_cols, keys, values, scores, top, delta, dq_acc, d_blocks
+            )
+            back_tile(i, i, chunk, width, refs)
             return carry
 
-        lax.fori_loop(low, own + 1, back_step, 0)
+        lax.fori_loop(low, cut, back_step, 0)
         return carry
 
     lax.fori_loop(0, tok // CHUNK, chunk_step, 0)
     for k in range(ranks):
         at = pl.ds(pl.multiple_of((rank ^ k) * part_rows, part_rows), part_rows)
         out_parts[k][...] = o_ref[at, :]
-    for k in range(back + 1):
-        pair = jnp.maximum(ctx // 2 - k, 0) if whole else back - k
+    for k in range(2, back + 1):
+        pair = jnp.maximum(last - k, 0)
         mine, other = 2 * pair + parity, 2 * pair + 1 - parity
-        mine_ref, other_ref = d_refs[2 * k], d_refs[2 * k + 1]
-        mine_ref[0:width, :] = d_blocks[mine, 0:width, :] * scale
-        mine_ref[width:, :] = d_blocks[mine, width:, :]
-        other_ref[0:width, :] = (d_blocks[other, 0:width, :] * scale).astype(jnp.bfloat16)
-        other_ref[width:, :] = d_blocks[other, width:, :].astype(jnp.bfloat16)
+        put(d_blocks, mine, other, d_refs[2 * k - 4], d_refs[2 * k - 3], width, scale)
 
 
 def attend(doc_lengths, prepared, own, near, arrived, far, ranks, whole):
@@ -178,7 +192,8 @@
     vmem = pl.BlockSpec(memory_space=pltpu.VMEM)
     smem = pl.BlockSpec(memory_space=pltpu.SMEM)
     out_part = jax.ShapeDtypeStruct((tok // ranks, heads * width), jnp.bfloat16)
-    return pl.pallas_call(
+    row_state = jax.ShapeDtypeStruct((chunks, rows, width), jnp.float32)
+    outputs = pl.pallas_call(
         functools.partial(
             attention_kernel,
             back=back,
@@ -190,26 +205,26 @@
         ),
         out_shape=[out_part] * ranks
         + [
-            jax.ShapeDtypeStruct((chunks, rows, width), jnp.float32),
+            jax.ShapeDtypeStruct((chunks, tiles, rows, TILE), jnp.float32),
+            row_state,
+            row_state,
+            jax.ShapeDtypeStruct((span, width), jnp.bfloat16),
+            jax.ShapeDtypeStruct((span, 2 * width), jnp.bfloat16),
+            row_state,
         ]
         + [
             jax.ShapeDtypeStruct((2 * width, tok), dtype)
-            for _ in range(back + 1)
+            for _ in range(back - 1)
             for dtype in (jnp.float32, jnp.bfloat16)
         ],
         in_specs=[smem] + [vmem] * (6 + 2 * back),
-        out_specs=[vmem] * (ranks + 2 * back + 3),
+        out_specs=[vmem] * (ranks + 4 + 2 * back),
         scratch_shapes=[
             pltpu.VMEM((tok, heads * width), jnp.bfloat16),
-            pltpu.VMEM((span, width), jnp.bfloat16),
-            pltpu.VMEM((span, 2 * width), jnp.bfloat16),
-            pltpu.VMEM((tiles, rows, TILE), jnp.float32),
             pltpu.VMEM((rows, 2 * width), jnp.float32),
-            pltpu.VMEM((rows, width), jnp.float32),
-            pltpu.VMEM((rows, width), jnp.float32),
             pltpu.VMEM((tiles, 2 * width, tok), jnp.float32),
         ],
-        compiler_params=pltpu.CompilerParams(vmem_limit_bytes=32 * 1024 * 1024),
+        compiler_params=pltpu.CompilerParams(vmem_limit_bytes=KERNEL_VMEM),
         cost_estimate=pl.CostEstimate(
             flops=14 * tok * heads * width * span,
             bytes_accessed=4 * tok * heads * width * 2 + 4 * span * width * 2,
@@ -217,6 +232,84 @@
         ),
         name="attention",
     )(doc_lengths, *prepared, own, near, *arrived, *far)
+    return outputs[:ranks], outputs[ranks : ranks + 6], outputs[ranks + 6 :]
+
+
+def near_kernel(
+    doc_ref,
+    q_cols,
+    do_rows,
+    do_cols,
+    scores,
+    top,
+    delta,
+    keys,
+    values,
+    dq_far,
+    dq_acc,
+    mine1_ref,
+    other1_ref,
+    mine0_ref,
+    other0_ref,
+    d_blocks,
+    *,
+    back,
+    whole,
+    width,
+    scale,
+):
+    tok = mine1_ref.shape[1]
+    parity, last, base, own = here(tok, back, whole)
+    cut = 2 * (last - 1)
+    d_blocks[...] = jnp.zeros_like(d_blocks)
+    dq_acc[...] = dq_far[...]
+
+    def chunk_step(chunk, carry):
+        t_first = base + own * TILE + chunk * CHUNK
+        low = jnp.maximum(starts_in(doc_ref, t_first) - base, 0) // TILE
+
+        def back_step(i, carry):
+            refs = (
+                q_cols, do_rows, do_cols, keys, values, scores, top, delta, dq_acc, d_blocks
+            )
+            back_tile(i, i - cut, chunk, width, refs)
+            return carry
+
+        lax.fori_loop(jnp.maximum(low, cut), own + 1, back_step, 0)
+        return carry
+
+    lax.fori_loop(0, tok // CHUNK, chunk_step, 0)
+    put(d_blocks, parity, 1 - parity, mine1_ref, other1_ref, width, scale)
+    put(d_blocks, 2 + parity, 3 - parity, mine0_ref, other0_ref, width, scale)
+
+
+def attend_near(doc_lengths, prepared, state, back, whole):
+    _, q_cols, do_rows, do_cols = prepared
+    chunks, rows, width = do_rows.shape
+    tok = chunks * CHUNK
+    vmem = pl.BlockSpec(memory_space=pltpu.VMEM)
+    smem = pl.BlockSpec(memory_space=pltpu.SMEM)
+    return pl.pallas_call(
+        functools.partial(
+            near_kernel, back=back, whole=whole, width=width, scale=1.0 / math.sqrt(width)
+        ),
+        out_shape=[jax.ShapeDtypeStruct((chunks, rows, width), jnp.float32)]
+        + [
+            jax.ShapeDtypeStruct((2 * width, tok), dtype)
+            for _ in range(2)
+            for dtype in (jnp.float32, jnp.bfloat16)
+        ],
+        in_specs=[smem] + [vmem] * 9,
+        out_specs=[vmem] * 5,
+        scratch_shapes=[pltpu.VMEM((4, 2 * width, tok), jnp.float32)],
+        compiler_params=pltpu.CompilerParams(vmem_limit_bytes=KERNEL_VMEM),
+        cost_estimate=pl.CostEstimate(
+            flops=8 * chunks * rows * width * 4 * tok,
+            bytes_accessed=4 * chunks * rows * width * 2,
+            transcendentals=4 * chunks * rows * tok,
+        ),
+        name="near",
+    )(doc_lengths, q_cols, do_rows, do_cols, *state)
 
 
 def split_kernel(grad_ref, *part_refs):
@@ -416,12 +509,14 @@
         far = [far_beside, far_across, far_passed]
     else:
         far = [exchanged(block, "ctx", 1) for block in arrived]
-    outputs = attend(doc_lengths, prepared, own, near, arrived, far, ranks, whole)
-    outs, dq_rows, parts = list(outputs[:ranks]), outputs[ranks], outputs[ranks + 1 :]
-    mine, other = list(parts[0::2]), list(parts[1::2])
+    outs, state, parts = attend(doc_lengths, prepared, own, near, arrived, far, ranks, whole)
+    outs, far_parts = list(outs), list(parts)
+    dq_rows, mine1, other1, mine0, other0 = attend_near(
+        doc_lengths, prepared, state, back, whole
+    )
     outs = [part if k == 0 else exchanged(part, "head", k) for k, part in enumerate(outs)]
-    for k in range(back, 1, -1):
-        other[k] = exchanged(other[k], "ctx", 1)
+    mine = [mine0, mine1] + far_parts[0::2]
+    other = [other0, other1] + [exchanged(part, "ctx", 1) for part in far_parts[1::2]]
     other[back], *outs[1:2] = after(other[back], *outs[1:2])
     returned = []
     for k in range(back, 0, -1):

time: 65.6 us -> 65 us (level)
  the two profiles are of different devices: /device:TPU:9 before, /device:TPU:0 now
where the time goes in v1:
time: 65 us; the launch traced here: 65.8 us
  starting transfers between devices  25.8 us (40%)
  waiting for transfers between devices  25.4 us (39%)
  Pallas kernels  10.2 us (16%)
  local copies, waits for them, and re-layouts  2.74 us (4%)
  other arithmetic  0.88 us (1%)
  between operations  0.77 us (1%)
    ppermute x17, starting transfers between devices, exchanged(): lax.ppermute(block, axis, [(i, i ^ by) for i in range(lax.axis_size(axis))])  21.9 us
    ppermute x3, waiting for transfers between devices, shifted(): return lax.ppermute(block, 'ctx', pairs)  17 us
    ppermute x17, waiting for transfers between devices, exchanged(): lax.ppermute(block, axis, [(i, i ^ by) for i in range(lax.axis_size(axis))])  8.4 us
    ppermute x3, starting transfers between devices, shifted(): return lax.ppermute(block, 'ctx', pairs)  3.88 us
    pallas_call x1, Pallas kernels, attend(): pl.pallas_call(functools.partial(attention_kernel, back=back, whole=whole...  3.64 us
    unnamed x6, local copies, waits for them, and re-layouts  2.74 us
    pallas_call x1, Pallas kernels, attend_near(): pl.pallas_call(functools.partial(near_kernel, back=back, whole=whole, wid...  2.17 us
    pallas_call x2, Pallas kernels, arrange(): pl.pallas_call(kernel, out_shape=[jax.ShapeDtypeStruct((chunks, rows, wid...  1.87 us
  transfers between devices with their start and end apart: 20, of which 7 were waited for; matrix products, arithmetic and copies ran while one was open for 0% of the time, Pallas kernels for 9%

profile of v1, /device:TPU:0, one launch (start us, length us, event | category | flops | bytes accessed | tf_op | source)
XLA Modules:
  0.0 65.8 jit_solution(7238053276299945039)
XLA Ops:
  0.6 0.9 %pad_maximum_fusion.own_ref = bf16[512,128]{1,0:T(8,128)(2,1)S(1)} fusion(bf16[256,128]{1,0:T(8,128)(2,1)} %bitcast.4, bf16[256,128]{1,0:T(8,128)(2,1)} %bitcast.5), kind=kLoop, calls=%fused_computation | loop fusion | flops 262144 | bytes 262144 | tf_op jit(solution)/shard_map/concatenate | solution.py:479
  1.5 3.0 %collective-permute-start.4 = (bf16[512,128]{1,0:T(8,128)(2,1)S(1)}, bf16[512,128]{1,0:T(8,128)(2,1)S(1)}, u32[]{:S(2)}, u32[]{:S(2)}) collective-permute-start(bf16[512,128]{1,0:T(8,128)(2,1)S(1)} %pad_maximum_fusion.own_ref), channel_id=1, source_target_pairs={{0,4},{4,0},{8,12},{12,8},{16,20},{20,16},{24,28},{28,24},{1,5},{5... | collective-permute-start | bytes 393224 | tf_op jit(solution)/shard_map/ppermute | solution.py:465
  4.5 1.6 %collective-permute-start.3 = (bf16[512,128]{1,0:T(8,128)(2,1)S(1)}, bf16[512,128]{1,0:T(8,128)(2,1)S(1)}, u32[]{:S(2)}, u32[]{:S(2)}) collective-permute-start(bf16[512,128]{1,0:T(8,128)(2,1)S(1)} %pad_maximum_fusion.own_ref), channel_id=1, source_target_pairs={{0,8},{4,12},{8,0},{12,4},{16,24},{20,28},{24,16},{28,20},{1,9},{5... | collective-permute-start | bytes 393224 | tf_op jit(solution)/shard_map/ppermute | solution.py:465
  6.1 2.6 %collective-permute-start = (bf16[512,128]{1,0:T(8,128)(2,1)S(1)}, bf16[512,128]{1,0:T(8,128)(2,1)S(1)}, u32[]{:S(2)}, u32[]{:S(2)}) collective-permute-start(bf16[512,128]{1,0:T(8,128)(2,1)S(1)} %pad_maximum_fusion.own_ref), channel_id=1, source_target_pairs={{0,16},{4,20},{8,24},{12,28},{16,0},{20,4},{24,8},{28,12},{1,17},{... | collective-permute-start | bytes 393224 | tf_op jit(solution)/shard_map/ppermute | solution.py:465
  8.7 0.0 copy-start
  8.7 1.0 %copy-done = bf16[64,4096]{1,0:T(8,128)(2,1)S(1)} copy-done((bf16[64,4096]{1,0:T(8,128)(2,1)S(1)}, bf16[64,4096]{1,0:T(8,128)(2,1)}, u32[]{:S(2)}) %copy-start) | copy-done | bytes 524312
  9.8 0.1 collective-permute-start.1
  9.9 1.6 %collective-permute-start.6 = (bf16[64,1024]{1,0:T(8,128)(2,1)S(1)}, bf16[64,1024]{1,0:T(8,128)(2,1)S(1)}, u32[]{:S(2)}, u32[]{:S(2)}) collective-permute-start(bf16[64,1024]{1,0:T(8,128)(2,1)S(1)} %get-tuple-element.64), channel_id=1, source_target_pairs={{0,2},{1,3},{2,0},{3,1},{4,6},{5,7},{6,4},{7,5},{8,10},{9,11},{10,... | collective-permute-start | bytes 393224 | tf_op jit(solution)/shard_map/ppermute | solution.py:465
  11.4 0.0 copy-start.1
  11.4 1.0 %copy-done.1 = bf16[256,8,128]{2,1,0:T(8,128)(2,1)S(1)} copy-done((bf16[256,8,128]{2,1,0:T(8,128)(2,1)S(1)}, bf16[256,8,128]{2,1,0:T(8,128)(2,1)}, u32[]{:S(2)}) %copy-start.1) | copy-done | bytes 524312
  12.5 1.5 %arrange.2 = (bf16[2,1024,128]{2,1,0:T(8,128)(2,1)S(1)}, bf16[2,128,1024]{2,1,0:T(8,128)(2,1)S(1)}) custom-call(bf16[256,8,128]{2,1,0:T(8,128)(2,1)S(1)} %copy-done.1), custom_call_target="tpu_custom_call" | custom-call | tf_op jit(solution)/shard_map/arrange/pallas_call | solution.py:367
  14.0 0.0 collective-permute-done.4.near_ref
  14.0 0.4 collective-permute-start.7
  14.4 0.0 collective-permute-done.3.refs_0_
  14.4 0.5 collective-permute-start.5
  14.9 0.0 collective-permute-done.refs_1_
  14.9 0.0 collective-permute-done.1.refs_1_
  14.9 0.4 collective-permute-start.2
  15.3 1.5 %collective-permute-start.8 = (bf16[512,128]{1,0:T(8,128)(2,1)S(1)}, bf16[512,128]{1,0:T(8,128)(2,1)S(1)}, u32[]{:S(2)}, u32[]{:S(2)}) collective-permute-start(bf16[512,128]{1,0:T(8,128)(2,1)S(1)} %collective-permute-done.refs_1_), channel_id=1, source_target_pairs={{0,4},{4,0},{8,12},{12,8},{16,20},{20,16},{24,28},{28,24},{1,5},{5... | collective-permute-start | bytes 393224 | tf_op jit(solution)/shard_map/ppermute | solution.py:465
  16.8 0.0 collective-permute-done.6.refs_2_
  16.8 2.7 %collective-permute-done.7.refs_3_ = bf16[64,1024]{1,0:T(8,128)(2,1)S(1)} collective-permute-done((bf16[64,1024]{1,0:T(8,128)(2,1)S(1)}, bf16[64,1024]{1,0:T(8,128)(2,1)S(1)}, u32[]{:S(2)}, u32[]{:S(2)}) %collective-permute-start.7) | collective-permute-done | bytes 131104 | tf_op jit(solution)/shard_map/ppermute | solution.py:465
  19.6 0.4 arrange.3
  20.0 0.7 %collective-permute-done.5.refs_3_ = bf16[512,128]{1,0:T(8,128)(2,1)S(1)} collective-permute-done((bf16[512,128]{1,0:T(8,128)(2,1)S(1)}, bf16[512,128]{1,0:T(8,128)(2,1)S(1)}, u32[]{:S(2)}, u32[]{:S(2)}) %collective-permute-start.5) | collective-permute-done | bytes 131104 | tf_op jit(solution)/shard_map/ppermute | solution.py:465
  20.7 0.0 collective-permute-done.2.refs_2_
  20.7 1.2 %collective-permute-start.9 = (bf16[512,128]{1,0:T(8,128)(2,1)S(1)}, bf16[512,128]{1,0:T(8,128)(2,1)S(1)}, u32[]{:S(2)}, u32[]{:S(2)}) collective-permute-start(bf16[512,128]{1,0:T(8,128)(2,1)S(1)} %collective-permute-done.2.refs_2_), channel_id=1, source_target_pairs={{0,4},{4,0},{8,12},{12,8},{16,20},{20,16},{24,28},{28,24},{1,5},{5... | collective-permute-start | bytes 393224 | tf_op jit(solution)/shard_map/ppermute | solution.py:465
  21.9 1.1 %collective-permute-done.8.refs_4_ = bf16[512,128]{1,0:T(8,128)(2,1)S(1)} collective-permute-done((bf16[512,128]{1,0:T(8,128)(2,1)S(1)}, bf16[512,128]{1,0:T(8,128)(2,1)S(1)}, u32[]{:S(2)}, u32[]{:S(2)}) %collective-permute-start.8) | collective-permute-done | bytes 131104 | tf_op jit(solution)/shard_map/ppermute | solution.py:465
  22.9 2.9 %collective-permute-done.9.refs_5_ = bf16[512,128]{1,0:T(8,128)(2,1)S(1)} collective-permute-done((bf16[512,128]{1,0:T(8,128)(2,1)S(1)}, bf16[512,128]{1,0:T(8,128)(2,1)S(1)}, u32[]{:S(2)}, u32[]{:S(2)}) %collective-permute-start.9) | collective-permute-done | bytes 131104 | tf_op jit(solution)/shard_map/ppermute | solution.py:465
  25.8 0.0 copy-start.2
  25.8 0.7 copy-done.2
  26.5 3.6 %attention.1 = (bf16[64,1024]{1,0:T(8,128)(2,1)S(1)}, bf16[64,1024]{1,0:T(8,128)(2,1)S(1)}, bf16[64,1024]{1,0:T(8,128)(2,1)S(1)}, bf16[64,1024]{1,0:T(8,128)(2,1...) custom-call(s32[8]{0:T(128)S(1)} %copy-done.2, ...), custom_call_target="tpu_custom_call" | custom-call | flops 7516192768 | bytes 4194304 | tf_op jit(solution)/shard_map/attention/pallas_call | solution.py:196
  30.1 2.4 %collective-permute-start.10 = (bf16[256,256]{1,0:T(8,128)(2,1)S(1)}, bf16[256,256]{1,0:T(8,128)(2,1)S(1)}, u32[]{:S(2)}, u32[]{:S(2)}) collective-permute-start(bf16[256,256]{1,0:T(8,128)(2,1)S(1)} %get-tuple-element.76), channel_id=1, source_target_pairs={{0,4},{4,0},{8,12},{12,8},{16,20},{20,16},{24,28},{28,24},{1,5},{5... | collective-permute-start | bytes 393224 | tf_op jit(solution)/shard_map/ppermute | solution.py:465
  32.5 0.0 collective-permute-start.11
  32.5 0.2 collective-permute-start.12
  32.6 1.5 %collective-permute-start.13 = (bf16[64,1024]{1,0:T(8,128)(2,1)S(1)}, bf16[64,1024]{1,0:T(8,128)(2,1)S(1)}, u32[]{:S(2)}, u32[]{:S(2)}) collective-permute-start(bf16[64,1024]{1,0:T(8,128)(2,1)S(1)} %get-tuple-element.80), channel_id=1, source_target_pairs={{0,2},{1,3},{2,0},{3,1},{4,6},{5,7},{6,4},{7,5},{8,10},{9,11},{10,... | collective-permute-start | bytes 393224 | tf_op jit(solution)/shard_map/ppermute | solution.py:465
  34.1 2.2 %near.1 = (f32[2,1024,128]{2,1,0:T(8,128)S(1)}, f32[256,256]{1,0:T(8,128)S(1)}, bf16[256,256]{1,0:T(8,128)(2,1)S(1)}, f32[256,256]{1,0:T(8,128)S(1)}, bf16[256,256]{1,0:T(8,128)(2,1)S(1)}) custom-call(s32[8]{0:T(128)S(1)} %copy-done.2, bf16[2,128,1024]{2,1,0:T(8,128)(2,1)S(1)} %get-tuple-element.69.q_cols, ...), custom_call_target="tpu_custom_call" | custom-call | flops 2147483648 | bytes 2097152 | tf_op jit(solution)/shard_map/near/pallas_call | solution.py:292
  36.3 0.0 collective-permute-done.10.refs_1_
  36.3 0.0 collective-permute-done.11.refs_1_
  36.4 3.3 %collective-permute-start.15 = (bf16[256,256]{1,0:T(8,128)(2,1)S(1)}, bf16[256,256]{1,0:T(8,128)(2,1)S(1)}, u32[]{:S(2)}, u32[]{:S(2)}) collective-permute-start(bf16[256,256]{1,0:T(8,128)(2,1)S(1)} %get-tuple-element.97), channel_id=1, source_target_pairs={{0,4},{4,0},{8,12},{12,8},{16,20},{20,16},{24,28},{28,24},{1,5},{5... | collective-permute-start | bytes 393224 | tf_op jit(solution)/shard_map/ppermute | solution.py:465
  39.7 0.0 collective-permute-start.14
  39.7 0.0 collective-permute-done.12.refs_1_
  39.7 0.0 collective-permute-done.13.refs_2_
  39.7 1.3 %collective-permute-start.18 = (bf16[256,256]{1,0:T(8,128)(2,1)S(1)}, bf16[256,256]{1,0:T(8,128)(2,1)S(1)}, u32[]{:S(2)}, u32[]{:S(2)}) collective-permute-start(bf16[256,256]{1,0:T(8,128)(2,1)S(1)} %merge.4), channel_id=1, source_target_pairs={{16,0},{20,4},{24,8},{28,12},{17,1},{21,5},{25,9},{29,13},{18,2},{... | collective-permute-start | bytes 393224 | tf_op jit(solution)/shard_map/ppermute | solution.py:461
  41.0 1.3 %collective-permute-start.17 = (bf16[256,256]{1,0:T(8,128)(2,1)S(1)}, bf16[256,256]{1,0:T(8,128)(2,1)S(1)}, u32[]{:S(2)}, u32[]{:S(2)}) collective-permute-start(bf16[256,256]{1,0:T(8,128)(2,1)S(1)} %merge.3), channel_id=1, source_target_pairs={{24,0},{28,4},{25,1},{29,5},{26,2},{30,6},{27,3},{31,7}} | collective-permute-start | bytes 393224 | tf_op jit(solution)/shard_map/ppermute | solution.py:461
  42.3 1.0 %collective-permute-done.15.refs_1_ = bf16[256,256]{1,0:T(8,128)(2,1)S(1)} collective-permute-done((bf16[256,256]{1,0:T(8,128)(2,1)S(1)}, bf16[256,256]{1,0:T(8,128)(2,1)S(1)}, u32[]{:S(2)}, u32[]{:S(2)}) %collective-permute-start.15) | collective-permute-done | bytes 131104 | tf_op jit(solution)/shard_map/ppermute | solution.py:465
  43.3 1.7 %collective-permute-start.16 = (bf16[256,256]{1,0:T(8,128)(2,1)S(1)}, bf16[256,256]{1,0:T(8,128)(2,1)S(1)}, u32[]{:S(2)}, u32[]{:S(2)}) collective-permute-start(bf16[256,256]{1,0:T(8,128)(2,1)S(1)} %get-tuple-element.98), channel_id=1, source_target_pairs={{0,4},{4,0},{8,12},{12,8},{16,20},{20,16},{24,28},{28,24},{1,5},{5... | collective-permute-start | bytes 393224 | tf_op jit(solution)/shard_map/ppermute | solution.py:465
  45.1 1.3 %collective-permute-start.19 = (bf16[256,256]{1,0:T(8,128)(2,1)S(1)}, bf16[256,256]{1,0:T(8,128)(2,1)S(1)}, u32[]{:S(2)}, u32[]{:S(2)}) collective-permute-start(bf16[256,256]{1,0:T(8,128)(2,1)S(1)} %merge.5), channel_id=1, source_target_pairs={{8,0},{12,4},{16,8},{20,12},{24,16},{28,20},{9,1},{13,5},{17,9},{2... | collective-permute-start | bytes 393224 | tf_op jit(solution)/shard_map/ppermute | solution.py:461
  46.4 0.0 collective-permute-done.14.refs_3_
  46.4 1.5 %join.1 = (bf16[64,4096]{1,0:T(8,128)(2,1)}, bf16[256,8,128]{2,1,0:T(8,128)(2,1)}) custom-call(bf16[64,1024]{1,0:T(8,128)(2,1)S(1)} %get-tuple-element.75.refs_0_, bf16[64,1024]{1,0:T(8,128)(2,1)S(1)} %collective-permute-done.11.refs_1_, bf16[64,1024]{1,0:T(8,128)(2,1)S(1)} %collective-permute-done.13.refs_2_, ...), custom_call_target="tpu_custom_call" | custom-call | tf_op jit(solution)/shard_map/join/pallas_call | solution.py:399
  47.9 8.5 %collective-permute-done.18.refs_2_ = bf16[256,256]{1,0:T(8,128)(2,1)S(1)} collective-permute-done((bf16[256,256]{1,0:T(8,128)(2,1)S(1)}, bf16[256,256]{1,0:T(8,128)(2,1)S(1)}, u32[]{:S(2)}, u32[]{:S(2)}) %collective-permute-start.18) | collective-permute-done | bytes 131104 | tf_op jit(solution)/shard_map/ppermute | solution.py:461
  56.3 8.5 %collective-permute-done.17.refs_1_ = bf16[256,256]{1,0:T(8,128)(2,1)S(1)} collective-permute-done((bf16[256,256]{1,0:T(8,128)(2,1)S(1)}, bf16[256,256]{1,0:T(8,128)(2,1)S(1)}, u32[]{:S(2)}, u32[]{:S(2)}) %collective-permute-start.17) | collective-permute-done | bytes 131104 | tf_op jit(solution)/shard_map/ppermute | solution.py:461
  64.9 0.0 collective-permute-done.16.refs_0_
  64.9 0.0 collective-permute-done.19.refs_3_
  64.9 0.9 %finish.1 = (bf16[256,128]{1,0:T(8,128)(2,1)}, bf16[256,128]{1,0:T(8,128)(2,1)}) custom-call(f32[256,256]{1,0:T(8,128)S(1)} %get-tuple-element.92.own_ref, bf16[256,256]{1,0:T(8,128)(2,1)S(1)} %collective-permute-done.16.refs_0_, bf16[256,256]{1,0:T(8,128)(2,1)S(1)} %collective-permute-done.17.refs_1_, bf16[256,256]{1,0:T(8,128)(2,1)S(1)} %collective-permute-done.18.refs_2_, ...), custom_call_target="tpu_custom_call" | custom-call | tf_op jit(solution)/shard_map/finish/pallas_call | solution.py:449
  (4 shorter events, 0.1 us)
Async XLA Ops:
  1.5 12.5 %collective-permute-start.4 = (bf16[512,128]{1,0:T(8,128)(2,1)S(1)}, bf16[512,128]{1,0:T(8,128)(2,1)S(1)}, u32[]{:S(2)}, u32[]{:S(2)}) collective-permute-start(bf16[512,128]{1,0:T(8,128)(2,1)S(1)} %pad_maximum_fusion.own_ref), channel_id=1, source_target_pairs={{0,4},{4,0},{8,12},{12,8},{16,20},{20,16},{24,28},{28,24},{1,5},{5... | collective-permute-start | bytes 393224 | tf_op jit(solution)/shard_map/ppermute | solution.py:465
  4.5 9.8 %collective-permute-start.3 = (bf16[512,128]{1,0:T(8,128)(2,1)S(1)}, bf16[512,128]{1,0:T(8,128)(2,1)S(1)}, u32[]{:S(2)}, u32[]{:S(2)}) collective-permute-start(bf16[512,128]{1,0:T(8,128)(2,1)S(1)} %pad_maximum_fusion.own_ref), channel_id=1, source_target_pairs={{0,8},{4,12},{8,0},{12,4},{16,24},{20,28},{24,16},{28,20},{1,9},{5... | collective-permute-start | bytes 393224 | tf_op jit(solution)/shard_map/ppermute | solution.py:465
  6.1 8.7 %collective-permute-start = (bf16[512,128]{1,0:T(8,128)(2,1)S(1)}, bf16[512,128]{1,0:T(8,128)(2,1)S(1)}, u32[]{:S(2)}, u32[]{:S(2)}) collective-permute-start(bf16[512,128]{1,0:T(8,128)(2,1)S(1)} %pad_maximum_fusion.own_ref), channel_id=1, source_target_pairs={{0,16},{4,20},{8,24},{12,28},{16,0},{20,4},{24,8},{28,12},{1,17},{... | collective-permute-start | bytes 393224 | tf_op jit(solution)/shard_map/ppermute | solution.py:465
  8.7 1.0 %copy-start = (bf16[64,4096]{1,0:T(8,128)(2,1)S(1)}, bf16[64,4096]{1,0:T(8,128)(2,1)}, u32[]{:S(2)}) copy-start(bf16[64,4096]{1,0:T(8,128)(2,1)} %grad_ref.1) | copy-start | bytes 1572868
  9.8 5.1 %collective-permute-start.1 = (bf16[64,1024]{1,0:T(8,128)(2,1)S(1)}, bf16[64,1024]{1,0:T(8,128)(2,1)S(1)}, u32[]{:S(2)}, u32[]{:S(2)}) collective-permute-start(bf16[64,1024]{1,0:T(8,128)(2,1)S(1)} %get-tuple-element.55), channel_id=1, source_target_pairs={{0,1},{1,0},{2,3},{3,2},{4,5},{5,4},{6,7},{7,6},{8,9},{9,8},{10,11... | collective-permute-start | bytes 393224 | tf_op jit(solution)/shard_map/ppermute | solution.py:465
  9.9 7.0 %collective-permute-start.6 = (bf16[64,1024]{1,0:T(8,128)(2,1)S(1)}, bf16[64,1024]{1,0:T(8,128)(2,1)S(1)}, u32[]{:S(2)}, u32[]{:S(2)}) collective-permute-start(bf16[64,1024]{1,0:T(8,128)(2,1)S(1)} %get-tuple-element.64), channel_id=1, source_target_pairs={{0,2},{1,3},{2,0},{3,1},{4,6},{5,7},{6,4},{7,5},{8,10},{9,11},{10,... | collective-permute-start | bytes 393224 | tf_op jit(solution)/shard_map/ppermute | solution.py:465
  11.4 1.0 %copy-start.1 = (bf16[256,8,128]{2,1,0:T(8,128)(2,1)S(1)}, bf16[256,8,128]{2,1,0:T(8,128)(2,1)}, u32[]{:S(2)}) copy-start(bf16[256,8,128]{2,1,0:T(8,128)(2,1)} %q_ref.1) | copy-start | bytes 1572868
  14.0 5.6 %collective-permute-start.7 = (bf16[64,1024]{1,0:T(8,128)(2,1)S(1)}, bf16[64,1024]{1,0:T(8,128)(2,1)S(1)}, u32[]{:S(2)}, u32[]{:S(2)}) collective-permute-start(bf16[64,1024]{1,0:T(8,128)(2,1)S(1)} %get-tuple-element.65), channel_id=1, source_target_pairs={{0,3},{1,2},{2,1},{3,0},{4,7},{5,6},{6,5},{7,4},{8,11},{9,10},{10,... | collective-permute-start | bytes 393224 | tf_op jit(solution)/shard_map/ppermute | solution.py:465
  14.4 6.3 %collective-permute-start.5 = (bf16[512,128]{1,0:T(8,128)(2,1)S(1)}, bf16[512,128]{1,0:T(8,128)(2,1)S(1)}, u32[]{:S(2)}, u32[]{:S(2)}) collective-permute-start(bf16[512,128]{1,0:T(8,128)(2,1)S(1)} %collective-permute-done.3.refs_0_), channel_id=1, source_target_pairs={{0,4},{4,0},{8,12},{12,8},{16,20},{20,16},{24,28},{28,24},{1,5},{5... | collective-permute-start | bytes 393224 | tf_op jit(solution)/shard_map/ppermute | solution.py:465
  14.9 5.8 %collective-permute-start.2 = (bf16[512,128]{1,0:T(8,128)(2,1)S(1)}, bf16[512,128]{1,0:T(8,128)(2,1)S(1)}, u32[]{:S(2)}, u32[]{:S(2)}) collective-permute-start(bf16[512,128]{1,0:T(8,128)(2,1)S(1)} %collective-permute-done.refs_1_), channel_id=1, source_target_pairs={{0,8},{4,12},{8,0},{12,4},{16,24},{20,28},{24,16},{28,20},{1,9},{5... | collective-permute-start | bytes 393224 | tf_op jit(solution)/shard_map/ppermute | solution.py:465
  15.3 7.6 %collective-permute-start.8 = (bf16[512,128]{1,0:T(8,128)(2,1)S(1)}, bf16[512,128]{1,0:T(8,128)(2,1)S(1)}, u32[]{:S(2)}, u32[]{:S(2)}) collective-permute-start(bf16[512,128]{1,0:T(8,128)(2,1)S(1)} %collective-permute-done.refs_1_), channel_id=1, source_target_pairs={{0,4},{4,0},{8,12},{12,8},{16,20},{20,16},{24,28},{28,24},{1,5},{5... | collective-permute-start | bytes 393224 | tf_op jit(solution)/shard_map/ppermute | solution.py:465
  20.7 5.2 %collective-permute-start.9 = (bf16[512,128]{1,0:T(8,128)(2,1)S(1)}, bf16[512,128]{1,0:T(8,128)(2,1)S(1)}, u32[]{:S(2)}, u32[]{:S(2)}) collective-permute-start(bf16[512,128]{1,0:T(8,128)(2,1)S(1)} %collective-permute-done.2.refs_2_), channel_id=1, source_target_pairs={{0,4},{4,0},{8,12},{12,8},{16,20},{20,16},{24,28},{28,24},{1,5},{5... | collective-permute-start | bytes 393224 | tf_op jit(solution)/shard_map/ppermute | solution.py:465
  25.8 0.7 copy-start.2
  30.1 6.2 %collective-permute-start.10 = (bf16[256,256]{1,0:T(8,128)(2,1)S(1)}, bf16[256,256]{1,0:T(8,128)(2,1)S(1)}, u32[]{:S(2)}, u32[]{:S(2)}) collective-permute-start(bf16[256,256]{1,0:T(8,128)(2,1)S(1)} %get-tuple-element.76), channel_id=1, source_target_pairs={{0,4},{4,0},{8,12},{12,8},{16,20},{20,16},{24,28},{28,24},{1,5},{5... | collective-permute-start | bytes 393224 | tf_op jit(solution)/shard_map/ppermute | solution.py:465
  32.5 3.8 %collective-permute-start.11 = (bf16[64,1024]{1,0:T(8,128)(2,1)S(1)}, bf16[64,1024]{1,0:T(8,128)(2,1)S(1)}, u32[]{:S(2)}, u32[]{:S(2)}) collective-permute-start(bf16[64,1024]{1,0:T(8,128)(2,1)S(1)} %get-tuple-element.77), channel_id=1, source_target_pairs={{0,1},{1,0},{2,3},{3,2},{4,5},{5,4},{6,7},{7,6},{8,9},{9,8},{10,11... | collective-permute-start | bytes 393224 | tf_op jit(solution)/shard_map/ppermute | solution.py:465
  32.5 7.2 %collective-permute-start.12 = (bf16[256,256]{1,0:T(8,128)(2,1)S(1)}, bf16[256,256]{1,0:T(8,128)(2,1)S(1)}, u32[]{:S(2)}, u32[]{:S(2)}) collective-permute-start(bf16[256,256]{1,0:T(8,128)(2,1)S(1)} %get-tuple-element.79), channel_id=1, source_target_pairs={{0,4},{4,0},{8,12},{12,8},{16,20},{20,16},{24,28},{28,24},{1,5},{5... | collective-permute-start | bytes 393224 | tf_op jit(solution)/shard_map/ppermute | solution.py:465
  32.6 7.1 %collective-permute-start.13 = (bf16[64,1024]{1,0:T(8,128)(2,1)S(1)}, bf16[64,1024]{1,0:T(8,128)(2,1)S(1)}, u32[]{:S(2)}, u32[]{:S(2)}) collective-permute-start(bf16[64,1024]{1,0:T(8,128)(2,1)S(1)} %get-tuple-element.80), channel_id=1, source_target_pairs={{0,2},{1,3},{2,0},{3,1},{4,6},{5,7},{6,4},{7,5},{8,10},{9,11},{10,... | collective-permute-start | bytes 393224 | tf_op jit(solution)/shard_map/ppermute | solution.py:465
  36.4 6.9 %collective-permute-start.15 = (bf16[256,256]{1,0:T(8,128)(2,1)S(1)}, bf16[256,256]{1,0:T(8,128)(2,1)S(1)}, u32[]{:S(2)}, u32[]{:S(2)}) collective-permute-start(bf16[256,256]{1,0:T(8,128)(2,1)S(1)} %get-tuple-element.97), channel_id=1, source_target_pairs={{0,4},{4,0},{8,12},{12,8},{16,20},{20,16},{24,28},{28,24},{1,5},{5... | collective-permute-start | bytes 393224 | tf_op jit(solution)/shard_map/ppermute | solution.py:465
  39.7 6.7 %collective-permute-start.14 = (bf16[64,1024]{1,0:T(8,128)(2,1)S(1)}, bf16[64,1024]{1,0:T(8,128)(2,1)S(1)}, u32[]{:S(2)}, u32[]{:S(2)}) collective-permute-start(bf16[64,1024]{1,0:T(8,128)(2,1)S(1)} %get-tuple-element.82), channel_id=1, source_target_pairs={{0,3},{1,2},{2,1},{3,0},{4,7},{5,6},{6,5},{7,4},{8,11},{9,10},{10,... | collective-permute-start | bytes 393224 | tf_op jit(solution)/shard_map/ppermute | solution.py:465
  39.7 16.6 %collective-permute-start.18 = (bf16[256,256]{1,0:T(8,128)(2,1)S(1)}, bf16[256,256]{1,0:T(8,128)(2,1)S(1)}, u32[]{:S(2)}, u32[]{:S(2)}) collective-permute-start(bf16[256,256]{1,0:T(8,128)(2,1)S(1)} %merge.4), channel_id=1, source_target_pairs={{16,0},{20,4},{24,8},{28,12},{17,1},{21,5},{25,9},{29,13},{18,2},{... | collective-permute-start | bytes 393224 | tf_op jit(solution)/shard_map/ppermute | solution.py:461
  41.0 23.8 %collective-permute-start.17 = (bf16[256,256]{1,0:T(8,128)(2,1)S(1)}, bf16[256,256]{1,0:T(8,128)(2,1)S(1)}, u32[]{:S(2)}, u32[]{:S(2)}) collective-permute-start(bf16[256,256]{1,0:T(8,128)(2,1)S(1)} %merge.3), channel_id=1, source_target_pairs={{24,0},{28,4},{25,1},{29,5},{26,2},{30,6},{27,3},{31,7}} | collective-permute-start | bytes 393224 | tf_op jit(solution)/shard_map/ppermute | solution.py:461
  43.3 21.6 %collective-permute-start.16 = (bf16[256,256]{1,0:T(8,128)(2,1)S(1)}, bf16[256,256]{1,0:T(8,128)(2,1)S(1)}, u32[]{:S(2)}, u32[]{:S(2)}) collective-permute-start(bf16[256,256]{1,0:T(8,128)(2,1)S(1)} %get-tuple-element.98), channel_id=1, source_target_pairs={{0,4},{4,0},{8,12},{12,8},{16,20},{20,16},{24,28},{28,24},{1,5},{5... | collective-permute-start | bytes 393224 | tf_op jit(solution)/shard_map/ppermute | solution.py:465
  45.1 19.8 %collective-permute-start.19 = (bf16[256,256]{1,0:T(8,128)(2,1)S(1)}, bf16[256,256]{1,0:T(8,128)(2,1)S(1)}, u32[]{:S(2)}, u32[]{:S(2)}) collective-permute-start(bf16[256,256]{1,0:T(8,128)(2,1)S(1)} %merge.5), channel_id=1, source_target_pairs={{8,0},{12,4},{16,8},{20,12},{24,16},{28,20},{9,1},{13,5},{17,9},{2... | collective-permute-start | bytes 393224 | tf_op jit(solution)/shard_map/ppermute | solution.py:461

commit v2 on v1

--- a/solution.py
+++ b/solution.py
@@ -179,7 +179,8 @@
     for k in range(2, back + 1):
         pair = jnp.maximum(last - k, 0)
         mine, other = 2 * pair + parity, 2 * pair + 1 - parity
-        put(d_blocks, mine, other, d_refs[2 * k - 4], d_refs[2 * k - 3], width, scale)
+        mine_ref, other_ref = (ref.at[k - 2] for ref in d_refs)
+        put(d_blocks, mine, other, mine_ref, other_ref, width, scale)
 
 
 def attend(doc_lengths, prepared, own, near, arrived, far, ranks, whole):
@@ -213,12 +214,11 @@
             row_state,
         ]
         + [
-            jax.ShapeDtypeStruct((2 * width, tok), dtype)
-            for _ in range(back - 1)
+            jax.ShapeDtypeStruct((back - 1, 2 * width, tok), dtype)
             for dtype in (jnp.float32, jnp.bfloat16)
         ],
         in_specs=[smem] + [vmem] * (6 + 2 * back),
-        out_specs=[vmem] * (ranks + 4 + 2 * back),
+        out_specs=[vmem] * (ranks + 8),
         scratch_shapes=[
             pltpu.VMEM((tok, heads * width), jnp.bfloat16),
             pltpu.VMEM((rows, 2 * width), jnp.float32),
@@ -258,7 +258,7 @@
     width,
     scale,
 ):
-    tok = mine1_ref.shape[1]
+    tok = mine0_ref.shape[1]
     parity, last, base, own = here(tok, back, whole)
     cut = 2 * (last - 1)
     d_blocks[...] = jnp.zeros_like(d_blocks)
@@ -279,7 +279,7 @@
         return carry
 
     lax.fori_loop(0, tok // CHUNK, chunk_step, 0)
-    put(d_blocks, parity, 1 - parity, mine1_ref, other1_ref, width, scale)
+    put(d_blocks, parity, 1 - parity, mine1_ref.at[0], other1_ref.at[0], width, scale)
     put(d_blocks, 2 + parity, 3 - parity, mine0_ref, other0_ref, width, scale)
 
 
@@ -295,8 +295,8 @@
         ),
         out_shape=[jax.ShapeDtypeStruct((chunks, rows, width), jnp.float32)]
         + [
-            jax.ShapeDtypeStruct((2 * width, tok), dtype)
-            for _ in range(2)
+            jax.ShapeDtypeStruct(shape, dtype)
+            for shape in ((1, 2 * width, tok), (2 * width, tok))
             for dtype in (jnp.float32, jnp.bfloat16)
         ],
         in_specs=[smem] + [vmem] * 9,
@@ -333,7 +333,9 @@
     )(grad_attended)
 
 
-def arrange_kernel(q_ref, rows_ref, cols_ref, wide):
+def arrange_kernel(doc_ref, q_ref, lengths_ref, rows_ref, cols_ref, wide):
+    for i in range(doc_ref.shape[0]):
+        lengths_ref[i] = doc_ref[i]
     small = unit(q_ref.shape[2])
     wide[...] = q_ref[...].astype(jnp.float32)
     for chunk in range(rows_ref.shape[0]):
@@ -360,22 +362,24 @@
         cols_ref[chunk] = dot_nt(small, rows_ref[chunk]).astype(jnp.bfloat16)
 
 
-def arrange(kernel, arrays, shape, scratch):
+def arrange(kernel, arrays, shape, scratch, lengths=()):
     tok, heads, width = shape
     vmem = pl.BlockSpec(memory_space=pltpu.VMEM)
+    smem = pl.BlockSpec(memory_space=pltpu.SMEM)
     chunks, rows = tok // CHUNK, heads * CHUNK
     return pl.pallas_call(
         kernel,
-        out_shape=[
+        out_shape=[jax.ShapeDtypeStruct(length.shape, length.dtype) for length in lengths]
+        + [
             jax.ShapeDtypeStruct((chunks, rows, width), jnp.bfloat16),
             jax.ShapeDtypeStruct((chunks, width, rows), jnp.bfloat16),
         ],
-        in_specs=[vmem] * len(arrays),
-        out_specs=[vmem, vmem],
+        in_specs=[smem] * len(lengths) + [vmem] * len(arrays),
+        out_specs=[smem] * len(lengths) + [vmem, vmem],
         scratch_shapes=[scratch],
         compiler_params=pltpu.CompilerParams(vmem_limit_bytes=SMALL_VMEM),
         name="arrange",
-    )(*arrays)
+    )(*lengths, *arrays)
 
 
 def join_kernel(*refs):
@@ -410,23 +414,22 @@
     )(*parts, dq_rows)
 
 
-def merge_kernel(*refs):
-    total = refs[0][...]
-    for ref in refs[1:-1]:
-        total = total + ref[...].astype(jnp.float32)
-    refs[-1][...] = total.astype(jnp.bfloat16)
-
-
-def merge(*blocks):
-    vmem = pl.BlockSpec(memory_space=pltpu.VMEM)
+def merge_kernel(mine_ref, other_ref, *block_refs):
+    for k, ref in enumerate(block_refs):
+        ref[...] = (mine_ref[k] + other_ref[k].astype(jnp.float32)).astype(ref.dtype)
+
+
+def merge(mine, other):
+    vmem = pl.BlockSpec(memory_space=pltpu.VMEM)
+    block = jax.ShapeDtypeStruct(mine.shape[1:], jnp.bfloat16)
     return pl.pallas_call(
         merge_kernel,
-        out_shape=jax.ShapeDtypeStruct(blocks[0].shape, jnp.bfloat16),
-        in_specs=[vmem] * len(blocks),
-        out_specs=vmem,
+        out_shape=[block] * mine.shape[0],
+        in_specs=[vmem, vmem],
+        out_specs=[vmem] * mine.shape[0],
         compiler_params=pltpu.CompilerParams(vmem_limit_bytes=SMALL_VMEM),
         name="merge",
-    )(*blocks)
+    )(mine, other)
 
 
 def finish_kernel(own_ref, *refs):
@@ -487,11 +490,15 @@
         arrived = [shifted(own, 2 * k, count) for k in range(1, back + 1)]
     grads = split(grad_attended, ranks)
     grads = [part if k == 0 else exchanged(part, "head", k) for k, part in enumerate(grads)]
-    prepared = arrange(
-        arrange_kernel, [queries], queries.shape, pltpu.VMEM(queries.shape, jnp.float32)
+    doc_lengths, *prepared = arrange(
+        arrange_kernel,
+        [queries],
+        queries.shape,
+        pltpu.VMEM(queries.shape, jnp.float32),
+        [doc_lengths],
     )
     if whole:
-        beside, near = after(beside, near)
+        beside, near, across = after(beside, near, across)
         far_beside = exchanged(beside, "ctx", 1)
         across, grads[1], *prepared = after(across, grads[1], *prepared)
         passed = exchanged(across, "ctx", 2)
@@ -510,26 +517,23 @@
     else:
         far = [exchanged(block, "ctx", 1) for block in arrived]
     outs, state, parts = attend(doc_lengths, prepared, own, near, arrived, far, ranks, whole)
-    outs, far_parts = list(outs), list(parts)
+    outs, (mine_far, other_far) = list(outs), parts
     dq_rows, mine1, other1, mine0, other0 = attend_near(
         doc_lengths, prepared, state, back, whole
     )
-    outs = [part if k == 0 else exchanged(part, "head", k) for k, part in enumerate(outs)]
-    mine = [mine0, mine1] + far_parts[0::2]
-    other = [other0, other1] + [exchanged(part, "ctx", 1) for part in far_parts[1::2]]
-    other[back], *outs[1:2] = after(other[back], *outs[1:2])
-    returned = []
-    for k in range(back, 0, -1):
-        if k == back - 1:
-            other[k], *outs[2:3] = after(other[k], *outs[2:3])
-        block = merge(mine[k], other[k])
-        if k == back:
-            block, other[1] = after(block, other[1])
-            other[1] = exchanged(other[1], "ctx", 1)
-            other[0], other[1] = after(other[0], other[1])
-            other[0] = exchanged(other[0], "ctx", 1)
-        returned.append(shifted(block, -2 * k, count))
-    grad_keys, grad_values = finish(mine[0], [other[0]] + returned)
+    other_far = exchanged(other_far, "ctx", 1)
+    outs[1:2] = [exchanged(part, "head", 1) for part in outs[1:2]]
+    other_far, mine0, *outs[1:2] = after(other_far, mine0, *outs[1:2])
+    blocks = list(merge(mine_far, other_far))
+    other1, blocks[0], *outs[2:] = after(other1, blocks[0], *outs[2:])
+    other1 = exchanged(other1, "ctx", 1)
+    outs[2:] = [exchanged(part, "head", k + 2) for k, part in enumerate(outs[2:])]
+    returned = [shifted(block, -2 * (k + 2), count) for k, block in enumerate(blocks)]
+    other0, returned[0] = after(other0, returned[0])
+    other0 = exchanged(other0, "ctx", 1)
+    (block,) = merge(mine1, other1)
+    returned.append(shifted(block, -2, count))
+    grad_keys, grad_values = finish(mine0, [other0] + returned)
     attended, grad_queries = join(outs, dq_rows, queries.shape)
     grad_keys = grad_keys.reshape(tok, 1, width)
     grad_values = grad_values.reshape(tok, 1, width)

time: 65 us -> 64 us (0.985); the launches traced: 65.8 us -> 63.5 us
  waiting for transfers between devices: 25.4 us -> 23.3 us
  starting transfers between devices: 25.8 us -> 25 us
    ppermute x3, waiting for transfers between devices: 17 us -> 13.2 us  [shifted(): return lax.ppermute(block, 'ctx', pairs)]
    ppermute x17 -> x16, waiting for transfers between devices: 8.4 us -> 10.1 us  [exchanged(): lax.ppermute(block, axis, [(i, i ^ by) for i in range(lax.axis_size(axis))])]
    ppermute x17 -> x16, starting transfers between devices: 21.9 us -> 21.1 us  [exchanged(): lax.ppermute(block, axis, [(i, i ^ by) for i in range(lax.axis_size(axis))])]
    pallas_call x5 -> x4, Pallas kernels: 1.95 us -> 2.54 us  [the longest x2 2.47 us: arrange(): pl.pallas_call(kernel, out_shape=[jax.ShapeDtypeStruct(length.shape, leng...]
  transfers between devices with their start and end apart: 20 -> 19, of which waited for: 7 -> 8; matrix products, arithmetic and copies ran while one was open for 0% -> 0% of each run, Pallas kernels for 9% -> 10%
where the time goes in v2:
time: 64 us; the launch traced here: 63.5 us
  starting transfers between devices  25 us (39%)
  waiting for transfers between devices  23.3 us (36%)
  Pallas kernels  10.8 us (17%)
  local copies, waits for them, and re-layouts  2.74 us (4%)
  other arithmetic  0.88 us (1%)
  between operations  0.76 us (1%)
    ppermute x16, starting transfers between devices, exchanged(): lax.ppermute(block, axis, [(i, i ^ by) for i in range(lax.axis_size(axis))])  21.1 us
    ppermute x3, waiting for transfers between devices, shifted(): return lax.ppermute(block, 'ctx', pairs)  13.2 us
    ppermute x16, waiting for transfers between devices, exchanged(): lax.ppermute(block, axis, [(i, i ^ by) for i in range(lax.axis_size(axis))])  10.1 us
    ppermute x3, starting transfers between devices, shifted(): return lax.ppermute(block, 'ctx', pairs)  3.86 us
    pallas_call x1, Pallas kernels, attend(): pl.pallas_call(functools.partial(attention_kernel, back=back, whole=whole...  3.63 us
    unnamed x6, local copies, waits for them, and re-layouts  2.74 us
    pallas_call x2, Pallas kernels, arrange(): pl.pallas_call(kernel, out_shape=[jax.ShapeDtypeStruct(length.shape, leng...  2.47 us
    pallas_call x1, Pallas kernels, attend_near(): pl.pallas_call(functools.partial(near_kernel, back=back, whole=whole, wid...  2.17 us
  transfers between devices with their start and end apart: 19, of which 8 were waited for; matrix products, arithmetic and copies ran while one was open for 0% of the time, Pallas kernels for 10%

profile of v2, /device:TPU:0, one launch (start us, length us, event | category | flops | bytes accessed | tf_op | source)
XLA Modules:
  0.0 63.5 jit_solution(1912223532875797147)
XLA Ops:
  0.6 0.9 %pad_maximum_fusion.own_ref = bf16[512,128]{1,0:T(8,128)(2,1)S(1)} fusion(bf16[256,128]{1,0:T(8,128)(2,1)} %bitcast.4, bf16[256,128]{1,0:T(8,128)(2,1)} %bitcast.5), kind=kLoop, calls=%fused_computation | loop fusion | flops 262144 | bytes 262144 | tf_op jit(solution)/shard_map/concatenate | solution.py:482
  1.5 4.1 %collective-permute-start.2 = (bf16[512,128]{1,0:T(8,128)(2,1)S(1)}, bf16[512,128]{1,0:T(8,128)(2,1)S(1)}, u32[]{:S(2)}, u32[]{:S(2)}) collective-permute-start(bf16[512,128]{1,0:T(8,128)(2,1)S(1)} %pad_maximum_fusion.own_ref), channel_id=1, source_target_pairs={{0,16},{4,20},{8,24},{12,28},{16,0},{20,4},{24,8},{28,12},{1,17},{... | collective-permute-start | bytes 393224 | tf_op jit(solution)/shard_map/ppermute | solution.py:468
  5.6 1.5 %collective-permute-start.1 = (bf16[512,128]{1,0:T(8,128)(2,1)S(1)}, bf16[512,128]{1,0:T(8,128)(2,1)S(1)}, u32[]{:S(2)}, u32[]{:S(2)}) collective-permute-start(bf16[512,128]{1,0:T(8,128)(2,1)S(1)} %pad_maximum_fusion.own_ref), channel_id=1, source_target_pairs={{0,4},{4,0},{8,12},{12,8},{16,20},{20,16},{24,28},{28,24},{1,5},{5... | collective-permute-start | bytes 393224 | tf_op jit(solution)/shard_map/ppermute | solution.py:468
  7.1 1.6 %collective-permute-start = (bf16[512,128]{1,0:T(8,128)(2,1)S(1)}, bf16[512,128]{1,0:T(8,128)(2,1)S(1)}, u32[]{:S(2)}, u32[]{:S(2)}) collective-permute-start(bf16[512,128]{1,0:T(8,128)(2,1)S(1)} %pad_maximum_fusion.own_ref), channel_id=1, source_target_pairs={{0,8},{4,12},{8,0},{12,4},{16,24},{20,28},{24,16},{28,20},{1,9},{5... | collective-permute-start | bytes 393224 | tf_op jit(solution)/shard_map/ppermute | solution.py:468
  8.7 0.0 copy-start.1
  8.7 1.0 %copy-done.1 = bf16[64,4096]{1,0:T(8,128)(2,1)S(1)} copy-done((bf16[64,4096]{1,0:T(8,128)(2,1)S(1)}, bf16[64,4096]{1,0:T(8,128)(2,1)}, u32[]{:S(2)}) %copy-start.1) | copy-done | bytes 524312
  9.8 0.1 collective-permute-start.3
  9.9 1.6 %collective-permute-start.6 = (bf16[64,1024]{1,0:T(8,128)(2,1)S(1)}, bf16[64,1024]{1,0:T(8,128)(2,1)S(1)}, u32[]{:S(2)}, u32[]{:S(2)}) collective-permute-start(bf16[64,1024]{1,0:T(8,128)(2,1)S(1)} %get-tuple-element.69), channel_id=1, source_target_pairs={{0,2},{1,3},{2,0},{3,1},{4,6},{5,7},{6,4},{7,5},{8,10},{9,11},{10,... | collective-permute-start | bytes 393224 | tf_op jit(solution)/shard_map/ppermute | solution.py:468
  11.4 0.0 copy-start
  11.4 1.0 %copy-done = bf16[256,8,128]{2,1,0:T(8,128)(2,1)S(1)} copy-done((bf16[256,8,128]{2,1,0:T(8,128)(2,1)S(1)}, bf16[256,8,128]{2,1,0:T(8,128)(2,1)}, u32[]{:S(2)}) %copy-start) | copy-done | bytes 524312
  12.5 0.0 copy-start.2
  12.5 0.7 %copy-done.2 = s32[8]{0:T(128)S(1)} copy-done((s32[8]{0:T(128)S(1)}, s32[8]{0:T(128)}, u32[]{:S(2)}) %copy-start.2) | copy-done | bytes 56
  13.1 2.1 %arrange.2 = (s32[8]{0:T(128)S(1)}, bf16[2,1024,128]{2,1,0:T(8,128)(2,1)S(1)}, bf16[2,128,1024]{2,1,0:T(8,128)(2,1)S(1)}) custom-call(s32[8]{0:T(128)S(1)} %copy-done.2, bf16[256,8,128]{2,1,0:T(8,128)(2,1)S(1)} %copy-done), custom_call_target="tpu_custom_call" | custom-call | tf_op jit(solution)/shard_map/arrange/pallas_call | solution.py:370
  15.2 0.0 collective-permute-done.2.refs_1_
  15.2 0.4 collective-permute-start.7
  15.6 0.0 collective-permute-done.1.near_ref
  15.6 0.0 collective-permute-done.refs_0_
  15.6 0.5 collective-permute-start.5
  16.1 0.0 collective-permute-done.3.refs_1_
  16.1 0.5 collective-permute-start.4
  16.6 1.5 %collective-permute-start.8 = (bf16[512,128]{1,0:T(8,128)(2,1)S(1)}, bf16[512,128]{1,0:T(8,128)(2,1)S(1)}, u32[]{:S(2)}, u32[]{:S(2)}) collective-permute-start(bf16[512,128]{1,0:T(8,128)(2,1)S(1)} %collective-permute-done.2.refs_1_), channel_id=1, source_target_pairs={{0,4},{4,0},{8,12},{12,8},{16,20},{20,16},{24,28},{28,24},{1,5},{5... | collective-permute-start | bytes 393224 | tf_op jit(solution)/shard_map/ppermute | solution.py:468
  18.1 0.0 collective-permute-done.6.refs_2_
  18.1 2.7 %collective-permute-done.7.refs_3_ = bf16[64,1024]{1,0:T(8,128)(2,1)S(1)} collective-permute-done((bf16[64,1024]{1,0:T(8,128)(2,1)S(1)}, bf16[64,1024]{1,0:T(8,128)(2,1)S(1)}, u32[]{:S(2)}, u32[]{:S(2)}) %collective-permute-start.7) | collective-permute-done | bytes 131104 | tf_op jit(solution)/shard_map/ppermute | solution.py:468
  20.8 0.4 arrange.3
  21.2 0.7 %collective-permute-done.5.refs_3_ = bf16[512,128]{1,0:T(8,128)(2,1)S(1)} collective-permute-done((bf16[512,128]{1,0:T(8,128)(2,1)S(1)}, bf16[512,128]{1,0:T(8,128)(2,1)S(1)}, u32[]{:S(2)}, u32[]{:S(2)}) %collective-permute-start.5) | collective-permute-done | bytes 131104 | tf_op jit(solution)/shard_map/ppermute | solution.py:468
  21.9 0.0 collective-permute-done.4.refs_2_
  21.9 1.2 %collective-permute-start.9 = (bf16[512,128]{1,0:T(8,128)(2,1)S(1)}, bf16[512,128]{1,0:T(8,128)(2,1)S(1)}, u32[]{:S(2)}, u32[]{:S(2)}) collective-permute-start(bf16[512,128]{1,0:T(8,128)(2,1)S(1)} %collective-permute-done.4.refs_2_), channel_id=1, source_target_pairs={{0,4},{4,0},{8,12},{12,8},{16,20},{20,16},{24,28},{28,24},{1,5},{5... | collective-permute-start | bytes 393224 | tf_op jit(solution)/shard_map/ppermute | solution.py:468
  23.1 1.1 %collective-permute-done.8.refs_4_ = bf16[512,128]{1,0:T(8,128)(2,1)S(1)} collective-permute-done((bf16[512,128]{1,0:T(8,128)(2,1)S(1)}, bf16[512,128]{1,0:T(8,128)(2,1)S(1)}, u32[]{:S(2)}, u32[]{:S(2)}) %collective-permute-start.8) | collective-permute-done | bytes 131104 | tf_op jit(solution)/shard_map/ppermute | solution.py:468
  24.2 2.9 %collective-permute-done.9.refs_5_ = bf16[512,128]{1,0:T(8,128)(2,1)S(1)} collective-permute-done((bf16[512,128]{1,0:T(8,128)(2,1)S(1)}, bf16[512,128]{1,0:T(8,128)(2,1)S(1)}, u32[]{:S(2)}, u32[]{:S(2)}) %collective-permute-start.9) | collective-permute-done | bytes 131104 | tf_op jit(solution)/shard_map/ppermute | solution.py:468
  27.1 3.6 %attention.1 = (bf16[64,1024]{1,0:T(8,128)(2,1)S(1)}, bf16[64,1024]{1,0:T(8,128)(2,1)S(1)}, bf16[64,1024]{1,0:T(8,128)(2,1)S(1)}, bf16[64,1024]{1,0:T(8,128)(2,1...) custom-call(s32[8]{0:T(128)S(1)} %get-tuple-element.58.doc_ref, ...), custom_call_target="tpu_custom_call" | custom-call | flops 7516192768 | bytes 4194304 | tf_op jit(solution)/shard_map/attention/pallas_call | solution.py:197
  30.7 2.3 %collective-permute-start.10 = (bf16[2,256,256]{2,1,0:T(8,128)(2,1)S(1)}, bf16[2,256,256]{2,1,0:T(8,128)(2,1)S(1)}, u32[]{:S(2)}, u32[]{:S(2)}) collective-permute-start(bf16[2,256,256]{2,1,0:T(8,128)(2,1)S(1)} %get-tuple-element.81), channel_id=1, source_target_pairs={{0,4},{4,0},{8,12},{12,8},{16,20},{20,16},{24,28},{28,24},{1,5},{5... | collective-permute-start | bytes 786440 | tf_op jit(solution)/shard_map/ppermute | solution.py:468
  33.0 0.0 collective-permute-start.11
  33.0 2.2 %near.1 = (f32[2,1024,128]{2,1,0:T(8,128)S(1)}, f32[1,256,256]{2,1,0:T(8,128)S(1)}, bf16[1,256,256]{2,1,0:T(8,128)(2,1)S(1)}, f32[256,256]{1,0:T(8,128)S(1)}, bf16[256,256]{1,0:T(8,128)(2,1)S(1)}) custom-call(s32[8]{0:T(128)S(1)} %get-tuple-element.58.doc_ref, bf16[2,128,1024]{2,1,0:T(8,128)(2,1)S(1)} %get-tuple-element.74.q_cols, ...), custom_call_target="tpu_custom_call" | custom-call | flops 2147483648 | bytes 2097152 | tf_op jit(solution)/shard_map/near/pallas_call | solution.py:292
  35.2 0.0 collective-permute-done.11.refs_1_
  35.2 2.7 %collective-permute-done.10.other_ref = bf16[2,256,256]{2,1,0:T(8,128)(2,1)S(1)} collective-permute-done((bf16[2,256,256]{2,1,0:T(8,128)(2,1)S(1)}, bf16[2,256,256]{2,1,0:T(8,128)(2,1)S(1)}, u32[]{:S(2)}, u32[]{:S(2)}) %collective-permute-start.10) | collective-permute-done | bytes 262176 | tf_op jit(solution)/shard_map/ppermute | solution.py:468
  37.9 1.3 %collective-permute-start.14 = (bf16[256,256]{1,0:T(8,128)(2,1)S(1)}, bf16[256,256]{1,0:T(8,128)(2,1)S(1)}, u32[]{:S(2)}, u32[]{:S(2)}) collective-permute-start(bf16[256,256]{1,0:T(8,128)(2,1)S(1)} %get-tuple-element.104), channel_id=1, source_target_pairs={{16,0},{20,4},{24,8},{28,12},{17,1},{21,5},{25,9},{29,13},{18,2},{... | collective-permute-start | bytes 393224 | tf_op jit(solution)/shard_map/ppermute | solution.py:464
  39.2 1.6 %collective-permute-start.17 = (bf16[1,256,256]{2,1,0:T(8,128)(2,1)S(1)}, bf16[1,256,256]{2,1,0:T(8,128)(2,1)S(1)}, u32[]{:S(2)}, u32[]{:S(2)}) collective-permute-start(bf16[1,256,256]{2,1,0:T(8,128)(2,1)S(1)} %get-tuple-element.109), channel_id=1, source_target_pairs={{0,4},{4,0},{8,12},{12,8},{16,20},{20,16},{24,28},{28,24},{1,5},{5... | collective-permute-start | bytes 393224 | tf_op jit(solution)/shard_map/ppermute | solution.py:468
  40.8 1.5 %collective-permute-start.12 = (bf16[64,1024]{1,0:T(8,128)(2,1)S(1)}, bf16[64,1024]{1,0:T(8,128)(2,1)S(1)}, u32[]{:S(2)}, u32[]{:S(2)}) collective-permute-start(bf16[64,1024]{1,0:T(8,128)(2,1)S(1)} %get-tuple-element.97), channel_id=1, source_target_pairs={{0,2},{1,3},{2,0},{3,1},{4,6},{5,7},{6,4},{7,5},{8,10},{9,11},{10,... | collective-permute-start | bytes 393224 | tf_op jit(solution)/shard_map/ppermute | solution.py:468
  42.3 0.0 collective-permute-start.13
  42.3 1.3 %collective-permute-start.16 = (bf16[256,256]{1,0:T(8,128)(2,1)S(1)}, bf16[256,256]{1,0:T(8,128)(2,1)S(1)}, u32[]{:S(2)}, u32[]{:S(2)}) collective-permute-start(bf16[256,256]{1,0:T(8,128)(2,1)S(1)} %get-tuple-element.107), channel_id=1, source_target_pairs={{24,0},{28,4},{25,1},{29,5},{26,2},{30,6},{27,3},{31,7}} | collective-permute-start | bytes 393224 | tf_op jit(solution)/shard_map/ppermute | solution.py:464
  43.6 8.0 %collective-permute-done.14.refs_1_ = bf16[256,256]{1,0:T(8,128)(2,1)S(1)} collective-permute-done((bf16[256,256]{1,0:T(8,128)(2,1)S(1)}, bf16[256,256]{1,0:T(8,128)(2,1)S(1)}, u32[]{:S(2)}, u32[]{:S(2)}) %collective-permute-start.14) | collective-permute-done | bytes 131104 | tf_op jit(solution)/shard_map/ppermute | solution.py:464
  51.6 2.9 %collective-permute-start.15 = (bf16[256,256]{1,0:T(8,128)(2,1)S(1)}, bf16[256,256]{1,0:T(8,128)(2,1)S(1)}, u32[]{:S(2)}, u32[]{:S(2)}) collective-permute-start(bf16[256,256]{1,0:T(8,128)(2,1)S(1)} %get-tuple-element.105), channel_id=1, source_target_pairs={{0,4},{4,0},{8,12},{12,8},{16,20},{20,16},{24,28},{28,24},{1,5},{5... | collective-permute-start | bytes 393224 | tf_op jit(solution)/shard_map/ppermute | solution.py:468
  54.5 0.0 collective-permute-done.17.other_ref
  54.5 1.3 %collective-permute-start.18 = (bf16[256,256]{1,0:T(8,128)(2,1)S(1)}, bf16[256,256]{1,0:T(8,128)(2,1)S(1)}, u32[]{:S(2)}, u32[]{:S(2)}) collective-permute-start(bf16[256,256]{1,0:T(8,128)(2,1)S(1)} %merge.3), channel_id=1, source_target_pairs={{8,0},{12,4},{16,8},{20,12},{24,16},{28,20},{9,1},{13,5},{17,9},{2... | collective-permute-start | bytes 393224 | tf_op jit(solution)/shard_map/ppermute | solution.py:464
  55.8 0.0 collective-permute-done.12.refs_2_
  55.8 0.0 collective-permute-done.13.refs_3_
  55.8 1.5 %join.1 = (bf16[64,4096]{1,0:T(8,128)(2,1)}, bf16[256,8,128]{2,1,0:T(8,128)(2,1)}) custom-call(bf16[64,1024]{1,0:T(8,128)(2,1)S(1)} %get-tuple-element.80.refs_0_, bf16[64,1024]{1,0:T(8,128)(2,1)S(1)} %collective-permute-done.11.refs_1_, bf16[64,1024]{1,0:T(8,128)(2,1)S(1)} %collective-permute-done.12.refs_2_, ...), custom_call_target="tpu_custom_call" | custom-call | tf_op jit(solution)/shard_map/join/pallas_call | solution.py:403
  57.3 1.5 %collective-permute-done.16.refs_2_ = bf16[256,256]{1,0:T(8,128)(2,1)S(1)} collective-permute-done((bf16[256,256]{1,0:T(8,128)(2,1)S(1)}, bf16[256,256]{1,0:T(8,128)(2,1)S(1)}, u32[]{:S(2)}, u32[]{:S(2)}) %collective-permute-start.16) | collective-permute-done | bytes 131104 | tf_op jit(solution)/shard_map/ppermute | solution.py:464
  58.8 0.0 collective-permute-done.15.refs_0_
  58.8 3.7 %collective-permute-done.18.refs_3_ = bf16[256,256]{1,0:T(8,128)(2,1)S(1)} collective-permute-done((bf16[256,256]{1,0:T(8,128)(2,1)S(1)}, bf16[256,256]{1,0:T(8,128)(2,1)S(1)}, u32[]{:S(2)}, u32[]{:S(2)}) %collective-permute-start.18) | collective-permute-done | bytes 131104 | tf_op jit(solution)/shard_map/ppermute | solution.py:464
  62.5 0.9 %finish.1 = (bf16[256,128]{1,0:T(8,128)(2,1)}, bf16[256,128]{1,0:T(8,128)(2,1)}) custom-call(f32[256,256]{1,0:T(8,128)S(1)} %get-tuple-element.102.own_ref, bf16[256,256]{1,0:T(8,128)(2,1)S(1)} %collective-permute-done.15.refs_0_, bf16[256,256]{1,0:T(8,128)(2,1)S(1)} %collective-permute-done.14.refs_1_, ...), custom_call_target="tpu_custom_call" | custom-call | tf_op jit(solution)/shard_map/finish/pallas_call | solution.py:452
  (3 shorter events, 0.1 us)
Async XLA Ops:
  1.5 13.7 %collective-permute-start.2 = (bf16[512,128]{1,0:T(8,128)(2,1)S(1)}, bf16[512,128]{1,0:T(8,128)(2,1)S(1)}, u32[]{:S(2)}, u32[]{:S(2)}) collective-permute-start(bf16[512,128]{1,0:T(8,128)(2,1)S(1)} %pad_maximum_fusion.own_ref), channel_id=1, source_target_pairs={{0,16},{4,20},{8,24},{12,28},{16,0},{20,4},{24,8},{28,12},{1,17},{... | collective-permute-start | bytes 393224 | tf_op jit(solution)/shard_map/ppermute | solution.py:468
  5.6 10.0 %collective-permute-start.1 = (bf16[512,128]{1,0:T(8,128)(2,1)S(1)}, bf16[512,128]{1,0:T(8,128)(2,1)S(1)}, u32[]{:S(2)}, u32[]{:S(2)}) collective-permute-start(bf16[512,128]{1,0:T(8,128)(2,1)S(1)} %pad_maximum_fusion.own_ref), channel_id=1, source_target_pairs={{0,4},{4,0},{8,12},{12,8},{16,20},{20,16},{24,28},{28,24},{1,5},{5... | collective-permute-start | bytes 393224 | tf_op jit(solution)/shard_map/ppermute | solution.py:468
  7.1 8.5 %collective-permute-start = (bf16[512,128]{1,0:T(8,128)(2,1)S(1)}, bf16[512,128]{1,0:T(8,128)(2,1)S(1)}, u32[]{:S(2)}, u32[]{:S(2)}) collective-permute-start(bf16[512,128]{1,0:T(8,128)(2,1)S(1)} %pad_maximum_fusion.own_ref), channel_id=1, source_target_pairs={{0,8},{4,12},{8,0},{12,4},{16,24},{20,28},{24,16},{28,20},{1,9},{5... | collective-permute-start | bytes 393224 | tf_op jit(solution)/shard_map/ppermute | solution.py:468
  8.7 1.0 %copy-start.1 = (bf16[64,4096]{1,0:T(8,128)(2,1)S(1)}, bf16[64,4096]{1,0:T(8,128)(2,1)}, u32[]{:S(2)}) copy-start(bf16[64,4096]{1,0:T(8,128)(2,1)} %grad_ref.1) | copy-start | bytes 1572868
  9.8 6.3 %collective-permute-start.3 = (bf16[64,1024]{1,0:T(8,128)(2,1)S(1)}, bf16[64,1024]{1,0:T(8,128)(2,1)S(1)}, u32[]{:S(2)}, u32[]{:S(2)}) collective-permute-start(bf16[64,1024]{1,0:T(8,128)(2,1)S(1)} %get-tuple-element.60), channel_id=1, source_target_pairs={{0,1},{1,0},{2,3},{3,2},{4,5},{5,4},{6,7},{7,6},{8,9},{9,8},{10,11... | collective-permute-start | bytes 393224 | tf_op jit(solution)/shard_map/ppermute | solution.py:468
  9.9 8.2 %collective-permute-start.6 = (bf16[64,1024]{1,0:T(8,128)(2,1)S(1)}, bf16[64,1024]{1,0:T(8,128)(2,1)S(1)}, u32[]{:S(2)}, u32[]{:S(2)}) collective-permute-start(bf16[64,1024]{1,0:T(8,128)(2,1)S(1)} %get-tuple-element.69), channel_id=1, source_target_pairs={{0,2},{1,3},{2,0},{3,1},{4,6},{5,7},{6,4},{7,5},{8,10},{9,11},{10,... | collective-permute-start | bytes 393224 | tf_op jit(solution)/shard_map/ppermute | solution.py:468
  11.4 1.0 %copy-start = (bf16[256,8,128]{2,1,0:T(8,128)(2,1)S(1)}, bf16[256,8,128]{2,1,0:T(8,128)(2,1)}, u32[]{:S(2)}) copy-start(bf16[256,8,128]{2,1,0:T(8,128)(2,1)} %q_ref.1) | copy-start | bytes 1572868
  12.5 0.7 %copy-start.2 = (s32[8]{0:T(128)S(1)}, s32[8]{0:T(128)}, u32[]{:S(2)}) copy-start(s32[8]{0:T(128)} %doc_ref.1) | copy-start | bytes 100
  15.2 5.6 %collective-permute-start.7 = (bf16[64,1024]{1,0:T(8,128)(2,1)S(1)}, bf16[64,1024]{1,0:T(8,128)(2,1)S(1)}, u32[]{:S(2)}, u32[]{:S(2)}) collective-permute-start(bf16[64,1024]{1,0:T(8,128)(2,1)S(1)} %get-tuple-element.70), channel_id=1, source_target_pairs={{0,3},{1,2},{2,1},{3,0},{4,7},{5,6},{6,5},{7,4},{8,11},{9,10},{10,... | collective-permute-start | bytes 393224 | tf_op jit(solution)/shard_map/ppermute | solution.py:468
  15.6 6.3 %collective-permute-start.5 = (bf16[512,128]{1,0:T(8,128)(2,1)S(1)}, bf16[512,128]{1,0:T(8,128)(2,1)S(1)}, u32[]{:S(2)}, u32[]{:S(2)}) collective-permute-start(bf16[512,128]{1,0:T(8,128)(2,1)S(1)} %collective-permute-done.refs_0_), channel_id=1, source_target_pairs={{0,4},{4,0},{8,12},{12,8},{16,20},{20,16},{24,28},{28,24},{1,5},{5... | collective-permute-start | bytes 393224 | tf_op jit(solution)/shard_map/ppermute | solution.py:468
  16.1 5.8 %collective-permute-start.4 = (bf16[512,128]{1,0:T(8,128)(2,1)S(1)}, bf16[512,128]{1,0:T(8,128)(2,1)S(1)}, u32[]{:S(2)}, u32[]{:S(2)}) collective-permute-start(bf16[512,128]{1,0:T(8,128)(2,1)S(1)} %collective-permute-done.2.refs_1_), channel_id=1, source_target_pairs={{0,8},{4,12},{8,0},{12,4},{16,24},{20,28},{24,16},{28,20},{1,9},{5... | collective-permute-start | bytes 393224 | tf_op jit(solution)/shard_map/ppermute | solution.py:468
  16.6 7.6 %collective-permute-start.8 = (bf16[512,128]{1,0:T(8,128)(2,1)S(1)}, bf16[512,128]{1,0:T(8,128)(2,1)S(1)}, u32[]{:S(2)}, u32[]{:S(2)}) collective-permute-start(bf16[512,128]{1,0:T(8,128)(2,1)S(1)} %collective-permute-done.2.refs_1_), channel_id=1, source_target_pairs={{0,4},{4,0},{8,12},{12,8},{16,20},{20,16},{24,28},{28,24},{1,5},{5... | collective-permute-start | bytes 393224 | tf_op jit(solution)/shard_map/ppermute | solution.py:468
  21.9 5.2 %collective-permute-start.9 = (bf16[512,128]{1,0:T(8,128)(2,1)S(1)}, bf16[512,128]{1,0:T(8,128)(2,1)S(1)}, u32[]{:S(2)}, u32[]{:S(2)}) collective-permute-start(bf16[512,128]{1,0:T(8,128)(2,1)S(1)} %collective-permute-done.4.refs_2_), channel_id=1, source_target_pairs={{0,4},{4,0},{8,12},{12,8},{16,20},{20,16},{24,28},{28,24},{1,5},{5... | collective-permute-start | bytes 393224 | tf_op jit(solution)/shard_map/ppermute | solution.py:468
  30.7 7.2 %collective-permute-start.10 = (bf16[2,256,256]{2,1,0:T(8,128)(2,1)S(1)}, bf16[2,256,256]{2,1,0:T(8,128)(2,1)S(1)}, u32[]{:S(2)}, u32[]{:S(2)}) collective-permute-start(bf16[2,256,256]{2,1,0:T(8,128)(2,1)S(1)} %get-tuple-element.81), channel_id=1, source_target_pairs={{0,4},{4,0},{8,12},{12,8},{16,20},{20,16},{24,28},{28,24},{1,5},{5... | collective-permute-start | bytes 786440 | tf_op jit(solution)/shard_map/ppermute | solution.py:468
  33.0 2.2 %collective-permute-start.11 = (bf16[64,1024]{1,0:T(8,128)(2,1)S(1)}, bf16[64,1024]{1,0:T(8,128)(2,1)S(1)}, u32[]{:S(2)}, u32[]{:S(2)}) collective-permute-start(bf16[64,1024]{1,0:T(8,128)(2,1)S(1)} %get-tuple-element.89), channel_id=1, source_target_pairs={{0,1},{1,0},{2,3},{3,2},{4,5},{5,4},{6,7},{7,6},{8,9},{9,8},{10,11... | collective-permute-start | bytes 393224 | tf_op jit(solution)/shard_map/ppermute | solution.py:468
  37.9 13.7 %collective-permute-start.14 = (bf16[256,256]{1,0:T(8,128)(2,1)S(1)}, bf16[256,256]{1,0:T(8,128)(2,1)S(1)}, u32[]{:S(2)}, u32[]{:S(2)}) collective-permute-start(bf16[256,256]{1,0:T(8,128)(2,1)S(1)} %get-tuple-element.104), channel_id=1, source_target_pairs={{16,0},{20,4},{24,8},{28,12},{17,1},{21,5},{25,9},{29,13},{18,2},{... | collective-permute-start | bytes 393224 | tf_op jit(solution)/shard_map/ppermute | solution.py:464
  39.2 15.3 %collective-permute-start.17 = (bf16[1,256,256]{2,1,0:T(8,128)(2,1)S(1)}, bf16[1,256,256]{2,1,0:T(8,128)(2,1)S(1)}, u32[]{:S(2)}, u32[]{:S(2)}) collective-permute-start(bf16[1,256,256]{2,1,0:T(8,128)(2,1)S(1)} %get-tuple-element.109), channel_id=1, source_target_pairs={{0,4},{4,0},{8,12},{12,8},{16,20},{20,16},{24,28},{28,24},{1,5},{5... | collective-permute-start | bytes 393224 | tf_op jit(solution)/shard_map/ppermute | solution.py:468
  40.8 15.0 %collective-permute-start.12 = (bf16[64,1024]{1,0:T(8,128)(2,1)S(1)}, bf16[64,1024]{1,0:T(8,128)(2,1)S(1)}, u32[]{:S(2)}, u32[]{:S(2)}) collective-permute-start(bf16[64,1024]{1,0:T(8,128)(2,1)S(1)} %get-tuple-element.97), channel_id=1, source_target_pairs={{0,2},{1,3},{2,0},{3,1},{4,6},{5,7},{6,4},{7,5},{8,10},{9,11},{10,... | collective-permute-start | bytes 393224 | tf_op jit(solution)/shard_map/ppermute | solution.py:468
  42.3 13.5 %collective-permute-start.13 = (bf16[64,1024]{1,0:T(8,128)(2,1)S(1)}, bf16[64,1024]{1,0:T(8,128)(2,1)S(1)}, u32[]{:S(2)}, u32[]{:S(2)}) collective-permute-start(bf16[64,1024]{1,0:T(8,128)(2,1)S(1)} %get-tuple-element.98), channel_id=1, source_target_pairs={{0,3},{1,2},{2,1},{3,0},{4,7},{5,6},{6,5},{7,4},{8,11},{9,10},{10,... | collective-permute-start | bytes 393224 | tf_op jit(solution)/shard_map/ppermute | solution.py:468
  42.3 16.5 %collective-permute-start.16 = (bf16[256,256]{1,0:T(8,128)(2,1)S(1)}, bf16[256,256]{1,0:T(8,128)(2,1)S(1)}, u32[]{:S(2)}, u32[]{:S(2)}) collective-permute-start(bf16[256,256]{1,0:T(8,128)(2,1)S(1)} %get-tuple-element.107), channel_id=1, source_target_pairs={{24,0},{28,4},{25,1},{29,5},{26,2},{30,6},{27,3},{31,7}} | collective-permute-start | bytes 393224 | tf_op jit(solution)/shard_map/ppermute | solution.py:464
  51.6 7.2 %collective-permute-start.15 = (bf16[256,256]{1,0:T(8,128)(2,1)S(1)}, bf16[256,256]{1,0:T(8,128)(2,1)S(1)}, u32[]{:S(2)}, u32[]{:S(2)}) collective-permute-start(bf16[256,256]{1,0:T(8,128)(2,1)S(1)} %get-tuple-element.105), channel_id=1, source_target_pairs={{0,4},{4,0},{8,12},{12,8},{16,20},{20,16},{24,28},{28,24},{1,5},{5... | collective-permute-start | bytes 393224 | tf_op jit(solution)/shard_map/ppermute | solution.py:468
  54.5 8.0 %collective-permute-start.18 = (bf16[256,256]{1,0:T(8,128)(2,1)S(1)}, bf16[256,256]{1,0:T(8,128)(2,1)S(1)}, u32[]{:S(2)}, u32[]{:S(2)}) collective-permute-start(bf16[256,256]{1,0:T(8,128)(2,1)S(1)} %merge.3), channel_id=1, source_target_pairs={{8,0},{12,4},{16,8},{20,12},{24,16},{28,20},{9,1},{13,5},{17,9},{2... | collective-permute-start | bytes 393224 | tf_op jit(solution)/shard_map/ppermute | solution.py:464

commit v3 on v2

--- a/solution.py
+++ b/solution.py
@@ -312,30 +312,31 @@
     )(doc_lengths, q_cols, do_rows, do_cols, *state)
 
 
-def split_kernel(grad_ref, *part_refs):
+def split_kernel(doc_ref, grad_ref, lengths_ref, *part_refs):
+    for i in range(doc_ref.shape[0]):
+        lengths_ref[i] = doc_ref[i]
     size = part_refs[0].shape[1]
     for k, ref in enumerate(part_refs):
         at = pl.multiple_of((lax.axis_index("head") ^ k) * size, size)
         ref[...] = grad_ref[:, pl.ds(at, size)]
 
 
-def split(grad_attended, ranks):
+def split(doc_lengths, grad_attended, ranks):
     rows, columns = grad_attended.shape
     vmem = pl.BlockSpec(memory_space=pltpu.VMEM)
+    smem = pl.BlockSpec(memory_space=pltpu.SMEM)
     part = jax.ShapeDtypeStruct((rows, columns // ranks), grad_attended.dtype)
     return pl.pallas_call(
         split_kernel,
-        out_shape=[part] * ranks,
-        in_specs=[vmem],
-        out_specs=[vmem] * ranks,
+        out_shape=[jax.ShapeDtypeStruct(doc_lengths.shape, doc_lengths.dtype)] + [part] * ranks,
+        in_specs=[smem, vmem],
+        out_specs=[smem] + [vmem] * ranks,
         compiler_params=pltpu.CompilerParams(vmem_limit_bytes=SMALL_VMEM),
         name="split",
-    )(grad_attended)
-
-
-def arrange_kernel(doc_ref, q_ref, lengths_ref, rows_ref, cols_ref, wide):
-    for i in range(doc_ref.shape[0]):
-        lengths_ref[i] = doc_ref[i]
+    )(doc_lengths, grad_attended)
+
+
+def arrange_kernel(q_ref, rows_ref, cols_ref, wide):
     small = unit(q_ref.shape[2])
     wide[...] = q_ref[...].astype(jnp.float32)
     for chunk in range(rows_ref.shape[0]):
@@ -362,24 +363,22 @@
         cols_ref[chunk] = dot_nt(small, rows_ref[chunk]).astype(jnp.bfloat16)
 
 
-def arrange(kernel, arrays, shape, scratch, lengths=()):
+def arrange(kernel, arrays, shape, scratch):
     tok, heads, width = shape
     vmem = pl.BlockSpec(memory_space=pltpu.VMEM)
-    smem = pl.BlockSpec(memory_space=pltpu.SMEM)
     chunks, rows = tok // CHUNK, heads * CHUNK
     return pl.pallas_call(
         kernel,
-        out_shape=[jax.ShapeDtypeStruct(length.shape, length.dtype) for length in lengths]
-        + [
+        out_shape=[
             jax.ShapeDtypeStruct((chunks, rows, width), jnp.bfloat16),
             jax.ShapeDtypeStruct((chunks, width, rows), jnp.bfloat16),
         ],
-        in_specs=[smem] * len(lengths) + [vmem] * len(arrays),
-        out_specs=[smem] * len(lengths) + [vmem, vmem],
+        in_specs=[vmem] * len(arrays),
+        out_specs=[vmem, vmem],
         scratch_shapes=[scratch],
         compiler_params=pltpu.CompilerParams(vmem_limit_bytes=SMALL_VMEM),
         name="arrange",
-    )(*lengths, *arrays)
+    )(*arrays)
 
 
 def join_kernel(*refs):
@@ -488,34 +487,28 @@
         across = exchanged(own, "ctx", 4)
     else:
         arrived = [shifted(own, 2 * k, count) for k in range(1, back + 1)]
-    grads = split(grad_attended, ranks)
+    doc_lengths, *grads = split(doc_lengths, grad_attended, ranks)
     grads = [part if k == 0 else exchanged(part, "head", k) for k, part in enumerate(grads)]
-    doc_lengths, *prepared = arrange(
-        arrange_kernel,
-        [queries],
-        queries.shape,
-        pltpu.VMEM(queries.shape, jnp.float32),
-        [doc_lengths],
-    )
     if whole:
-        beside, near, across = after(beside, near, across)
         far_beside = exchanged(beside, "ctx", 1)
-        across, grads[1], *prepared = after(across, grads[1], *prepared)
+        across, *grads[1:3] = after(across, *grads[1:3])
         passed = exchanged(across, "ctx", 2)
         far_across = exchanged(across, "ctx", 1)
-    prepared = [*prepared, *arrange(
-        arrange_grads_kernel,
-        grads,
-        queries.shape,
-        pltpu.VMEM((tok, heads * width), jnp.bfloat16),
-    )]
-    if whole:
-        passed, far_beside, *prepared = after(passed, far_beside, *prepared)
+        passed, far_beside, near, grads[3] = after(passed, far_beside, near, grads[3])
         far_passed = exchanged(passed, "ctx", 1)
         arrived = [beside, across, passed]
         far = [far_beside, far_across, far_passed]
     else:
         far = [exchanged(block, "ctx", 1) for block in arrived]
+    prepared = arrange(
+        arrange_kernel, [queries], queries.shape, pltpu.VMEM(queries.shape, jnp.float32)
+    )
+    prepared += arrange(
+        arrange_grads_kernel,
+        grads,
+        queries.shape,
+        pltpu.VMEM((tok, heads * width), jnp.bfloat16),
+    )
     outs, state, parts = attend(doc_lengths, prepared, own, near, arrived, far, ranks, whole)
     outs, (mine_far, other_far) = list(outs), parts
     dq_rows, mine1, other1, mine0, other0 = attend_near(

time: 64 us -> 65.7 us (1.027)
  waiting for transfers between devices: 23.3 us -> 24.9 us
    ppermute x3, waiting for transfers between devices: 13.2 us -> 16.8 us  [shifted(): return lax.ppermute(block, 'ctx', pairs)]
    ppermute x16, waiting for transfers between devices: 10.1 us -> 8.14 us  [exchanged(): lax.ppermute(block, axis, [(i, i ^ by) for i in range(lax.axis_size(axis))])]
  transfers between devices with their start and end apart: 19 -> 19, of which waited for: 8 -> 9; matrix products, arithmetic and copies ran while one was open for 0% -> 0% of each run, Pallas kernels for 10% -> 10%
where the time goes in v3:
time: 65.7 us; the launch traced here: 65.4 us
  waiting for transfers between devices  24.9 us (38%)
  starting transfers between devices  24.7 us (38%)
  Pallas kernels  11.3 us (17%)
  local copies, waits for them, and re-layouts  2.74 us (4%)
  other arithmetic  0.88 us (1%)
  between operations  0.76 us (1%)
    ppermute x16, starting transfers between devices, exchanged(): lax.ppermute(block, axis, [(i, i ^ by) for i in range(lax.axis_size(axis))])  20.9 us
    ppermute x3, waiting for transfers between devices, shifted(): return lax.ppermute(block, 'ctx', pairs)  16.8 us
    ppermute x16, waiting for transfers between devices, exchanged(): lax.ppermute(block, axis, [(i, i ^ by) for i in range(lax.axis_size(axis))])  8.14 us
    ppermute x3, starting transfers between devices, shifted(): return lax.ppermute(block, 'ctx', pairs)  3.86 us
    pallas_call x1, Pallas kernels, attend(): pl.pallas_call(functools.partial(attention_kernel, back=back, whole=whole...  3.63 us
    unnamed x6, local copies, waits for them, and re-layouts  2.74 us
    pallas_call x1, Pallas kernels, attend_near(): pl.pallas_call(functools.partial(near_kernel, back=back, whole=whole, wid...  2.17 us
    pallas_call x2, Pallas kernels, arrange(): pl.pallas_call(kernel, out_shape=[jax.ShapeDtypeStruct((chunks, rows, wid...  1.88 us
  transfers between devices with their start and end apart: 19, of which 9 were waited for; matrix products, arithmetic and copies ran while one was open for 0% of the time, Pallas kernels for 10%

profile of v3, /device:TPU:0, one launch (start us, length us, event | category | flops | bytes accessed | tf_op | source)
XLA Modules:
  0.0 65.4 jit_solution(16032532878921851856)
XLA Ops:
  0.6 0.9 %pad_maximum_fusion.own_ref = bf16[512,128]{1,0:T(8,128)(2,1)S(1)} fusion(bf16[256,128]{1,0:T(8,128)(2,1)} %bitcast.4, bf16[256,128]{1,0:T(8,128)(2,1)} %bitcast.5), kind=kLoop, calls=%fused_computation | loop fusion | flops 262144 | bytes 262144 | tf_op jit(solution)/shard_map/concatenate | solution.py:481
  1.5 4.1 %collective-permute-start = (bf16[512,128]{1,0:T(8,128)(2,1)S(1)}, bf16[512,128]{1,0:T(8,128)(2,1)S(1)}, u32[]{:S(2)}, u32[]{:S(2)}) collective-permute-start(bf16[512,128]{1,0:T(8,128)(2,1)S(1)} %pad_maximum_fusion.own_ref), channel_id=1, source_target_pairs={{0,16},{4,20},{8,24},{12,28},{16,0},{20,4},{24,8},{28,12},{1,17},{... | collective-permute-start | bytes 393224 | tf_op jit(solution)/shard_map/ppermute | solution.py:467
  5.6 0.0 copy-start
  5.6 1.0 %copy-done = bf16[64,4096]{1,0:T(8,128)(2,1)S(1)} copy-done((bf16[64,4096]{1,0:T(8,128)(2,1)S(1)}, bf16[64,4096]{1,0:T(8,128)(2,1)}, u32[]{:S(2)}) %copy-start) | copy-done | bytes 524312
  6.7 0.0 copy-start.2
  6.7 0.7 copy-done.2
  7.3 1.1 %split.1 = (s32[8]{0:T(128)S(1)}, bf16[64,1024]{1,0:T(8,128)(2,1)S(1)}, bf16[64,1024]{1,0:T(8,128)(2,1)S(1)}, bf16[64,1024]{1,0:T(8,128)(2,1)S(1)}, bf16[64,1024]{1,0:T(8,128)(2,1)S(1)}) custom-call(s32[8]{0:T(128)S(1)} %copy-done.2, bf16[64,4096]{1,0:T(8,128)(2,1)S(1)} %copy-done), custom_call_target="tpu_custom_call" | custom-call | tf_op jit(solution)/shard_map/split/pallas_call | solution.py:329
  8.5 0.1 collective-permute-start.1
  8.5 1.6 %collective-permute-start.2 = (bf16[64,1024]{1,0:T(8,128)(2,1)S(1)}, bf16[64,1024]{1,0:T(8,128)(2,1)S(1)}, u32[]{:S(2)}, u32[]{:S(2)}) collective-permute-start(bf16[64,1024]{1,0:T(8,128)(2,1)S(1)} %get-tuple-element.57), channel_id=1, source_target_pairs={{0,2},{1,3},{2,0},{3,1},{4,6},{5,7},{6,4},{7,5},{8,10},{9,11},{10,... | collective-permute-start | bytes 393224 | tf_op jit(solution)/shard_map/ppermute | solution.py:467
  10.1 1.6 %collective-permute-start.4 = (bf16[512,128]{1,0:T(8,128)(2,1)S(1)}, bf16[512,128]{1,0:T(8,128)(2,1)S(1)}, u32[]{:S(2)}, u32[]{:S(2)}) collective-permute-start(bf16[512,128]{1,0:T(8,128)(2,1)S(1)} %pad_maximum_fusion.own_ref), channel_id=1, source_target_pairs={{0,8},{4,12},{8,0},{12,4},{16,24},{20,28},{24,16},{28,20},{1,9},{5... | collective-permute-start | bytes 393224 | tf_op jit(solution)/shard_map/ppermute | solution.py:467
  11.7 1.5 %collective-permute-start.6 = (bf16[512,128]{1,0:T(8,128)(2,1)S(1)}, bf16[512,128]{1,0:T(8,128)(2,1)S(1)}, u32[]{:S(2)}, u32[]{:S(2)}) collective-permute-start(bf16[512,128]{1,0:T(8,128)(2,1)S(1)} %pad_maximum_fusion.own_ref), channel_id=1, source_target_pairs={{0,4},{4,0},{8,12},{12,8},{16,20},{20,16},{24,28},{28,24},{1,5},{5... | collective-permute-start | bytes 393224 | tf_op jit(solution)/shard_map/ppermute | solution.py:467
  13.2 0.0 collective-permute-done.refs_1_
  13.2 0.0 collective-permute-start.7
  13.2 0.0 collective-permute-done.1.refs_1_
  13.2 1.2 %collective-permute-done.2.refs_2_ = bf16[64,1024]{1,0:T(8,128)(2,1)S(1)} collective-permute-done((bf16[64,1024]{1,0:T(8,128)(2,1)S(1)}, bf16[64,1024]{1,0:T(8,128)(2,1)S(1)}, u32[]{:S(2)}, u32[]{:S(2)}) %collective-permute-start.2) | collective-permute-done | bytes 131104 | tf_op jit(solution)/shard_map/ppermute | solution.py:467
  14.5 1.2 %collective-permute-done.4.refs_0_ = bf16[512,128]{1,0:T(8,128)(2,1)S(1)} collective-permute-done((bf16[512,128]{1,0:T(8,128)(2,1)S(1)}, bf16[512,128]{1,0:T(8,128)(2,1)S(1)}, u32[]{:S(2)}, u32[]{:S(2)}) %collective-permute-start.4) | collective-permute-done | bytes 131104 | tf_op jit(solution)/shard_map/ppermute | solution.py:467
  15.7 1.5 %collective-permute-start.5 = (bf16[512,128]{1,0:T(8,128)(2,1)S(1)}, bf16[512,128]{1,0:T(8,128)(2,1)S(1)}, u32[]{:S(2)}, u32[]{:S(2)}) collective-permute-start(bf16[512,128]{1,0:T(8,128)(2,1)S(1)} %collective-permute-done.4.refs_0_), channel_id=1, source_target_pairs={{0,4},{4,0},{8,12},{12,8},{16,20},{20,16},{24,28},{28,24},{1,5},{5... | collective-permute-start | bytes 393224 | tf_op jit(solution)/shard_map/ppermute | solution.py:467
  17.2 1.6 %collective-permute-start.3 = (bf16[512,128]{1,0:T(8,128)(2,1)S(1)}, bf16[512,128]{1,0:T(8,128)(2,1)S(1)}, u32[]{:S(2)}, u32[]{:S(2)}) collective-permute-start(bf16[512,128]{1,0:T(8,128)(2,1)S(1)} %collective-permute-done.refs_1_), channel_id=1, source_target_pairs={{0,8},{4,12},{8,0},{12,4},{16,24},{20,28},{24,16},{28,20},{1,9},{5... | collective-permute-start | bytes 393224 | tf_op jit(solution)/shard_map/ppermute | solution.py:467
  18.8 0.5 collective-permute-start.8
  19.3 0.0 collective-permute-done.6.near_ref
  19.3 0.0 collective-permute-done.7.refs_3_
  19.3 1.9 %collective-permute-done.5.refs_3_ = bf16[512,128]{1,0:T(8,128)(2,1)S(1)} collective-permute-done((bf16[512,128]{1,0:T(8,128)(2,1)S(1)}, bf16[512,128]{1,0:T(8,128)(2,1)S(1)}, u32[]{:S(2)}, u32[]{:S(2)}) %collective-permute-start.5) | collective-permute-done | bytes 131104 | tf_op jit(solution)/shard_map/ppermute | solution.py:467
  21.2 1.0 %collective-permute-done.3.refs_2_ = bf16[512,128]{1,0:T(8,128)(2,1)S(1)} collective-permute-done((bf16[512,128]{1,0:T(8,128)(2,1)S(1)}, bf16[512,128]{1,0:T(8,128)(2,1)S(1)}, u32[]{:S(2)}, u32[]{:S(2)}) %collective-permute-start.3) | collective-permute-done | bytes 131104 | tf_op jit(solution)/shard_map/ppermute | solution.py:467
  22.2 1.4 %collective-permute-start.9 = (bf16[512,128]{1,0:T(8,128)(2,1)S(1)}, bf16[512,128]{1,0:T(8,128)(2,1)S(1)}, u32[]{:S(2)}, u32[]{:S(2)}) collective-permute-start(bf16[512,128]{1,0:T(8,128)(2,1)S(1)} %collective-permute-done.3.refs_2_), channel_id=1, source_target_pairs={{0,4},{4,0},{8,12},{12,8},{16,20},{20,16},{24,28},{28,24},{1,5},{5... | collective-permute-start | bytes 393224 | tf_op jit(solution)/shard_map/ppermute | solution.py:467
  23.6 0.0 copy-start.1
  23.6 1.0 %copy-done.1 = bf16[256,8,128]{2,1,0:T(8,128)(2,1)S(1)} copy-done((bf16[256,8,128]{2,1,0:T(8,128)(2,1)S(1)}, bf16[256,8,128]{2,1,0:T(8,128)(2,1)}, u32[]{:S(2)}) %copy-start.1) | copy-done | bytes 524312
  24.6 1.5 %arrange.2 = (bf16[2,1024,128]{2,1,0:T(8,128)(2,1)S(1)}, bf16[2,128,1024]{2,1,0:T(8,128)(2,1)S(1)}) custom-call(bf16[256,8,128]{2,1,0:T(8,128)(2,1)S(1)} %copy-done.1), custom_call_target="tpu_custom_call" | custom-call | tf_op jit(solution)/shard_map/arrange/pallas_call | solution.py:370
  26.1 0.4 arrange.3
  26.5 0.0 collective-permute-done.8.refs_4_
  26.5 0.6 collective-permute-done.9.refs_5_
  27.1 3.6 %attention.1 = (bf16[64,1024]{1,0:T(8,128)(2,1)S(1)}, bf16[64,1024]{1,0:T(8,128)(2,1)S(1)}, bf16[64,1024]{1,0:T(8,128)(2,1)S(1)}, bf16[64,1024]{1,0:T(8,128)(2,1...) custom-call(s32[8]{0:T(128)S(1)} %get-tuple-element.52.doc_ref, ...), custom_call_target="tpu_custom_call" | custom-call | flops 7516192768 | bytes 4194304 | tf_op jit(solution)/shard_map/attention/pallas_call | solution.py:197
  30.8 2.8 %collective-permute-start.10 = (bf16[2,256,256]{2,1,0:T(8,128)(2,1)S(1)}, bf16[2,256,256]{2,1,0:T(8,128)(2,1)S(1)}, u32[]{:S(2)}, u32[]{:S(2)}) collective-permute-start(bf16[2,256,256]{2,1,0:T(8,128)(2,1)S(1)} %get-tuple-element.69), channel_id=1, source_target_pairs={{0,4},{4,0},{8,12},{12,8},{16,20},{20,16},{24,28},{28,24},{1,5},{5... | collective-permute-start | bytes 786440 | tf_op jit(solution)/shard_map/ppermute | solution.py:467
  33.5 0.0 collective-permute-start.11
  33.5 2.2 %near.1 = (f32[2,1024,128]{2,1,0:T(8,128)S(1)}, f32[1,256,256]{2,1,0:T(8,128)S(1)}, bf16[1,256,256]{2,1,0:T(8,128)(2,1)S(1)}, f32[256,256]{1,0:T(8,128)S(1)}, bf16[256,256]{1,0:T(8,128)(2,1)S(1)}) custom-call(s32[8]{0:T(128)S(1)} %get-tuple-element.52.doc_ref, bf16[2,128,1024]{2,1,0:T(8,128)(2,1)S(1)} %get-tuple-element.54.q_cols, ...), custom_call_target="tpu_custom_call" | custom-call | flops 2147483648 | bytes 2097152 | tf_op jit(solution)/shard_map/near/pallas_call | solution.py:292
  35.7 0.0 collective-permute-done.11.refs_1_
  35.7 2.2 %collective-permute-done.10.other_ref = bf16[2,256,256]{2,1,0:T(8,128)(2,1)S(1)} collective-permute-done((bf16[2,256,256]{2,1,0:T(8,128)(2,1)S(1)}, bf16[2,256,256]{2,1,0:T(8,128)(2,1)S(1)}, u32[]{:S(2)}, u32[]{:S(2)}) %collective-permute-start.10) | collective-permute-done | bytes 262176 | tf_op jit(solution)/shard_map/ppermute | solution.py:467
  37.9 1.3 %collective-permute-start.14 = (bf16[256,256]{1,0:T(8,128)(2,1)S(1)}, bf16[256,256]{1,0:T(8,128)(2,1)S(1)}, u32[]{:S(2)}, u32[]{:S(2)}) collective-permute-start(bf16[256,256]{1,0:T(8,128)(2,1)S(1)} %get-tuple-element.92), channel_id=1, source_target_pairs={{16,0},{20,4},{24,8},{28,12},{17,1},{21,5},{25,9},{29,13},{18,2},{... | collective-permute-start | bytes 393224 | tf_op jit(solution)/shard_map/ppermute | solution.py:463
  39.2 2.1 %collective-permute-start.17 = (bf16[1,256,256]{2,1,0:T(8,128)(2,1)S(1)}, bf16[1,256,256]{2,1,0:T(8,128)(2,1)S(1)}, u32[]{:S(2)}, u32[]{:S(2)}) collective-permute-start(bf16[1,256,256]{2,1,0:T(8,128)(2,1)S(1)} %get-tuple-element.97), channel_id=1, source_target_pairs={{0,4},{4,0},{8,12},{12,8},{16,20},{20,16},{24,28},{28,24},{1,5},{5... | collective-permute-start | bytes 393224 | tf_op jit(solution)/shard_map/ppermute | solution.py:467
  41.3 0.5 collective-permute-start.12
  41.8 0.0 collective-permute-start.13
  41.8 1.3 %collective-permute-start.16 = (bf16[256,256]{1,0:T(8,128)(2,1)S(1)}, bf16[256,256]{1,0:T(8,128)(2,1)S(1)}, u32[]{:S(2)}, u32[]{:S(2)}) collective-permute-start(bf16[256,256]{1,0:T(8,128)(2,1)S(1)} %get-tuple-element.95), channel_id=1, source_target_pairs={{24,0},{28,4},{25,1},{29,5},{26,2},{30,6},{27,3},{31,7}} | collective-permute-start | bytes 393224 | tf_op jit(solution)/shard_map/ppermute | solution.py:463
  43.1 9.4 %collective-permute-done.14.refs_1_ = bf16[256,256]{1,0:T(8,128)(2,1)S(1)} collective-permute-done((bf16[256,256]{1,0:T(8,128)(2,1)S(1)}, bf16[256,256]{1,0:T(8,128)(2,1)S(1)}, u32[]{:S(2)}, u32[]{:S(2)}) %collective-permute-start.14) | collective-permute-done | bytes 131104 | tf_op jit(solution)/shard_map/ppermute | solution.py:463
  52.5 1.7 %collective-permute-start.15 = (bf16[256,256]{1,0:T(8,128)(2,1)S(1)}, bf16[256,256]{1,0:T(8,128)(2,1)S(1)}, u32[]{:S(2)}, u32[]{:S(2)}) collective-permute-start(bf16[256,256]{1,0:T(8,128)(2,1)S(1)} %get-tuple-element.93), channel_id=1, source_target_pairs={{0,4},{4,0},{8,12},{12,8},{16,20},{20,16},{24,28},{28,24},{1,5},{5... | collective-permute-start | bytes 393224 | tf_op jit(solution)/shard_map/ppermute | solution.py:467
  54.1 0.0 collective-permute-done.17.other_ref
  54.2 1.3 %collective-permute-start.18 = (bf16[256,256]{1,0:T(8,128)(2,1)S(1)}, bf16[256,256]{1,0:T(8,128)(2,1)S(1)}, u32[]{:S(2)}, u32[]{:S(2)}) collective-permute-start(bf16[256,256]{1,0:T(8,128)(2,1)S(1)} %merge.3), channel_id=1, source_target_pairs={{8,0},{12,4},{16,8},{20,12},{24,16},{28,20},{9,1},{13,5},{17,9},{2... | collective-permute-start | bytes 393224 | tf_op jit(solution)/shard_map/ppermute | solution.py:463
  55.5 0.0 collective-permute-done.12.refs_2_
  55.5 0.0 collective-permute-done.13.refs_3_
  55.5 1.5 %join.1 = (bf16[64,4096]{1,0:T(8,128)(2,1)}, bf16[256,8,128]{2,1,0:T(8,128)(2,1)}) custom-call(bf16[64,1024]{1,0:T(8,128)(2,1)S(1)} %get-tuple-element.68.refs_0_, bf16[64,1024]{1,0:T(8,128)(2,1)S(1)} %collective-permute-done.11.refs_1_, bf16[64,1024]{1,0:T(8,128)(2,1)S(1)} %collective-permute-done.12.refs_2_, ...), custom_call_target="tpu_custom_call" | custom-call | tf_op jit(solution)/shard_map/join/pallas_call | solution.py:402
  57.0 4.7 %collective-permute-done.16.refs_2_ = bf16[256,256]{1,0:T(8,128)(2,1)S(1)} collective-permute-done((bf16[256,256]{1,0:T(8,128)(2,1)S(1)}, bf16[256,256]{1,0:T(8,128)(2,1)S(1)}, u32[]{:S(2)}, u32[]{:S(2)}) %collective-permute-start.16) | collective-permute-done | bytes 131104 | tf_op jit(solution)/shard_map/ppermute | solution.py:463
  61.6 0.0 collective-permute-done.15.refs_0_
  61.6 2.8 %collective-permute-done.18.refs_3_ = bf16[256,256]{1,0:T(8,128)(2,1)S(1)} collective-permute-done((bf16[256,256]{1,0:T(8,128)(2,1)S(1)}, bf16[256,256]{1,0:T(8,128)(2,1)S(1)}, u32[]{:S(2)}, u32[]{:S(2)}) %collective-permute-start.18) | collective-permute-done | bytes 131104 | tf_op jit(solution)/shard_map/ppermute | solution.py:463
  64.4 0.9 %finish.1 = (bf16[256,128]{1,0:T(8,128)(2,1)}, bf16[256,128]{1,0:T(8,128)(2,1)}) custom-call(f32[256,256]{1,0:T(8,128)S(1)} %get-tuple-element.90.own_ref, bf16[256,256]{1,0:T(8,128)(2,1)S(1)} %collective-permute-done.15.refs_0_, bf16[256,256]{1,0:T(8,128)(2,1)S(1)} %collective-permute-done.14.refs_1_, bf16[256,256]{1,0:T(8,128)(2,1)S(1)} %collective-permute-done.16.refs_2_, ...), custom_call_target="tpu_custom_call" | custom-call | tf_op jit(solution)/shard_map/finish/pallas_call | solution.py:451
  (2 shorter events, 0.1 us)
Async XLA Ops:
  1.5 11.7 %collective-permute-start = (bf16[512,128]{1,0:T(8,128)(2,1)S(1)}, bf16[512,128]{1,0:T(8,128)(2,1)S(1)}, u32[]{:S(2)}, u32[]{:S(2)}) collective-permute-start(bf16[512,128]{1,0:T(8,128)(2,1)S(1)} %pad_maximum_fusion.own_ref), channel_id=1, source_target_pairs={{0,16},{4,20},{8,24},{12,28},{16,0},{20,4},{24,8},{28,12},{1,17},{... | collective-permute-start | bytes 393224 | tf_op jit(solution)/shard_map/ppermute | solution.py:467
  5.6 1.0 %copy-start = (bf16[64,4096]{1,0:T(8,128)(2,1)S(1)}, bf16[64,4096]{1,0:T(8,128)(2,1)}, u32[]{:S(2)}) copy-start(bf16[64,4096]{1,0:T(8,128)(2,1)} %grad_ref.1) | copy-start | bytes 1572868
  6.7 0.7 %copy-start.2 = (s32[8]{0:T(128)S(1)}, s32[8]{0:T(128)}, u32[]{:S(2)}) copy-start(s32[8]{0:T(128)} %doc_ref.1) | copy-start | bytes 100
  8.5 4.7 %collective-permute-start.1 = (bf16[64,1024]{1,0:T(8,128)(2,1)S(1)}, bf16[64,1024]{1,0:T(8,128)(2,1)S(1)}, u32[]{:S(2)}, u32[]{:S(2)}) collective-permute-start(bf16[64,1024]{1,0:T(8,128)(2,1)S(1)} %get-tuple-element.56), channel_id=1, source_target_pairs={{0,1},{1,0},{2,3},{3,2},{4,5},{5,4},{6,7},{7,6},{8,9},{9,8},{10,11... | collective-permute-start | bytes 393224 | tf_op jit(solution)/shard_map/ppermute | solution.py:467
  8.5 5.9 %collective-permute-start.2 = (bf16[64,1024]{1,0:T(8,128)(2,1)S(1)}, bf16[64,1024]{1,0:T(8,128)(2,1)S(1)}, u32[]{:S(2)}, u32[]{:S(2)}) collective-permute-start(bf16[64,1024]{1,0:T(8,128)(2,1)S(1)} %get-tuple-element.57), channel_id=1, source_target_pairs={{0,2},{1,3},{2,0},{3,1},{4,6},{5,7},{6,4},{7,5},{8,10},{9,11},{10,... | collective-permute-start | bytes 393224 | tf_op jit(solution)/shard_map/ppermute | solution.py:467
  10.1 5.6 %collective-permute-start.4 = (bf16[512,128]{1,0:T(8,128)(2,1)S(1)}, bf16[512,128]{1,0:T(8,128)(2,1)S(1)}, u32[]{:S(2)}, u32[]{:S(2)}) collective-permute-start(bf16[512,128]{1,0:T(8,128)(2,1)S(1)} %pad_maximum_fusion.own_ref), channel_id=1, source_target_pairs={{0,8},{4,12},{8,0},{12,4},{16,24},{20,28},{24,16},{28,20},{1,9},{5... | collective-permute-start | bytes 393224 | tf_op jit(solution)/shard_map/ppermute | solution.py:467
  11.7 7.6 %collective-permute-start.6 = (bf16[512,128]{1,0:T(8,128)(2,1)S(1)}, bf16[512,128]{1,0:T(8,128)(2,1)S(1)}, u32[]{:S(2)}, u32[]{:S(2)}) collective-permute-start(bf16[512,128]{1,0:T(8,128)(2,1)S(1)} %pad_maximum_fusion.own_ref), channel_id=1, source_target_pairs={{0,4},{4,0},{8,12},{12,8},{16,20},{20,16},{24,28},{28,24},{1,5},{5... | collective-permute-start | bytes 393224 | tf_op jit(solution)/shard_map/ppermute | solution.py:467
  13.2 6.1 %collective-permute-start.7 = (bf16[64,1024]{1,0:T(8,128)(2,1)S(1)}, bf16[64,1024]{1,0:T(8,128)(2,1)S(1)}, u32[]{:S(2)}, u32[]{:S(2)}) collective-permute-start(bf16[64,1024]{1,0:T(8,128)(2,1)S(1)} %get-tuple-element.61), channel_id=1, source_target_pairs={{0,3},{1,2},{2,1},{3,0},{4,7},{5,6},{6,5},{7,4},{8,11},{9,10},{10,... | collective-permute-start | bytes 393224 | tf_op jit(solution)/shard_map/ppermute | solution.py:467
  15.7 5.5 %collective-permute-start.5 = (bf16[512,128]{1,0:T(8,128)(2,1)S(1)}, bf16[512,128]{1,0:T(8,128)(2,1)S(1)}, u32[]{:S(2)}, u32[]{:S(2)}) collective-permute-start(bf16[512,128]{1,0:T(8,128)(2,1)S(1)} %collective-permute-done.4.refs_0_), channel_id=1, source_target_pairs={{0,4},{4,0},{8,12},{12,8},{16,20},{20,16},{24,28},{28,24},{1,5},{5... | collective-permute-start | bytes 393224 | tf_op jit(solution)/shard_map/ppermute | solution.py:467
  17.2 5.0 %collective-permute-start.3 = (bf16[512,128]{1,0:T(8,128)(2,1)S(1)}, bf16[512,128]{1,0:T(8,128)(2,1)S(1)}, u32[]{:S(2)}, u32[]{:S(2)}) collective-permute-start(bf16[512,128]{1,0:T(8,128)(2,1)S(1)} %collective-permute-done.refs_1_), channel_id=1, source_target_pairs={{0,8},{4,12},{8,0},{12,4},{16,24},{20,28},{24,16},{28,20},{1,9},{5... | collective-permute-start | bytes 393224 | tf_op jit(solution)/shard_map/ppermute | solution.py:467
  18.8 7.7 %collective-permute-start.8 = (bf16[512,128]{1,0:T(8,128)(2,1)S(1)}, bf16[512,128]{1,0:T(8,128)(2,1)S(1)}, u32[]{:S(2)}, u32[]{:S(2)}) collective-permute-start(bf16[512,128]{1,0:T(8,128)(2,1)S(1)} %collective-permute-done.refs_1_), channel_id=1, source_target_pairs={{0,4},{4,0},{8,12},{12,8},{16,20},{20,16},{24,28},{28,24},{1,5},{5... | collective-permute-start | bytes 393224 | tf_op jit(solution)/shard_map/ppermute | solution.py:467
  22.2 5.0 %collective-permute-start.9 = (bf16[512,128]{1,0:T(8,128)(2,1)S(1)}, bf16[512,128]{1,0:T(8,128)(2,1)S(1)}, u32[]{:S(2)}, u32[]{:S(2)}) collective-permute-start(bf16[512,128]{1,0:T(8,128)(2,1)S(1)} %collective-permute-done.3.refs_2_), channel_id=1, source_target_pairs={{0,4},{4,0},{8,12},{12,8},{16,20},{20,16},{24,28},{28,24},{1,5},{5... | collective-permute-start | bytes 393224 | tf_op jit(solution)/shard_map/ppermute | solution.py:467
  23.6 1.0 %copy-start.1 = (bf16[256,8,128]{2,1,0:T(8,128)(2,1)S(1)}, bf16[256,8,128]{2,1,0:T(8,128)(2,1)}, u32[]{:S(2)}) copy-start(bf16[256,8,128]{2,1,0:T(8,128)(2,1)} %q_ref.1) | copy-start | bytes 1572868
  30.8 7.1 %collective-permute-start.10 = (bf16[2,256,256]{2,1,0:T(8,128)(2,1)S(1)}, bf16[2,256,256]{2,1,0:T(8,128)(2,1)S(1)}, u32[]{:S(2)}, u32[]{:S(2)}) collective-permute-start(bf16[2,256,256]{2,1,0:T(8,128)(2,1)S(1)} %get-tuple-element.69), channel_id=1, source_target_pairs={{0,4},{4,0},{8,12},{12,8},{16,20},{20,16},{24,28},{28,24},{1,5},{5... | collective-permute-start | bytes 786440 | tf_op jit(solution)/shard_map/ppermute | solution.py:467
  33.5 2.2 %collective-permute-start.11 = (bf16[64,1024]{1,0:T(8,128)(2,1)S(1)}, bf16[64,1024]{1,0:T(8,128)(2,1)S(1)}, u32[]{:S(2)}, u32[]{:S(2)}) collective-permute-start(bf16[64,1024]{1,0:T(8,128)(2,1)S(1)} %get-tuple-element.77), channel_id=1, source_target_pairs={{0,1},{1,0},{2,3},{3,2},{4,5},{5,4},{6,7},{7,6},{8,9},{9,8},{10,11... | collective-permute-start | bytes 393224 | tf_op jit(solution)/shard_map/ppermute | solution.py:467
  37.9 14.5 %collective-permute-start.14 = (bf16[256,256]{1,0:T(8,128)(2,1)S(1)}, bf16[256,256]{1,0:T(8,128)(2,1)S(1)}, u32[]{:S(2)}, u32[]{:S(2)}) collective-permute-start(bf16[256,256]{1,0:T(8,128)(2,1)S(1)} %get-tuple-element.92), channel_id=1, source_target_pairs={{16,0},{20,4},{24,8},{28,12},{17,1},{21,5},{25,9},{29,13},{18,2},{... | collective-permute-start | bytes 393224 | tf_op jit(solution)/shard_map/ppermute | solution.py:463
  39.2 14.9 %collective-permute-start.17 = (bf16[1,256,256]{2,1,0:T(8,128)(2,1)S(1)}, bf16[1,256,256]{2,1,0:T(8,128)(2,1)S(1)}, u32[]{:S(2)}, u32[]{:S(2)}) collective-permute-start(bf16[1,256,256]{2,1,0:T(8,128)(2,1)S(1)} %get-tuple-element.97), channel_id=1, source_target_pairs={{0,4},{4,0},{8,12},{12,8},{16,20},{20,16},{24,28},{28,24},{1,5},{5... | collective-permute-start | bytes 393224 | tf_op jit(solution)/shard_map/ppermute | solution.py:467
  41.3 14.1 %collective-permute-start.12 = (bf16[64,1024]{1,0:T(8,128)(2,1)S(1)}, bf16[64,1024]{1,0:T(8,128)(2,1)S(1)}, u32[]{:S(2)}, u32[]{:S(2)}) collective-permute-start(bf16[64,1024]{1,0:T(8,128)(2,1)S(1)} %get-tuple-element.85), channel_id=1, source_target_pairs={{0,2},{1,3},{2,0},{3,1},{4,6},{5,7},{6,4},{7,5},{8,10},{9,11},{10,... | collective-permute-start | bytes 393224 | tf_op jit(solution)/shard_map/ppermute | solution.py:467
  41.8 13.7 %collective-permute-start.13 = (bf16[64,1024]{1,0:T(8,128)(2,1)S(1)}, bf16[64,1024]{1,0:T(8,128)(2,1)S(1)}, u32[]{:S(2)}, u32[]{:S(2)}) collective-permute-start(bf16[64,1024]{1,0:T(8,128)(2,1)S(1)} %get-tuple-element.86), channel_id=1, source_target_pairs={{0,3},{1,2},{2,1},{3,0},{4,7},{5,6},{6,5},{7,4},{8,11},{9,10},{10,... | collective-permute-start | bytes 393224 | tf_op jit(solution)/shard_map/ppermute | solution.py:467
  41.8 19.8 %collective-permute-start.16 = (bf16[256,256]{1,0:T(8,128)(2,1)S(1)}, bf16[256,256]{1,0:T(8,128)(2,1)S(1)}, u32[]{:S(2)}, u32[]{:S(2)}) collective-permute-start(bf16[256,256]{1,0:T(8,128)(2,1)S(1)} %get-tuple-element.95), channel_id=1, source_target_pairs={{24,0},{28,4},{25,1},{29,5},{26,2},{30,6},{27,3},{31,7}} | collective-permute-start | bytes 393224 | tf_op jit(solution)/shard_map/ppermute | solution.py:463
  52.5 9.2 %collective-permute-start.15 = (bf16[256,256]{1,0:T(8,128)(2,1)S(1)}, bf16[256,256]{1,0:T(8,128)(2,1)S(1)}, u32[]{:S(2)}, u32[]{:S(2)}) collective-permute-start(bf16[256,256]{1,0:T(8,128)(2,1)S(1)} %get-tuple-element.93), channel_id=1, source_target_pairs={{0,4},{4,0},{8,12},{12,8},{16,20},{20,16},{24,28},{28,24},{1,5},{5... | collective-permute-start | bytes 393224 | tf_op jit(solution)/shard_map/ppermute | solution.py:467
  54.2 10.3 %collective-permute-start.18 = (bf16[256,256]{1,0:T(8,128)(2,1)S(1)}, bf16[256,256]{1,0:T(8,128)(2,1)S(1)}, u32[]{:S(2)}, u32[]{:S(2)}) collective-permute-start(bf16[256,256]{1,0:T(8,128)(2,1)S(1)} %merge.3), channel_id=1, source_target_pairs={{8,0},{12,4},{16,8},{20,12},{24,16},{28,20},{9,1},{13,5},{17,9},{2... | collective-permute-start | bytes 393224 | tf_op jit(solution)/shard_map/ppermute | solution.py:463

commit v4 on v2

--- a/solution.py
+++ b/solution.py
@@ -498,7 +498,7 @@
         [doc_lengths],
     )
     if whole:
-        beside, near, across = after(beside, near, across)
+        beside, near = after(beside, near)
         far_beside = exchanged(beside, "ctx", 1)
         across, grads[1], *prepared = after(across, grads[1], *prepared)
         passed = exchanged(across, "ctx", 2)
@@ -523,15 +523,15 @@
     )
     other_far = exchanged(other_far, "ctx", 1)
     outs[1:2] = [exchanged(part, "head", 1) for part in outs[1:2]]
+    other1 = exchanged(other1, "ctx", 1)
     other_far, mine0, *outs[1:2] = after(other_far, mine0, *outs[1:2])
     blocks = list(merge(mine_far, other_far))
-    other1, blocks[0], *outs[2:] = after(other1, blocks[0], *outs[2:])
-    other1 = exchanged(other1, "ctx", 1)
     outs[2:] = [exchanged(part, "head", k + 2) for k, part in enumerate(outs[2:])]
     returned = [shifted(block, -2 * (k + 2), count) for k, block in enumerate(blocks)]
-    other0, returned[0] = after(other0, returned[0])
+    other1, returned[-1] = after(other1, returned[-1])
+    (block,) = merge(mine1, other1)
+    block, other0 = after(block, other0)
     other0 = exchanged(other0, "ctx", 1)
-    (block,) = merge(mine1, other1)
     returned.append(shifted(block, -2, count))
     grad_keys, grad_values = finish(mine0, [other0] + returned)
     attended, grad_queries = join(outs, dq_rows, queries.shape)

time: 64 us -> 64.2 us (level)
  waiting for transfers between devices: 23.3 us -> 28.2 us
  starting transfers between devices: 25 us -> 20.6 us
    ppermute x16, starting transfers between devices: 21.1 us -> 16.7 us  [exchanged(): lax.ppermute(block, axis, [(i, i ^ by) for i in range(lax.axis_size(axis))])]
    ppermute x16, waiting for transfers between devices: 10.1 us -> 12.6 us  [exchanged(): lax.ppermute(block, axis, [(i, i ^ by) for i in range(lax.axis_size(axis))])]
    ppermute x3, waiting for transfers between devices: 13.2 us -> 15.6 us  [shifted(): return lax.ppermute(block, 'ctx', pairs)]
where the time goes in v4:
time: 64.2 us; the launch traced here: 63.9 us
  waiting for transfers between devices  28.2 us (44%)
  starting transfers between devices  20.6 us (32%)
  Pallas kernels  10.8 us (17%)
  local copies, waits for them, and re-layouts  2.74 us (4%)
  other arithmetic  0.88 us (1%)
  between operations  0.76 us (1%)
    ppermute x16, starting transfers between devices, exchanged(): lax.ppermute(block, axis, [(i, i ^ by) for i in range(lax.axis_size(axis))])  16.7 us
    ppermute x3, waiting for transfers between devices, shifted(): return lax.ppermute(block, 'ctx', pairs)  15.6 us
    ppermute x16, waiting for transfers between devices, exchanged(): lax.ppermute(block, axis, [(i, i ^ by) for i in range(lax.axis_size(axis))])  12.6 us
    ppermute x3, starting transfers between devices, shifted(): return lax.ppermute(block, 'ctx', pairs)  3.85 us
    pallas_call x1, Pallas kernels, attend(): pl.pallas_call(functools.partial(attention_kernel, back=back, whole=whole...  3.63 us
    unnamed x6, local copies, waits for them, and re-layouts  2.74 us
    pallas_call x2, Pallas kernels, arrange(): pl.pallas_call(kernel, out_shape=[jax.ShapeDtypeStruct(length.shape, leng...  2.47 us
    pallas_call x1, Pallas kernels, attend_near(): pl.pallas_call(functools.partial(near_kernel, back=back, whole=whole, wid...  2.17 us
  transfers between devices with their start and end apart: 19, of which 8 were waited for; matrix products, arithmetic and copies ran while one was open for 0% of the time, Pallas kernels for 10%

profile of v4, /device:TPU:0, one launch (start us, length us, event | category | flops | bytes accessed | tf_op | source)
XLA Modules:
  0.0 63.9 jit_solution(9830598727289523887)
XLA Ops:
  0.6 0.9 %pad_maximum_fusion.own_ref = bf16[512,128]{1,0:T(8,128)(2,1)S(1)} fusion(bf16[256,128]{1,0:T(8,128)(2,1)} %bitcast.4, bf16[256,128]{1,0:T(8,128)(2,1)} %bitcast.5), kind=kLoop, calls=%fused_computation | loop fusion | flops 262144 | bytes 262144 | tf_op jit(solution)/shard_map/concatenate | solution.py:482
  1.5 3.0 %collective-permute-start.4 = (bf16[512,128]{1,0:T(8,128)(2,1)S(1)}, bf16[512,128]{1,0:T(8,128)(2,1)S(1)}, u32[]{:S(2)}, u32[]{:S(2)}) collective-permute-start(bf16[512,128]{1,0:T(8,128)(2,1)S(1)} %pad_maximum_fusion.own_ref), channel_id=1, source_target_pairs={{0,4},{4,0},{8,12},{12,8},{16,20},{20,16},{24,28},{28,24},{1,5},{5... | collective-permute-start | bytes 393224 | tf_op jit(solution)/shard_map/ppermute | solution.py:468
  4.5 1.6 %collective-permute-start.3 = (bf16[512,128]{1,0:T(8,128)(2,1)S(1)}, bf16[512,128]{1,0:T(8,128)(2,1)S(1)}, u32[]{:S(2)}, u32[]{:S(2)}) collective-permute-start(bf16[512,128]{1,0:T(8,128)(2,1)S(1)} %pad_maximum_fusion.own_ref), channel_id=1, source_target_pairs={{0,8},{4,12},{8,0},{12,4},{16,24},{20,28},{24,16},{28,20},{1,9},{5... | collective-permute-start | bytes 393224 | tf_op jit(solution)/shard_map/ppermute | solution.py:468
  6.1 2.6 %collective-permute-start = (bf16[512,128]{1,0:T(8,128)(2,1)S(1)}, bf16[512,128]{1,0:T(8,128)(2,1)S(1)}, u32[]{:S(2)}, u32[]{:S(2)}) collective-permute-start(bf16[512,128]{1,0:T(8,128)(2,1)S(1)} %pad_maximum_fusion.own_ref), channel_id=1, source_target_pairs={{0,16},{4,20},{8,24},{12,28},{16,0},{20,4},{24,8},{28,12},{1,17},{... | collective-permute-start | bytes 393224 | tf_op jit(solution)/shard_map/ppermute | solution.py:468
  8.7 0.0 copy-start.1
  8.7 1.0 %copy-done.1 = bf16[64,4096]{1,0:T(8,128)(2,1)S(1)} copy-done((bf16[64,4096]{1,0:T(8,128)(2,1)S(1)}, bf16[64,4096]{1,0:T(8,128)(2,1)}, u32[]{:S(2)}) %copy-start.1) | copy-done | bytes 524312
  9.8 0.1 collective-permute-start.1
  9.9 1.6 %collective-permute-start.6 = (bf16[64,1024]{1,0:T(8,128)(2,1)S(1)}, bf16[64,1024]{1,0:T(8,128)(2,1)S(1)}, u32[]{:S(2)}, u32[]{:S(2)}) collective-permute-start(bf16[64,1024]{1,0:T(8,128)(2,1)S(1)} %get-tuple-element.65), channel_id=1, source_target_pairs={{0,2},{1,3},{2,0},{3,1},{4,6},{5,7},{6,4},{7,5},{8,10},{9,11},{10,... | collective-permute-start | bytes 393224 | tf_op jit(solution)/shard_map/ppermute | solution.py:468
  11.4 0.0 copy-start
  11.4 1.0 %copy-done = bf16[256,8,128]{2,1,0:T(8,128)(2,1)S(1)} copy-done((bf16[256,8,128]{2,1,0:T(8,128)(2,1)S(1)}, bf16[256,8,128]{2,1,0:T(8,128)(2,1)}, u32[]{:S(2)}) %copy-start) | copy-done | bytes 524312
  12.5 0.0 copy-start.2
  12.5 0.7 %copy-done.2 = s32[8]{0:T(128)S(1)} copy-done((s32[8]{0:T(128)S(1)}, s32[8]{0:T(128)}, u32[]{:S(2)}) %copy-start.2) | copy-done | bytes 56
  13.1 2.1 %arrange.2 = (s32[8]{0:T(128)S(1)}, bf16[2,1024,128]{2,1,0:T(8,128)(2,1)S(1)}, bf16[2,128,1024]{2,1,0:T(8,128)(2,1)S(1)}) custom-call(s32[8]{0:T(128)S(1)} %copy-done.2, bf16[256,8,128]{2,1,0:T(8,128)(2,1)S(1)} %copy-done), custom_call_target="tpu_custom_call" | custom-call | tf_op jit(solution)/shard_map/arrange/pallas_call | solution.py:370
  15.2 0.0 collective-permute-done.4.near_ref
  15.2 0.4 collective-permute-start.7
  15.6 0.0 collective-permute-done.3.refs_0_
  15.6 0.5 collective-permute-start.5
  16.1 0.0 collective-permute-done.refs_1_
  16.1 0.0 collective-permute-done.1.refs_1_
  16.1 0.5 collective-permute-start.2
  16.6 1.5 %collective-permute-start.8 = (bf16[512,128]{1,0:T(8,128)(2,1)S(1)}, bf16[512,128]{1,0:T(8,128)(2,1)S(1)}, u32[]{:S(2)}, u32[]{:S(2)}) collective-permute-start(bf16[512,128]{1,0:T(8,128)(2,1)S(1)} %collective-permute-done.refs_1_), channel_id=1, source_target_pairs={{0,4},{4,0},{8,12},{12,8},{16,20},{20,16},{24,28},{28,24},{1,5},{5... | collective-permute-start | bytes 393224 | tf_op jit(solution)/shard_map/ppermute | solution.py:468
  18.1 0.0 collective-permute-done.6.refs_2_
  18.1 2.7 %collective-permute-done.7.refs_3_ = bf16[64,1024]{1,0:T(8,128)(2,1)S(1)} collective-permute-done((bf16[64,1024]{1,0:T(8,128)(2,1)S(1)}, bf16[64,1024]{1,0:T(8,128)(2,1)S(1)}, u32[]{:S(2)}, u32[]{:S(2)}) %collective-permute-start.7) | collective-permute-done | bytes 131104 | tf_op jit(solution)/shard_map/ppermute | solution.py:468
  20.8 0.4 arrange.3
  21.2 0.7 %collective-permute-done.5.refs_3_ = bf16[512,128]{1,0:T(8,128)(2,1)S(1)} collective-permute-done((bf16[512,128]{1,0:T(8,128)(2,1)S(1)}, bf16[512,128]{1,0:T(8,128)(2,1)S(1)}, u32[]{:S(2)}, u32[]{:S(2)}) %collective-permute-start.5) | collective-permute-done | bytes 131104 | tf_op jit(solution)/shard_map/ppermute | solution.py:468
  21.9 0.0 collective-permute-done.2.refs_2_
  21.9 1.2 %collective-permute-start.9 = (bf16[512,128]{1,0:T(8,128)(2,1)S(1)}, bf16[512,128]{1,0:T(8,128)(2,1)S(1)}, u32[]{:S(2)}, u32[]{:S(2)}) collective-permute-start(bf16[512,128]{1,0:T(8,128)(2,1)S(1)} %collective-permute-done.2.refs_2_), channel_id=1, source_target_pairs={{0,4},{4,0},{8,12},{12,8},{16,20},{20,16},{24,28},{28,24},{1,5},{5... | collective-permute-start | bytes 393224 | tf_op jit(solution)/shard_map/ppermute | solution.py:468
  23.1 1.1 %collective-permute-done.8.refs_4_ = bf16[512,128]{1,0:T(8,128)(2,1)S(1)} collective-permute-done((bf16[512,128]{1,0:T(8,128)(2,1)S(1)}, bf16[512,128]{1,0:T(8,128)(2,1)S(1)}, u32[]{:S(2)}, u32[]{:S(2)}) %collective-permute-start.8) | collective-permute-done | bytes 131104 | tf_op jit(solution)/shard_map/ppermute | solution.py:468
  24.2 2.9 %collective-permute-done.9.refs_5_ = bf16[512,128]{1,0:T(8,128)(2,1)S(1)} collective-permute-done((bf16[512,128]{1,0:T(8,128)(2,1)S(1)}, bf16[512,128]{1,0:T(8,128)(2,1)S(1)}, u32[]{:S(2)}, u32[]{:S(2)}) %collective-permute-start.9) | collective-permute-done | bytes 131104 | tf_op jit(solution)/shard_map/ppermute | solution.py:468
  27.1 3.6 %attention.1 = (bf16[64,1024]{1,0:T(8,128)(2,1)S(1)}, bf16[64,1024]{1,0:T(8,128)(2,1)S(1)}, bf16[64,1024]{1,0:T(8,128)(2,1)S(1)}, bf16[64,1024]{1,0:T(8,128)(2,1...) custom-call(s32[8]{0:T(128)S(1)} %get-tuple-element.55.doc_ref, ...), custom_call_target="tpu_custom_call" | custom-call | flops 7516192768 | bytes 4194304 | tf_op jit(solution)/shard_map/attention/pallas_call | solution.py:197
  30.7 1.1 %collective-permute-start.10 = (bf16[2,256,256]{2,1,0:T(8,128)(2,1)S(1)}, bf16[2,256,256]{2,1,0:T(8,128)(2,1)S(1)}, u32[]{:S(2)}, u32[]{:S(2)}) collective-permute-start(bf16[2,256,256]{2,1,0:T(8,128)(2,1)S(1)} %get-tuple-element.77), channel_id=1, source_target_pairs={{0,4},{4,0},{8,12},{12,8},{16,20},{20,16},{24,28},{28,24},{1,5},{5... | collective-permute-start | bytes 786440 | tf_op jit(solution)/shard_map/ppermute | solution.py:468
  31.8 0.0 collective-permute-start.11
  31.8 2.2 %near.1 = (f32[2,1024,128]{2,1,0:T(8,128)S(1)}, f32[1,256,256]{2,1,0:T(8,128)S(1)}, bf16[1,256,256]{2,1,0:T(8,128)(2,1)S(1)}, f32[256,256]{1,0:T(8,128)S(1)}, bf16[256,256]{1,0:T(8,128)(2,1)S(1)}) custom-call(s32[8]{0:T(128)S(1)} %get-tuple-element.55.doc_ref, bf16[2,128,1024]{2,1,0:T(8,128)(2,1)S(1)} %get-tuple-element.70.q_cols, ...), custom_call_target="tpu_custom_call" | custom-call | flops 2147483648 | bytes 2097152 | tf_op jit(solution)/shard_map/near/pallas_call | solution.py:292
  34.0 1.1 %collective-permute-start.14 = (bf16[1,256,256]{2,1,0:T(8,128)(2,1)S(1)}, bf16[1,256,256]{2,1,0:T(8,128)(2,1)S(1)}, u32[]{:S(2)}, u32[]{:S(2)}) collective-permute-start(bf16[1,256,256]{2,1,0:T(8,128)(2,1)S(1)} %get-tuple-element.94), channel_id=1, source_target_pairs={{0,4},{4,0},{8,12},{12,8},{16,20},{20,16},{24,28},{28,24},{1,5},{5... | collective-permute-start | bytes 393224 | tf_op jit(solution)/shard_map/ppermute | solution.py:468
  35.1 0.0 collective-permute-done.11.refs_1_
  35.1 3.5 %collective-permute-done.10.other_ref = bf16[2,256,256]{2,1,0:T(8,128)(2,1)S(1)} collective-permute-done((bf16[2,256,256]{2,1,0:T(8,128)(2,1)S(1)}, bf16[2,256,256]{2,1,0:T(8,128)(2,1)S(1)}, u32[]{:S(2)}, u32[]{:S(2)}) %collective-permute-start.10) | collective-permute-done | bytes 262176 | tf_op jit(solution)/shard_map/ppermute | solution.py:468
  38.6 1.3 %collective-permute-start.15 = (bf16[256,256]{1,0:T(8,128)(2,1)S(1)}, bf16[256,256]{1,0:T(8,128)(2,1)S(1)}, u32[]{:S(2)}, u32[]{:S(2)}) collective-permute-start(bf16[256,256]{1,0:T(8,128)(2,1)S(1)} %get-tuple-element.97), channel_id=1, source_target_pairs={{24,0},{28,4},{25,1},{29,5},{26,2},{30,6},{27,3},{31,7}} | collective-permute-start | bytes 393224 | tf_op jit(solution)/shard_map/ppermute | solution.py:464
  39.9 1.1 %collective-permute-start.12 = (bf16[64,1024]{1,0:T(8,128)(2,1)S(1)}, bf16[64,1024]{1,0:T(8,128)(2,1)S(1)}, u32[]{:S(2)}, u32[]{:S(2)}) collective-permute-start(bf16[64,1024]{1,0:T(8,128)(2,1)S(1)} %get-tuple-element.87), channel_id=1, source_target_pairs={{0,2},{1,3},{2,0},{3,1},{4,6},{5,7},{6,4},{7,5},{8,10},{9,11},{10,... | collective-permute-start | bytes 393224 | tf_op jit(solution)/shard_map/ppermute | solution.py:468
  40.9 0.0 collective-permute-start.13
  40.9 1.3 %collective-permute-start.17 = (bf16[256,256]{1,0:T(8,128)(2,1)S(1)}, bf16[256,256]{1,0:T(8,128)(2,1)S(1)}, u32[]{:S(2)}, u32[]{:S(2)}) collective-permute-start(bf16[256,256]{1,0:T(8,128)(2,1)S(1)} %get-tuple-element.101), channel_id=1, source_target_pairs={{16,0},{20,4},{24,8},{28,12},{17,1},{21,5},{25,9},{29,13},{18,2},{... | collective-permute-start | bytes 393224 | tf_op jit(solution)/shard_map/ppermute | solution.py:464
  42.2 0.0 collective-permute-done.14.other_ref
  42.2 13.2 %collective-permute-done.15.refs_2_ = bf16[256,256]{1,0:T(8,128)(2,1)S(1)} collective-permute-done((bf16[256,256]{1,0:T(8,128)(2,1)S(1)}, bf16[256,256]{1,0:T(8,128)(2,1)S(1)}, u32[]{:S(2)}, u32[]{:S(2)}) %collective-permute-start.15) | collective-permute-done | bytes 131104 | tf_op jit(solution)/shard_map/ppermute | solution.py:464
  55.5 0.6 collective-permute-start.16
  56.1 1.3 %collective-permute-start.18 = (bf16[256,256]{1,0:T(8,128)(2,1)S(1)}, bf16[256,256]{1,0:T(8,128)(2,1)S(1)}, u32[]{:S(2)}, u32[]{:S(2)}) collective-permute-start(bf16[256,256]{1,0:T(8,128)(2,1)S(1)} %merge.3), channel_id=1, source_target_pairs={{8,0},{12,4},{16,8},{20,12},{24,16},{28,20},{9,1},{13,5},{17,9},{2... | collective-permute-start | bytes 393224 | tf_op jit(solution)/shard_map/ppermute | solution.py:464
  57.4 0.0 collective-permute-done.12.refs_2_
  57.4 0.0 collective-permute-done.13.refs_3_
  57.4 1.5 %join.1 = (bf16[64,4096]{1,0:T(8,128)(2,1)}, bf16[256,8,128]{2,1,0:T(8,128)(2,1)}) custom-call(bf16[64,1024]{1,0:T(8,128)(2,1)S(1)} %get-tuple-element.76.refs_0_, bf16[64,1024]{1,0:T(8,128)(2,1)S(1)} %collective-permute-done.11.refs_1_, bf16[64,1024]{1,0:T(8,128)(2,1)S(1)} %collective-permute-done.12.refs_2_, ...), custom_call_target="tpu_custom_call" | custom-call | tf_op jit(solution)/shard_map/join/pallas_call | solution.py:403
  58.9 0.0 collective-permute-done.17.refs_1_
  58.9 1.7 %collective-permute-done.16.refs_0_ = bf16[256,256]{1,0:T(8,128)(2,1)S(1)} collective-permute-done((bf16[256,256]{1,0:T(8,128)(2,1)S(1)}, bf16[256,256]{1,0:T(8,128)(2,1)S(1)}, u32[]{:S(2)}, u32[]{:S(2)}) %collective-permute-start.16) | collective-permute-done | bytes 131104 | tf_op jit(solution)/shard_map/ppermute | solution.py:468
  60.6 2.4 %collective-permute-done.18.refs_3_ = bf16[256,256]{1,0:T(8,128)(2,1)S(1)} collective-permute-done((bf16[256,256]{1,0:T(8,128)(2,1)S(1)}, bf16[256,256]{1,0:T(8,128)(2,1)S(1)}, u32[]{:S(2)}, u32[]{:S(2)}) %collective-permute-start.18) | collective-permute-done | bytes 131104 | tf_op jit(solution)/shard_map/ppermute | solution.py:464
  63.0 0.9 %finish.1 = (bf16[256,128]{1,0:T(8,128)(2,1)}, bf16[256,128]{1,0:T(8,128)(2,1)}) custom-call(f32[256,256]{1,0:T(8,128)S(1)} %get-tuple-element.92.own_ref, bf16[256,256]{1,0:T(8,128)(2,1)S(1)} %collective-permute-done.16.refs_0_, bf16[256,256]{1,0:T(8,128)(2,1)S(1)} %collective-permute-done.17.refs_1_, bf16[256,256]{1,0:T(8,128)(2,1)S(1)} %collective-permute-done.15.refs_2_, ...), custom_call_target="tpu_custom_call" | custom-call | tf_op jit(solution)/shard_map/finish/pallas_call | solution.py:452
  (3 shorter events, 0.1 us)
Async XLA Ops:
  1.5 13.7 %collective-permute-start.4 = (bf16[512,128]{1,0:T(8,128)(2,1)S(1)}, bf16[512,128]{1,0:T(8,128)(2,1)S(1)}, u32[]{:S(2)}, u32[]{:S(2)}) collective-permute-start(bf16[512,128]{1,0:T(8,128)(2,1)S(1)} %pad_maximum_fusion.own_ref), channel_id=1, source_target_pairs={{0,4},{4,0},{8,12},{12,8},{16,20},{20,16},{24,28},{28,24},{1,5},{5... | collective-permute-start | bytes 393224 | tf_op jit(solution)/shard_map/ppermute | solution.py:468
  4.5 11.1 %collective-permute-start.3 = (bf16[512,128]{1,0:T(8,128)(2,1)S(1)}, bf16[512,128]{1,0:T(8,128)(2,1)S(1)}, u32[]{:S(2)}, u32[]{:S(2)}) collective-permute-start(bf16[512,128]{1,0:T(8,128)(2,1)S(1)} %pad_maximum_fusion.own_ref), channel_id=1, source_target_pairs={{0,8},{4,12},{8,0},{12,4},{16,24},{20,28},{24,16},{28,20},{1,9},{5... | collective-permute-start | bytes 393224 | tf_op jit(solution)/shard_map/ppermute | solution.py:468
  6.1 10.0 %collective-permute-start = (bf16[512,128]{1,0:T(8,128)(2,1)S(1)}, bf16[512,128]{1,0:T(8,128)(2,1)S(1)}, u32[]{:S(2)}, u32[]{:S(2)}) collective-permute-start(bf16[512,128]{1,0:T(8,128)(2,1)S(1)} %pad_maximum_fusion.own_ref), channel_id=1, source_target_pairs={{0,16},{4,20},{8,24},{12,28},{16,0},{20,4},{24,8},{28,12},{1,17},{... | collective-permute-start | bytes 393224 | tf_op jit(solution)/shard_map/ppermute | solution.py:468
  8.7 1.0 %copy-start.1 = (bf16[64,4096]{1,0:T(8,128)(2,1)S(1)}, bf16[64,4096]{1,0:T(8,128)(2,1)}, u32[]{:S(2)}) copy-start(bf16[64,4096]{1,0:T(8,128)(2,1)} %grad_ref.1) | copy-start | bytes 1572868
  9.8 6.3 %collective-permute-start.1 = (bf16[64,1024]{1,0:T(8,128)(2,1)S(1)}, bf16[64,1024]{1,0:T(8,128)(2,1)S(1)}, u32[]{:S(2)}, u32[]{:S(2)}) collective-permute-start(bf16[64,1024]{1,0:T(8,128)(2,1)S(1)} %get-tuple-element.56), channel_id=1, source_target_pairs={{0,1},{1,0},{2,3},{3,2},{4,5},{5,4},{6,7},{7,6},{8,9},{9,8},{10,11... | collective-permute-start | bytes 393224 | tf_op jit(solution)/shard_map/ppermute | solution.py:468
  9.9 8.2 %collective-permute-start.6 = (bf16[64,1024]{1,0:T(8,128)(2,1)S(1)}, bf16[64,1024]{1,0:T(8,128)(2,1)S(1)}, u32[]{:S(2)}, u32[]{:S(2)}) collective-permute-start(bf16[64,1024]{1,0:T(8,128)(2,1)S(1)} %get-tuple-element.65), channel_id=1, source_target_pairs={{0,2},{1,3},{2,0},{3,1},{4,6},{5,7},{6,4},{7,5},{8,10},{9,11},{10,... | collective-permute-start | bytes 393224 | tf_op jit(solution)/shard_map/ppermute | solution.py:468
  11.4 1.0 %copy-start = (bf16[256,8,128]{2,1,0:T(8,128)(2,1)S(1)}, bf16[256,8,128]{2,1,0:T(8,128)(2,1)}, u32[]{:S(2)}) copy-start(bf16[256,8,128]{2,1,0:T(8,128)(2,1)} %q_ref.1) | copy-start | bytes 1572868
  12.5 0.7 %copy-start.2 = (s32[8]{0:T(128)S(1)}, s32[8]{0:T(128)}, u32[]{:S(2)}) copy-start(s32[8]{0:T(128)} %doc_ref.1) | copy-start | bytes 100
  15.2 5.6 %collective-permute-start.7 = (bf16[64,1024]{1,0:T(8,128)(2,1)S(1)}, bf16[64,1024]{1,0:T(8,128)(2,1)S(1)}, u32[]{:S(2)}, u32[]{:S(2)}) collective-permute-start(bf16[64,1024]{1,0:T(8,128)(2,1)S(1)} %get-tuple-element.66), channel_id=1, source_target_pairs={{0,3},{1,2},{2,1},{3,0},{4,7},{5,6},{6,5},{7,4},{8,11},{9,10},{10,... | collective-permute-start | bytes 393224 | tf_op jit(solution)/shard_map/ppermute | solution.py:468
  15.6 6.3 %collective-permute-start.5 = (bf16[512,128]{1,0:T(8,128)(2,1)S(1)}, bf16[512,128]{1,0:T(8,128)(2,1)S(1)}, u32[]{:S(2)}, u32[]{:S(2)}) collective-permute-start(bf16[512,128]{1,0:T(8,128)(2,1)S(1)} %collective-permute-done.3.refs_0_), channel_id=1, source_target_pairs={{0,4},{4,0},{8,12},{12,8},{16,20},{20,16},{24,28},{28,24},{1,5},{5... | collective-permute-start | bytes 393224 | tf_op jit(solution)/shard_map/ppermute | solution.py:468
  16.1 5.8 %collective-permute-start.2 = (bf16[512,128]{1,0:T(8,128)(2,1)S(1)}, bf16[512,128]{1,0:T(8,128)(2,1)S(1)}, u32[]{:S(2)}, u32[]{:S(2)}) collective-permute-start(bf16[512,128]{1,0:T(8,128)(2,1)S(1)} %collective-permute-done.refs_1_), channel_id=1, source_target_pairs={{0,8},{4,12},{8,0},{12,4},{16,24},{20,28},{24,16},{28,20},{1,9},{5... | collective-permute-start | bytes 393224 | tf_op jit(solution)/shard_map/ppermute | solution.py:468
  16.6 7.6 %collective-permute-start.8 = (bf16[512,128]{1,0:T(8,128)(2,1)S(1)}, bf16[512,128]{1,0:T(8,128)(2,1)S(1)}, u32[]{:S(2)}, u32[]{:S(2)}) collective-permute-start(bf16[512,128]{1,0:T(8,128)(2,1)S(1)} %collective-permute-done.refs_1_), channel_id=1, source_target_pairs={{0,4},{4,0},{8,12},{12,8},{16,20},{20,16},{24,28},{28,24},{1,5},{5... | collective-permute-start | bytes 393224 | tf_op jit(solution)/shard_map/ppermute | solution.py:468
  21.9 5.2 %collective-permute-start.9 = (bf16[512,128]{1,0:T(8,128)(2,1)S(1)}, bf16[512,128]{1,0:T(8,128)(2,1)S(1)}, u32[]{:S(2)}, u32[]{:S(2)}) collective-permute-start(bf16[512,128]{1,0:T(8,128)(2,1)S(1)} %collective-permute-done.2.refs_2_), channel_id=1, source_target_pairs={{0,4},{4,0},{8,12},{12,8},{16,20},{20,16},{24,28},{28,24},{1,5},{5... | collective-permute-start | bytes 393224 | tf_op jit(solution)/shard_map/ppermute | solution.py:468
  30.7 7.8 %collective-permute-start.10 = (bf16[2,256,256]{2,1,0:T(8,128)(2,1)S(1)}, bf16[2,256,256]{2,1,0:T(8,128)(2,1)S(1)}, u32[]{:S(2)}, u32[]{:S(2)}) collective-permute-start(bf16[2,256,256]{2,1,0:T(8,128)(2,1)S(1)} %get-tuple-element.77), channel_id=1, source_target_pairs={{0,4},{4,0},{8,12},{12,8},{16,20},{20,16},{24,28},{28,24},{1,5},{5... | collective-permute-start | bytes 786440 | tf_op jit(solution)/shard_map/ppermute | solution.py:468
  31.8 3.3 %collective-permute-start.11 = (bf16[64,1024]{1,0:T(8,128)(2,1)S(1)}, bf16[64,1024]{1,0:T(8,128)(2,1)S(1)}, u32[]{:S(2)}, u32[]{:S(2)}) collective-permute-start(bf16[64,1024]{1,0:T(8,128)(2,1)S(1)} %get-tuple-element.85), channel_id=1, source_target_pairs={{0,1},{1,0},{2,3},{3,2},{4,5},{5,4},{6,7},{7,6},{8,9},{9,8},{10,11... | collective-permute-start | bytes 393224 | tf_op jit(solution)/shard_map/ppermute | solution.py:468
  34.0 8.3 %collective-permute-start.14 = (bf16[1,256,256]{2,1,0:T(8,128)(2,1)S(1)}, bf16[1,256,256]{2,1,0:T(8,128)(2,1)S(1)}, u32[]{:S(2)}, u32[]{:S(2)}) collective-permute-start(bf16[1,256,256]{2,1,0:T(8,128)(2,1)S(1)} %get-tuple-element.94), channel_id=1, source_target_pairs={{0,4},{4,0},{8,12},{12,8},{16,20},{20,16},{24,28},{28,24},{1,5},{5... | collective-permute-start | bytes 393224 | tf_op jit(solution)/shard_map/ppermute | solution.py:468
  38.6 16.9 %collective-permute-start.15 = (bf16[256,256]{1,0:T(8,128)(2,1)S(1)}, bf16[256,256]{1,0:T(8,128)(2,1)S(1)}, u32[]{:S(2)}, u32[]{:S(2)}) collective-permute-start(bf16[256,256]{1,0:T(8,128)(2,1)S(1)} %get-tuple-element.97), channel_id=1, source_target_pairs={{24,0},{28,4},{25,1},{29,5},{26,2},{30,6},{27,3},{31,7}} | collective-permute-start | bytes 393224 | tf_op jit(solution)/shard_map/ppermute | solution.py:464
  39.9 17.5 %collective-permute-start.12 = (bf16[64,1024]{1,0:T(8,128)(2,1)S(1)}, bf16[64,1024]{1,0:T(8,128)(2,1)S(1)}, u32[]{:S(2)}, u32[]{:S(2)}) collective-permute-start(bf16[64,1024]{1,0:T(8,128)(2,1)S(1)} %get-tuple-element.87), channel_id=1, source_target_pairs={{0,2},{1,3},{2,0},{3,1},{4,6},{5,7},{6,4},{7,5},{8,10},{9,11},{10,... | collective-permute-start | bytes 393224 | tf_op jit(solution)/shard_map/ppermute | solution.py:468
  40.9 16.5 %collective-permute-start.13 = (bf16[64,1024]{1,0:T(8,128)(2,1)S(1)}, bf16[64,1024]{1,0:T(8,128)(2,1)S(1)}, u32[]{:S(2)}, u32[]{:S(2)}) collective-permute-start(bf16[64,1024]{1,0:T(8,128)(2,1)S(1)} %get-tuple-element.88), channel_id=1, source_target_pairs={{0,3},{1,2},{2,1},{3,0},{4,7},{5,6},{6,5},{7,4},{8,11},{9,10},{10,... | collective-permute-start | bytes 393224 | tf_op jit(solution)/shard_map/ppermute | solution.py:468
  40.9 18.0 %collective-permute-start.17 = (bf16[256,256]{1,0:T(8,128)(2,1)S(1)}, bf16[256,256]{1,0:T(8,128)(2,1)S(1)}, u32[]{:S(2)}, u32[]{:S(2)}) collective-permute-start(bf16[256,256]{1,0:T(8,128)(2,1)S(1)} %get-tuple-element.101), channel_id=1, source_target_pairs={{16,0},{20,4},{24,8},{28,12},{17,1},{21,5},{25,9},{29,13},{18,2},{... | collective-permute-start | bytes 393224 | tf_op jit(solution)/shard_map/ppermute | solution.py:464
  55.5 5.1 %collective-permute-start.16 = (bf16[256,256]{1,0:T(8,128)(2,1)S(1)}, bf16[256,256]{1,0:T(8,128)(2,1)S(1)}, u32[]{:S(2)}, u32[]{:S(2)}) collective-permute-start(bf16[256,256]{1,0:T(8,128)(2,1)S(1)} %get-tuple-element.100), channel_id=1, source_target_pairs={{0,4},{4,0},{8,12},{12,8},{16,20},{20,16},{24,28},{28,24},{1,5},{5... | collective-permute-start | bytes 393224 | tf_op jit(solution)/shard_map/ppermute | solution.py:468
  56.1 6.8 %collective-permute-start.18 = (bf16[256,256]{1,0:T(8,128)(2,1)S(1)}, bf16[256,256]{1,0:T(8,128)(2,1)S(1)}, u32[]{:S(2)}, u32[]{:S(2)}) collective-permute-start(bf16[256,256]{1,0:T(8,128)(2,1)S(1)} %merge.3), channel_id=1, source_target_pairs={{8,0},{12,4},{16,8},{20,12},{24,16},{28,20},{9,1},{13,5},{17,9},{2... | collective-permute-start | bytes 393224 | tf_op jit(solution)/shard_map/ppermute | solution.py:464
